TPU v7x, 32 devices: a whole 2x2x4 slice. The times are simulated.
32 devices in a mesh: dp: 4 (over x, core), tensor: 8 (over z, y).
Axes of the slice: x: 2, y: 2, z: 4, core: 2. Of those that a mesh axis runs over, the one named last changes fastest.
Arguments:
- tokens: bfloat16 [16384, 1152], P(('dp', 'tensor')), may hold values from -6 to 6
- labels: int32 [64], P('dp'), may hold values from 0 to 999
- timesteps: int32 [64], P('dp'), may hold values from 0 to 999
- image_counts: int32 [4], P('dp'), may hold values from 4 to 16, as said below
- class_table: bfloat16 [1000, 1152], P(None, 'tensor'), may hold values from -6 to 6
- ada_weight: bfloat16 [1152, 6, 1152], P('tensor'), may hold values from -0.1875 to 0.1875
- ada_bias: bfloat16 [6, 1152], replicated, may hold values from -3 to 3
- qkv_weight: bfloat16 [1152, 3, 1152], P(None, None, 'tensor'), may hold values from -0.1875 to 0.1875
- qkv_bias: bfloat16 [3, 1152], P(None, 'tensor'), may hold values from -3 to 3
- qk_scale: bfloat16 [2, 72], replicated, may hold values from 0.25 to 1.75
- out_weight: bfloat16 [1152, 1152], P('tensor'), may hold values from -3 to 3
- gate_up_weight: bfloat16 [1152, 2, 3072], P(None, None, 'tensor'), may hold values from -0.1875 to 0.1875
- down_weight: bfloat16 [3072, 1152], P('tensor'), may hold values from -0.109375 to 0.109375
- out_grad: bfloat16 [16384, 1152], P(('dp', 'tensor')), may hold values from -6 to 6
Outputs:
- out: bfloat16 [16384, 1152], P(('dp', 'tensor'))
- tokens_grad: float32 [16384, 1152], P(('dp', 'tensor'))
- cond_grad: float32 [64, 1152], P('dp', 'tensor')
- class_table_grad: float32 [1000, 1152], P(None, 'tensor')
- ada_weight_grad: float32 [1152, 6, 1152], P('tensor')
- ada_bias_grad: float32 [6, 1152], replicated
- qkv_weight_grad: float32 [1152, 3, 1152], P(None, None, 'tensor')
- qkv_bias_grad: float32 [3, 1152], P(None, 'tensor')
- qk_scale_grad: float32 [2, 72], replicated
- out_weight_grad: float32 [1152, 1152], P('tensor')
- gate_up_grad: float32 [1152, 2, 3072], P(None, None, 'tensor')
- down_grad: float32 [3072, 1152], P('tensor')
Inputs may be any that keep to these rules, and one draw needn't show every extreme that they name: `image_counts`: each entry is 16, 8 or 16 // 4 (never under 1); at least one group holds 16 images.
All inputs are finite; a program needn't handle non-finite values.
Results may differ from a plain program's by a relative error of at most 0.023.
Values may be sent and summed in bfloat16 or wider, within the bound.
A program may use at most 256 MiB of HBM per device.

v0:
```python
import math

import jax
import jax.numpy as jnp
from jax import lax
from jax.sharding import PartitionSpec as P

HD = 72
GRID = 16
PATCH = 256


HIGH = lax.Precision.HIGHEST
epsilon = 1e-06


def normalize(vectors):
    inverse = lax.rsqrt(jnp.mean(vectors * vectors, axis=-1, keepdims=True) + epsilon)
    return (vectors * inverse, inverse)


def normalize_back(grad, normed, inverse):
    return inverse * (grad - normed * jnp.mean(grad * normed, axis=-1, keepdims=True))


def rope_tables(count):
    pairs = HD // 4
    theta = jnp.exp(-math.log(100.0) * jnp.arange(pairs, dtype=jnp.float32) / pairs)
    place = jnp.arange(count) % PATCH
    row_angle = (place // GRID).astype(jnp.float32)[:, None] * theta
    col_angle = (place % GRID).astype(jnp.float32)[:, None] * theta
    return ((jnp.cos(row_angle), jnp.sin(row_angle)), (jnp.cos(col_angle), jnp.sin(col_angle)))


def rotate_part(segment, cosine, sine, direction):
    half_len = segment.shape[-1] // 2
    first, second = (segment[..., :half_len], segment[..., half_len:])
    cosine = cosine[:, None, :]
    sine = direction * sine[:, None, :]
    return jnp.concatenate(
        [first * cosine - second * sine, second * cosine + first * sine], axis=-1
    )


def rotate(vectors, tables, direction):
    half_len = vectors.shape[-1] // 2
    return jnp.concatenate(
        [
            rotate_part(vectors[..., :half_len], tables[0][0], tables[0][1], direction),
            rotate_part(vectors[..., half_len:], tables[1][0], tables[1][1], direction),
        ],
        axis=-1,
    )


def silu_slope(values):
    sigma = jax.nn.sigmoid(values)
    return sigma * (1.0 + values * (1.0 - sigma))


def local(
    tokens,
    labels,
    timesteps,
    image_counts,
    class_table,
    ada_weight,
    ada_bias,
    qkv_weight,
    qkv_bias,
    qk_scale,
    out_weight,
    gate_up_weight,
    down_weight,
    out_grad,
):
    width = tokens.shape[1]
    local_rows = tokens.shape[0]
    members = lax.axis_size("tensor")
    place = lax.axis_index("tensor")
    images = labels.shape[0]
    all_rows = local_rows * members
    columns_here = class_table.shape[1]
    heads_here = columns_here // HD
    column = place * columns_here + jnp.arange(columns_here)
    half_width = width // 2
    frequency = jnp.exp(-math.log(10000.0) * (column % half_width).astype(jnp.float32) / half_width)
    angles = timesteps.astype(jnp.float32)[:, None] * frequency[None, :]
    time_embed = jnp.where(column[None, :] < half_width, jnp.cos(angles), jnp.sin(angles))
    chosen = (labels[:, None] == jnp.arange(class_table.shape[0])[None, :]).astype(jnp.bfloat16)
    condition = jnp.dot(chosen, class_table, preferred_element_type=jnp.float32) + time_embed
    cond_act = jax.nn.silu(condition).astype(jnp.bfloat16)
    mod_part = jnp.einsum("ic,ckd->ikd", cond_act, ada_weight, preferred_element_type=jnp.float32)
    modulation = lax.psum(mod_part, "tensor") + ada_bias.astype(jnp.float32)
    row_index = place * local_rows + jnp.arange(local_rows)
    row_image = row_index // PATCH
    selector = (row_image[:, None] == jnp.arange(images)[None, :]).astype(jnp.float32)
    mod_rows = jnp.dot(selector, modulation.reshape(images, 6 * width), precision=HIGH).reshape(
        local_rows, 6, width
    )
    kept = (row_image < image_counts[0]).astype(jnp.float32)[:, None]
    shift_one, scale_one, gate_one, shift_two, scale_two, gate_two = [
        mod_rows[:, index] for index in range(6)
    ]
    tokens_f = tokens.astype(jnp.float32)
    first_norm, first_inverse = normalize(tokens_f)
    first_in = (first_norm * (1.0 + scale_one) + shift_one).astype(jnp.bfloat16)
    first_all = lax.all_gather(first_in, "tensor", axis=0, tiled=True)
    qkv = jnp.einsum(
        "nd,dkc->nkc", first_all, qkv_weight, preferred_element_type=jnp.float32
    ) + qkv_bias.astype(jnp.float32)
    head_view = qkv.reshape(all_rows, 3, heads_here, HD)
    tables = rope_tables(all_rows)
    qk_gains = qk_scale.astype(jnp.float32)
    query_normed, query_inverse = normalize(head_view[:, 0])
    key_normed, key_inverse = normalize(head_view[:, 1])
    block_shape = (all_rows // PATCH, PATCH, heads_here, HD)
    queries = (
        rotate(query_normed * qk_gains[0], tables, 1.0).astype(jnp.bfloat16).reshape(block_shape)
    )
    keys_rot = (
        rotate(key_normed * qk_gains[1], tables, 1.0).astype(jnp.bfloat16).reshape(block_shape)
    )
    values = head_view[:, 2].astype(jnp.bfloat16).reshape(block_shape)
    factor = HD ** (-0.5)
    scores = (
        jnp.einsum("iqhe,ikhe->ihqk", queries, keys_rot, preferred_element_type=jnp.float32)
        * factor
    )
    row_max = jnp.max(scores, axis=-1, keepdims=True)
    exponent = jnp.exp(scores - row_max)
    totals = jnp.sum(exponent, axis=-1, keepdims=True)
    logsum = row_max + jnp.log(totals)
    probability = (exponent / totals).astype(jnp.bfloat16)
    mixed_heads = (
        jnp.einsum("ihqk,ikhe->iqhe", probability, values, preferred_element_type=jnp.float32)
        .reshape(all_rows, columns_here)
        .astype(jnp.bfloat16)
    )
    attention = lax.psum_scatter(
        jnp.dot(mixed_heads, out_weight, preferred_element_type=jnp.float32).astype(jnp.bfloat16),
        "tensor",
        scatter_dimension=0,
        tiled=True,
    ).astype(jnp.float32)
    after_attn = tokens_f + kept * gate_one * attention
    second_norm, second_inverse = normalize(after_attn)
    second_in = (second_norm * (1.0 + scale_two) + shift_two).astype(jnp.bfloat16)
    second_all = lax.all_gather(second_in, "tensor", axis=0, tiled=True)
    gate_up = jnp.einsum(
        "nd,dkf->nkf", second_all, gate_up_weight, preferred_element_type=jnp.float32
    )
    gate_value, up_value = (gate_up[:, 0], gate_up[:, 1])
    activated = jax.nn.silu(gate_value)
    hidden = (activated * up_value).astype(jnp.bfloat16)
    feed = lax.psum_scatter(
        jnp.dot(hidden, down_weight, preferred_element_type=jnp.float32).astype(jnp.bfloat16),
        "tensor",
        scatter_dimension=0,
        tiled=True,
    ).astype(jnp.float32)
    result = (after_attn + kept * gate_two * feed).astype(jnp.bfloat16)
    grad_out = out_grad.astype(jnp.float32)
    feed_grad = (grad_out * kept * gate_two).astype(jnp.bfloat16)
    gate_two_grad = grad_out * kept * feed
    feed_grad_all = lax.all_gather(feed_grad, "tensor", axis=0, tiled=True)
    hidden_grad = jnp.einsum(
        "nd,fd->nf", feed_grad_all, down_weight, preferred_element_type=jnp.float32
    )
    down_grad = jnp.einsum("nf,nd->fd", hidden, feed_grad_all, preferred_element_type=jnp.float32)
    gate_grad = hidden_grad * up_value * silu_slope(gate_value)
    up_grad = hidden_grad * activated
    gu_grad = jnp.stack([gate_grad, up_grad], axis=1).astype(jnp.bfloat16)
    gate_up_grad = jnp.einsum(
        "nd,nkf->dkf", second_all, gu_grad, preferred_element_type=jnp.float32
    )
    second_grad = lax.psum_scatter(
        jnp.einsum(
            "nkf,dkf->nd", gu_grad, gate_up_weight, preferred_element_type=jnp.float32
        ).astype(jnp.bfloat16),
        "tensor",
        scatter_dimension=0,
        tiled=True,
    ).astype(jnp.float32)
    after_grad = grad_out + normalize_back(
        second_grad * (1.0 + scale_two), second_norm, second_inverse
    )
    attention_grad = (after_grad * kept * gate_one).astype(jnp.bfloat16)
    gate_one_grad = after_grad * kept * attention
    attention_grad_all = lax.all_gather(attention_grad, "tensor", axis=0, tiled=True)
    mixed_grad = jnp.einsum(
        "nd,cd->nc", attention_grad_all, out_weight, preferred_element_type=jnp.float32
    ).astype(jnp.bfloat16)
    out_weight_grad = jnp.einsum(
        "nc,nd->cd", mixed_heads, attention_grad_all, preferred_element_type=jnp.float32
    )
    scores_again = (
        jnp.einsum("iqhe,ikhe->ihqk", queries, keys_rot, preferred_element_type=jnp.float32)
        * factor
    )
    prob_again = jnp.exp(scores_again - logsum)
    mixed_blocks = mixed_grad.reshape(block_shape)
    values_grad = jnp.einsum(
        "ihqk,iqhe->ikhe",
        prob_again.astype(jnp.bfloat16),
        mixed_blocks,
        preferred_element_type=jnp.float32,
    )
    prob_grad = jnp.einsum(
        "iqhe,ikhe->ihqk", mixed_blocks, values, preferred_element_type=jnp.float32
    )
    score_grad = (
        prob_again * (prob_grad - jnp.sum(prob_again * prob_grad, axis=-1, keepdims=True))
    ).astype(jnp.bfloat16)
    queries_grad = (
        jnp.einsum("ihqk,ikhe->iqhe", score_grad, keys_rot, preferred_element_type=jnp.float32)
        * factor
    )
    keys_grad = (
        jnp.einsum("ihqk,iqhe->ikhe", score_grad, queries, preferred_element_type=jnp.float32)
        * factor
    )
    query_back = rotate(queries_grad.reshape(all_rows, heads_here, HD), tables, -1.0)
    key_back = rotate(keys_grad.reshape(all_rows, heads_here, HD), tables, -1.0)
    scale_part = jnp.stack(
        [
            jnp.sum(query_back * query_normed, axis=(0, 1)),
            jnp.sum(key_back * key_normed, axis=(0, 1)),
        ]
    )
    query_raw = normalize_back(query_back * qk_gains[0], query_normed, query_inverse)
    key_raw = normalize_back(key_back * qk_gains[1], key_normed, key_inverse)
    qkv_grad = (
        jnp.stack([query_raw, key_raw, values_grad.reshape(all_rows, heads_here, HD)], axis=1)
        .reshape(all_rows, 3, columns_here)
        .astype(jnp.bfloat16)
    )
    qkv_weight_grad = jnp.einsum(
        "nd,nkc->dkc", first_all, qkv_grad, preferred_element_type=jnp.float32
    )
    qkv_bias_grad = jnp.sum(qkv_grad.astype(jnp.float32), axis=0)
    first_grad = lax.psum_scatter(
        jnp.einsum("nkc,dkc->nd", qkv_grad, qkv_weight, preferred_element_type=jnp.float32).astype(
            jnp.bfloat16
        ),
        "tensor",
        scatter_dimension=0,
        tiled=True,
    ).astype(jnp.float32)
    tokens_grad = after_grad + normalize_back(
        first_grad * (1.0 + scale_one), first_norm, first_inverse
    )
    row_mod_grad = jnp.stack(
        [
            first_grad,
            first_grad * first_norm,
            gate_one_grad,
            second_grad,
            second_grad * second_norm,
            gate_two_grad,
        ],
        axis=1,
    ).reshape(local_rows, 6 * width)
    mod_grad_part = jnp.dot(selector.T, row_mod_grad, precision=HIGH).reshape(images, 6, width)
    mod_grad, scale_grad = (
        lax.psum(mod_grad_part.astype(jnp.bfloat16), "tensor").astype(jnp.float32),
        lax.psum(scale_part.astype(jnp.bfloat16), "tensor").astype(jnp.float32),
    )
    mod_grad_low = mod_grad.astype(jnp.bfloat16)
    ada_weight_grad = jnp.einsum(
        "ic,ikd->ckd", cond_act, mod_grad_low, preferred_element_type=jnp.float32
    )
    ada_bias_grad = jnp.sum(mod_grad_low.astype(jnp.float32), axis=0)
    act_grad = jnp.einsum(
        "ikd,ckd->ic", mod_grad_low, ada_weight, preferred_element_type=jnp.float32
    )
    cond_grad = act_grad * silu_slope(condition)
    table_grad = jnp.dot(chosen.astype(jnp.float32).T, cond_grad, precision=HIGH)
    summed = (
        lax.psum(table_grad.astype(jnp.bfloat16), "dp").astype(jnp.float32),
        lax.psum(ada_weight_grad.astype(jnp.bfloat16), "dp").astype(jnp.float32),
        lax.psum(ada_bias_grad.astype(jnp.bfloat16), "dp").astype(jnp.float32),
        lax.psum(qkv_weight_grad.astype(jnp.bfloat16), "dp").astype(jnp.float32),
        lax.psum(qkv_bias_grad.astype(jnp.bfloat16), "dp").astype(jnp.float32),
        lax.psum(scale_grad.astype(jnp.bfloat16), "dp").astype(jnp.float32),
        lax.psum(out_weight_grad.astype(jnp.bfloat16), "dp").astype(jnp.float32),
        lax.psum(gate_up_grad.astype(jnp.bfloat16), "dp").astype(jnp.float32),
        lax.psum(down_grad.astype(jnp.bfloat16), "dp").astype(jnp.float32),
    )
    return (result, tokens_grad, cond_grad) + tuple(summed)


def solution(mesh):
    placed = (
        P(("dp", "tensor"), None),
        P("dp"),
        P("dp"),
        P("dp"),
        P(None, "tensor"),
        P("tensor", None, None),
        P(),
        P(None, None, "tensor"),
        P(None, "tensor"),
        P(),
        P("tensor", None),
        P(None, None, "tensor"),
        P("tensor", None),
        P(("dp", "tensor"), None),
    )
    return jax.shard_map(
        local,
        mesh=mesh,
        in_specs=placed,
        out_specs=(
            P(("dp", "tensor"), None),
            P(("dp", "tensor"), None),
            P("dp", "tensor"),
            P(None, "tensor"),
            P("tensor", None, None),
            P(),
            P(None, None, "tensor"),
            P(None, "tensor"),
            P(),
            P("tensor", None),
            P(None, None, "tensor"),
            P("tensor", None),
        ),
        check_vma=False,
    )
```

profile of v0, /device:TPU:0, one launch (start us, length us, event | category | flops | bytes accessed | tf_op | source)
XLA Modules:
  0.0 1707.5 jit_solution(18154193487712994105)
XLA Ops:
  11.6 75.0 %all-reduce.6.cloned.1.call-done = f32[16,6,1152]{2,0,1:T(8,128)} async-done(((f32[16,6,1152]{2,0,1:T(8,128)}), f32[16,6,1152]{2,0,1:T(8,128)}) %all-reduce.6.cloned.1.call-update) | async-done | bytes 442384 | tf_op jit(solution)/shard_map/psum | solution.py:94
  86.6 6.8 fusion.76
  93.4 5.0 copy-done.2
  100.3 3.9 broadcast_multiply_fusion.1
  104.2 133.2 %all-gather.5.cloned.1.call-done = bf16[4096,1152]{1,0:T(8,128)(2,1)} async-done(((bf16[512,1152]{1,0:T(8,128)(2,1)}), bf16[4096,1152]{1,0:T(8,128)(2,1)}) %all-gather.5.cloned.1.call-update) | async-done | bytes 9437200 | tf_op jit(solution)/shard_map/all_gather | solution.py:108
  237.4 7.6 fusion.114
  271.1 3.7 multiply_reduce_fusion.1
  278.1 2.8 fusion.69
  282.8 5.3 convolution_convert_fusion.1
  288.8 161.1 %reduce-scatter.5.cloned.1.call-done = bf16[512,1152]{1,0:T(8,128)(2,1)} async-done(((bf16[4096,1152]{1,0:T(8,128)(2,1)}), bf16[512,1152]{1,0:T(8,128)(2,1)}) %reduce-scatter.5.cloned.1.call-update) | async-done | bytes 1179664 | tf_op jit(solution)/shard_map/reduce_scatter | solution.py:140
  449.9 5.6 multiply_reduce_fusion.7
  455.6 4.6 fusion.44
  460.2 132.6 %all-gather.9.cloned.1.call-done = bf16[4096,1152]{1,0:T(8,128)(2,1)} async-done(((bf16[512,1152]{1,0:T(8,128)(2,1)}), bf16[4096,1152]{1,0:T(8,128)(2,1)}) %all-gather.9.cloned.1.call-update) | async-done | bytes 9437200 | tf_op jit(solution)/shard_map/all_gather | solution.py:166
  592.8 9.5 fusion.115
  602.3 129.6 %all-gather.7.cloned.1.call-done = bf16[4096,1152]{1,0:T(8,128)(2,1)} async-done(((bf16[512,1152]{1,0:T(8,128)(2,1)}), bf16[4096,1152]{1,0:T(8,128)(2,1)}) %all-gather.7.cloned.1.call-update) | async-done | bytes 9437200 | tf_op jit(solution)/shard_map/all_gather | solution.py:149
  731.9 11.8 fusion.4
  743.7 5.3 fusion.21
  750.6 12.9 bitcast_convert_fusion.1
  763.6 9.8 convolution_convert_fusion
  773.4 151.7 %reduce-scatter.9.cloned.1.call-done = bf16[512,1152]{1,0:T(8,128)(2,1)} async-done(((bf16[4096,1152]{1,0:T(8,128)(2,1)}), bf16[512,1152]{1,0:T(8,128)(2,1)}) %reduce-scatter.9.cloned.1.call-update) | async-done | bytes 1179664 | tf_op jit(solution)/shard_map/reduce_scatter | solution.py:177
  925.2 3.3 multiply_reduce_fusion.6
  928.5 163.3 %reduce-scatter.7.cloned.1.call-done = bf16[512,1152]{1,0:T(8,128)(2,1)} async-done(((bf16[4096,1152]{1,0:T(8,128)(2,1)}), bf16[512,1152]{1,0:T(8,128)(2,1)}) %reduce-scatter.7.cloned.1.call-update) | async-done | bytes 1179664 | tf_op jit(solution)/shard_map/reduce_scatter | solution.py:156
  1091.8 6.7 multiply_convert_fusion.4
  1098.6 137.2 %all-gather.11.cloned.1.call-done = bf16[4096,1152]{1,0:T(8,128)(2,1)} async-done(((bf16[512,1152]{1,0:T(8,128)(2,1)}), bf16[4096,1152]{1,0:T(8,128)(2,1)}) %all-gather.11.cloned.1.call-update) | async-done | bytes 9437200 | tf_op jit(solution)/shard_map/all_gather | solution.py:190
  1235.8 6.9 convolution_convert_fusion.2
  1243.0 5.7 fusion.66
  1248.7 6.4 multiply_reduce_fusion
  1255.1 2.3 multiply_convert_fusion
  1257.5 2.9 multiply_bitcast_fusion
  1260.4 2.2 multiply_bitcast_fusion.1
  1264.4 2.1 copy.95
  1277.7 8.0 bitcast_convert_fusion
  1286.0 10.0 convolution_convert_fusion.4
  1296.0 12.1 fusion.17
  1308.2 6.0 fusion.116
  1314.2 133.2 %reduce-scatter.11.cloned.1.call-done = bf16[512,1152]{1,0:T(8,128)(2,1)} async-done(((bf16[4096,1152]{1,0:T(8,128)(2,1)}), bf16[512,1152]{1,0:T(8,128)(2,1)}) %reduce-scatter.11.cloned.1.call-update) | async-done | bytes 1179664 | tf_op jit(solution)/shard_map/reduce_scatter | solution.py:242
  1447.4 2.9 fusion.40
  1461.7 15.2 copy.68
  1476.8 10.5 fusion.55
  1487.4 6.6 convolution_convert_fusion.5
  1495.0 61.9 %all-reduce.8.cloned.1.call-done = bf16[16,6,1152]{2,0,1:T(8,128)(2,1)} async-done(((bf16[16,6,1152]{2,0,1:T(8,128)(2,1)}), bf16[16,6,1152]{2,0,1:T(8,128)(2,1)}) %all-reduce.8.cloned.1.call-update) | async-done | bytes 221200 | tf_op jit(solution)/shard_map/psum | solution.py:266
  1561.8 19.7 %psum.91 = bf16[2,72]{1,0:T(2,128)(2,1)S(1)} all-reduce(bf16[2,72]{1,0:T(2,128)(2,1)S(1)} %pad_maximum_fusion.14), channel_id=1, replica_groups=mesh['dp'=4,'tensor'=8] {'tensor'}, use_global_device_ids=true, to_apply=%region_26.27 | all-reduce | flops 144 | bytes 576 | tf_op jit(solution)/shard_map/psum | solution.py:267
  1581.5 2.8 fusion.32
  1584.7 3.9 fusion.35
  1588.7 12.3 all-reduce
  1602.8 79.3 %all-reduce.10.cloned.1.call-done = (bf16[1152,2,384]{2,0,1:T(8,128)(2,1)}, bf16[1000,144]{0,1:T(8,128)(2,1)}, bf16[144,6,1152]{2,0,1:T(8,128)(2,1)}, bf16[1152,...) async-done(((bf16[1152,2,384]{2,0,1:T(8,128)(2,1)}, bf16[1000,144]{0,1:T(8,128)(2,1)}, bf16[144,6,1152]{2,0,1:T(8,128)(2,1)}, ...) | async-done | bytes 6259984 | tf_op jit(solution)/shard_map/psum | solution.py:287
  1686.0 9.5 copy.70
  1698.5 2.2 convert_element_type.280
  (242 shorter events, 79.1 us)
Async XLA Ops:
  7.2 4.0 copy-start.58
  7.2 4.1 copy-start.5
  7.2 79.4 %all-reduce.6.cloned.1.call-start = ((), (), s32[]{:S(2)}) async-start(), calls=%async_computation.4 | async-start | bytes 884736 | tf_op jit(solution)/shard_map/psum | solution.py:94
  11.2 226.2 %all-gather.5.cloned.1.call-start = ((), (), s32[]{:S(2)}) async-start(), calls=%async_computation.5 | async-start | bytes 10616832 | tf_op jit(solution)/shard_map/all_gather | solution.py:108
  11.2 82.2 %copy-start.56 = (s32[512]{0:T(512)}, s32[512]{0:T(512)S(1)}, u32[]{:S(2)}) copy-start(s32[512]{0:T(512)S(1)} %add_select_fusion.3) | copy-start | bytes 6148
  11.6 81.8 %copy-start.54 = (f32[512]{0:T(512)}, f32[512]{0:T(512)S(1)}, u32[]{:S(2)}) copy-start(f32[512]{0:T(512)S(1)} %add_rsqrt_fusion.3) | copy-start | bytes 6148
  93.4 5.0 copy-start.2
  100.0 349.9 %reduce-scatter.5.cloned.1.call-start = ((), (), s32[]{:S(2)}) async-start(), calls=%async_computation.6 | async-start | bytes 10616832 | tf_op jit(solution)/shard_map/reduce_scatter | solution.py:140
  246.1 3.3 copy-start.3
  271.1 3.7 copy-start.46
  274.8 3.2 copy-start.1
  274.8 3.2 copy-start.21
  288.1 304.7 %all-gather.9.cloned.1.call-start = ((), (), s32[]{:S(2)}) async-start(), calls=%async_computation.9 | async-start | bytes 10616832 | tf_op jit(solution)/shard_map/all_gather | solution.py:166
  455.5 276.4 %all-gather.7.cloned.1.call-start = ((), (), s32[]{:S(2)}) async-start(), calls=%async_computation.7 | async-start | bytes 10616832 | tf_op jit(solution)/shard_map/all_gather | solution.py:149
  455.5 137.3 %copy-start.62 = (bf16[384,1152]{1,0:T(8,128)(2,1)S(1)}, bf16[384,1152]{1,0:T(8,128)(2,1)}, u32[]{:S(2)}) copy-start(bf16[384,1152]{1,0:T(8,128)(2,1)} %param.26) | copy-start | bytes 2654212
  460.2 465.0 %reduce-scatter.9.cloned.1.call-start = ((), (), s32[]{:S(2)}) async-start(), calls=%async_computation.10 | async-start | bytes 10616832 | tf_op jit(solution)/shard_map/reduce_scatter | solution.py:177
  731.9 11.8 copy-start.20
  763.5 328.3 %reduce-scatter.7.cloned.1.call-start = ((), (), s32[]{:S(2)}) async-start(), calls=%async_computation.8 | async-start | bytes 10616832 | tf_op jit(solution)/shard_map/reduce_scatter | solution.py:156
  773.4 462.4 %all-gather.11.cloned.1.call-start = ((), (), s32[]{:S(2)}) async-start(), calls=%async_computation.11 | async-start | bytes 10616832 | tf_op jit(solution)/shard_map/all_gather | solution.py:190
  925.2 166.6 %copy-start.10 = (bf16[512,1152]{1,0:T(8,128)(2,1)S(1)}, bf16[512,1152]{1,0:T(8,128)(2,1)}, u32[]{:S(2)}) copy-start(bf16[512,1152]{1,0:T(8,128)(2,1)} %reduce-scatter.9.cloned.1.call-done) | copy-start | bytes 3538948
  1098.5 349.0 %reduce-scatter.11.cloned.1.call-start = ((), (), s32[]{:S(2)}) async-start(), calls=%async_computation.12 | async-start | bytes 10616832 | tf_op jit(solution)/shard_map/reduce_scatter | solution.py:242
  1243.0 5.7 copy-start.22
  1243.0 12.1 slice-start
  1248.7 6.4 slice-start.1
  1257.5 2.9 copy-start.39
  1257.5 2.9 copy-start.44
  1257.5 2.9 copy-start.45
  1257.5 2.9 copy-start.47
  1285.8 271.2 %all-reduce.8.cloned.1.call-start = ((), (), s32[]{:S(2)}) async-start(), calls=%async_computation.13 | async-start | bytes 442368 | tf_op jit(solution)/shard_map/psum | solution.py:266
  1286.0 10.0 copy-start.33
  1286.0 10.0 copy-start.34
  1286.0 22.2 %slice-start.4 = ((s8[9437184]{0:T(1024)(128)(4,1)}), s8[4194304]{0:T(1024)(128)(4,1)S(1)}, s32[]{:S(2)}) async-start(s8[9437184]{0:T(1024)(128)(4,1)} %bitcast.308), calls=%async_computation.19 | async-start | bytes 8388608
  1286.0 22.2 %slice-start.5 = ((s8[9437184]{0:T(1024)(128)(4,1)}), s8[4194304]{0:T(1024)(128)(4,1)S(1)}, s32[]{:S(2)}) async-start(s8[9437184]{0:T(1024)(128)(4,1)} %bitcast.308), calls=%async_computation.20 | async-start | bytes 8388608
  1296.0 12.2 copy-start.29
  1296.0 12.2 slice-start.6
  1314.2 136.1 %copy-start.6 = (bf16[512,1152]{1,0:T(8,128)(2,1)S(1)}, bf16[512,1152]{1,0:T(8,128)(2,1)}, u32[]{:S(2)}) copy-start(bf16[512,1152]{1,0:T(8,128)(2,1)} %param.14) | copy-start | bytes 3538948
  1314.2 136.1 %copy-start.55 = (f32[512]{0:T(512)S(1)}, f32[512]{0:T(512)}, u32[]{:S(2)}) copy-start(f32[512]{0:T(512)} %copy-done.54) | copy-start | bytes 6148
  1447.4 2.9 copy-start.12
  1461.7 15.2 copy-start.57
  1487.3 194.8 %all-reduce.10.cloned.1.call-start = ((), (), s32[]{:S(2)}) async-start(), calls=%async_computation.14 | async-start | bytes 12533760 | tf_op jit(solution)/shard_map/psum | solution.py:287
  1487.4 6.6 copy-start.37
  1494.0 63.0 %copy-start.52 = (f32[16,144]{1,0:T(8,128)S(1)}, f32[16,144]{1,0:T(8,128)}, u32[]{:S(2)}) copy-start(f32[16,144]{1,0:T(8,128)} %copy-done.51) | copy-start | bytes 27652
  1494.0 64.6 %copy-start.60 = (s32[16]{0:T(128)S(1)}, s32[16]{0:T(128)}, u32[]{:S(2)}) copy-start(s32[16]{0:T(128)} %param.15) | copy-start | bytes 196
  1558.6 3.2 copy-start.53
  1581.5 3.2 copy-start.13
  1682.1 3.8 copy-start.38
  1686.0 9.5 copy-start.49
  1695.5 3.0 copy-start.36
  (34 other events, 64.7 us)
Sparse Core Ops, SparseCore 0:
  12.0 74.5 all-reduce.5
  100.1 137.1 all-gather.4
  288.2 161.6 reduce-scatter.4
  455.6 137.1 all-gather.8
  595.6 136.2 all-gather.6
  763.6 161.4 reduce-scatter.8
  929.2 162.5 reduce-scatter.6
  1098.6 137.1 all-gather.10
  1285.9 161.5 reduce-scatter.10
  1487.4 69.4 all-reduce.7
  1561.9 120.1 all-reduce.9
where the time goes:
time: 1710 us
  waiting for transfers between devices  1360 us (80%)
  matrix products  154 us (9%)
  other arithmetic  77.1 us (5%)
  local copies, waits for them, and re-layouts  69.1 us (4%)
  blocking collectives  32 us (2%)
    reduce_scatter x1, waiting for transfers between devices, local(): lax.psum_scatter(jnp.dot(hidden, down_weight, preferred_element_type=jnp....  163 us
    reduce_scatter x1, waiting for transfers between devices, local(): lax.psum_scatter(jnp.dot(mixed_heads, out_weight, preferred_element_type=...  161 us
    reduce_scatter x1, waiting for transfers between devices, local(): lax.psum_scatter(jnp.einsum('nkf,dkf->nd', gu_grad, gate_up_weight, prefe...  152 us
    all_gather x1, waiting for transfers between devices, local(): lax.all_gather(attention_grad, 'tensor', axis=0, tiled=True)  137 us
    reduce_scatter x1, waiting for transfers between devices, local(): lax.psum_scatter(jnp.einsum('nkc,dkc->nd', qkv_grad, qkv_weight, preferre...  133 us
    all_gather x1, waiting for transfers between devices, local(): first_all = lax.all_gather(first_in, 'tensor', axis=0, tiled=True)  133 us
    all_gather x1, waiting for transfers between devices, local(): feed_grad_all = lax.all_gather(feed_grad, 'tensor', axis=0, tiled=True)  133 us
    all_gather x1, waiting for transfers between devices, local(): second_all = lax.all_gather(second_in, 'tensor', axis=0, tiled=True)  130 us
  transfers between devices with their start and end apart: 11, of which 11 were waited for; matrix products, arithmetic and copies ran while one was open for 4% of the time, Pallas kernels for 0%

commit v1 on v0

--- a/solution.py
+++ b/solution.py
@@ -2,25 +2,840 @@
 
 import jax
 import jax.numpy as jnp
+import numpy as np
 from jax import lax
+from jax.experimental import pallas as pl
+from jax.experimental.pallas import tpu as pltpu
 from jax.sharding import PartitionSpec as P
 
 HD = 72
 GRID = 16
 PATCH = 256
-
-
 HIGH = lax.Precision.HIGHEST
+MESH = pl.DeviceIdType.MESH
 epsilon = 1e-06
 
-
-def normalize(vectors):
-    inverse = lax.rsqrt(jnp.mean(vectors * vectors, axis=-1, keepdims=True) + epsilon)
+HEAD = 80
+HALF = 40
+SHARD_FF = 192
+A_ROWS = 4 * HEAD
+B_ROWS = 2 * SHARD_FF
+C_ROWS = SHARD_FF
+ROWS_ALL = A_ROWS + B_ROWS + C_ROWS
+D = 1152
+
+G_STAGE, G_LONE = 128, 48
+R_STAGE, R_LONE = 64, 16
+G_STAGES = ROWS_ALL // G_STAGE
+R_STAGES = ROWS_ALL // R_STAGE
+PAY = 16
+
+
+def place():
+    d = lax.axis_index("dp")
+    t = lax.axis_index("tensor")
+    return d // 2, d % 2, t // 2, t % 2
+
+
+def at(x, c, z, y):
+    return (x * 2 + c, z * 2 + y)
+
+
+def greet(targets):
+    barrier = pltpu.get_barrier_semaphore()
+    for o in targets:
+        pl.semaphore_signal(barrier, inc=1, device_id=o, device_id_type=MESH)
+    pl.semaphore_wait(barrier, len(targets))
+
+
+def rows_at(first, size):
+    return pl.ds(pl.multiple_of(first, 16), size)
+
+
+def nt(a, b):
+    return lax.dot_general(a, b, (((1,), (1,)), ((), ())), preferred_element_type=jnp.float32)
+
+
+def tn(a, b):
+    return lax.dot_general(a, b, (((0,), (0,)), ((), ())), preferred_element_type=jnp.float32)
+
+
+def nn(a, b):
+    return lax.dot_general(a, b, (((1,), (0,)), ((), ())), preferred_element_type=jnp.float32)
+
+
+def low(v):
+    return v.astype(jnp.bfloat16)
+
+
+def wide(v):
+    return v.astype(jnp.float32)
+
+
+def turn(v, cos, sin):
+    a, b = v[:HALF], v[HALF:]
+    return jnp.concatenate([a * cos - b * sin, b * cos + a * sin], axis=0)
+
+
+def remote(src, dst, ss, rs, to):
+    return pltpu.make_async_remote_copy(
+        src_ref=src, dst_ref=dst, send_sem=ss, recv_sem=rs, device_id=to, device_id_type=MESH)
+
+
+CHUNK = 64
+FACTOR = HD ** (-0.5)
+
+
+def forward_kernel(
+    own, mod_in, cond_in, tokens, out_grad, ada, keep, gains, table,
+    full, cond_out, mod_out, fi_out, si_out, fg_out, att_out, qkv_out, norm_out, stat_out, mixed_out, gu_out, hid_out,
+    mod_all, mod, fi, si, fg, att, att_send, att_recv, wa, ow, mixed, qkv, norm, stat, wb, gu, hid,
+    send, recv, ms, mr, cs, cr, es, er, ls, qs, hs, ws, save,
+):
+    x, c, z, y = place()
+    t = z * 2 + y
+    d = x * 2 + c
+    peers = [lax.rem(t + k, 8) for k in range(1, 8)]
+    groups = [lax.rem(d + k, 4) for k in range(1, 4)]
+    greet([(d, p) for p in peers] + [(g, t) for g in groups])
+    y_side, x_side, core = at(x, c, z, 1 - y), at(1 - x, c, z, y), at(x, 1 - c, z, y)
+    up, down = at(x, c, z + 1, y), at(x, c, z - 1, y)
+    small = []
+    for k, p in enumerate(peers):
+        small.append(remote(mod_in.at[p], mod_all.at[t], ms.at[k], mr.at[t], (d, p)))
+    for k, g in enumerate(groups):
+        small.append(remote(cond_in, cond_out.at[d], cs.at[k], cr.at[d], (g, t)))
+    for cp in small:
+        cp.start()
+    kept = [
+        pltpu.make_async_copy(own, full.at[t], ls.at[0]),
+        pltpu.make_async_copy(mod_in.at[t], mod_all.at[t], ls.at[1]),
+        pltpu.make_async_copy(cond_in, cond_out.at[d], ls.at[2]),
+    ]
+    for cp in kept:
+        cp.start()
+
+    def plane(g):
+        return rows_at(g * G_STAGE + x * G_LONE, G_STAGE - G_LONE)
+
+    def lone(g, side):
+        return rows_at(g * G_STAGE + side * (G_STAGE - G_LONE), G_LONE)
+
+    def copy(g, kind, src, slot, rows, path, to):
+        return remote(src.at[rows], full.at[slot, rows], send.at[g, kind], recv.at[g, slot, path], to)
+
+    def arrived(g, slot, rows, path):
+        copy(g, 0, own, slot, rows, path, x_side).wait_recv()
+
+    def issue(g):
+        copy(g, 2, own, t, plane(g), 0, y_side).start()
+        pl.when(z < 3)(lambda: copy(g, 0, own, t, plane(g), 0, up).start())
+        pl.when(z > 0)(lambda: copy(g, 1, own, t, plane(g), 0, down).start())
+
+    def along_z(g, j):
+        def below():
+            slot = (z - j) * 2 + y
+            arrived(g, slot, plane(g), 0)
+            pl.when(z < 3)(lambda: copy(g, 1 + 2 * j, full.at[slot], slot, plane(g), 0, up).start())
+            copy(g, 8 + j, full.at[slot], slot, plane(g), 0, y_side).start()
+            copy(g, 11 + j, full.at[slot], slot, lone(g, x), 1, x_side).start()
+
+        def above():
+            slot = (z + j) * 2 + y
+            arrived(g, slot, plane(g), 0)
+            pl.when(z > 0)(lambda: copy(g, 2 + 2 * j, full.at[slot], slot, plane(g), 0, down).start())
+            copy(g, 14 + j, full.at[slot], slot, plane(g), 0, y_side).start()
+            copy(g, 17 + j, full.at[slot], slot, lone(g, x), 1, x_side).start()
+
+        pl.when(z >= j)(below)
+        pl.when(z + j <= 3)(above)
+
+    def along_y(g, zz):
+        slot = zz * 2 + 1 - y
+        arrived(g, slot, plane(g), 0)
+        copy(g, 21 + zz, full.at[slot], slot, lone(g, x), 1, x_side).start()
+
+    def service(i):
+        def on(g, act):
+            pl.when(jnp.logical_and(g >= 0, g < G_STAGES))(lambda: act(g))
+
+        on(i, issue)
+        for j in (1, 2, 3):
+            on(i - j, lambda g: along_z(g, j))
+        on(i - 1, lambda g: along_y(g, z))
+        for j in (1, 2, 3):
+            @pl.when(z >= j)
+            def _():
+                on(i - j - 1, lambda g: along_y(g, z - j))
+
+            @pl.when(z + j <= 3)
+            def _():
+                on(i - j - 1, lambda g: along_y(g, z + j))
+
+    def lone_in(first, last):
+        @pl.loop(first, last)
+        def _(g):
+            for k in range(1, 8):
+                arrived(g, lax.rem(t + k, 8), lone(g, 1 - x), 1)
+
+    def mod_row(image, k):
+        return mod[pl.ds(image * 8 + k, 1), :]
+
+    def by_rows(act):
+        for image in range(2):
+            @pl.loop(0, PATCH // CHUNK)
+            def _(i):
+                act(image, rows_at(image * PATCH + i * CHUNK, CHUNK))
+
+    service(0)
+
+    for k, p in enumerate(peers):
+        remote(mod_in.at[p], mod_all.at[p], ms.at[0], mr.at[p], (d, p)).wait_recv()
+    kept[1].wait()
+    total = ada[...]
+    for s in range(8):
+        total = total + wide(mod_all[s])
+    mod[...] = total * keep[...]
+
+    def first_rows(image, rows):
+        v = wide(tokens[rows, :])
+        n = v * lax.rsqrt(jnp.mean(v * v, axis=-1, keepdims=True) + epsilon)
+        fi[0, rows, :] = low(n * (1.0 + mod_row(image, 1)) + mod_row(image, 0))
+
+    by_rows(first_rows)
+    share_fi = remote(fi.at[0], fi.at[1], es.at[0], er.at[0], core)
+    share_fi.start()
+    service(1)
+
+    def feed_rows(image, rows):
+        fg[0, rows, :] = low(wide(out_grad[rows, :]) * mod_row(image, 5))
+
+    by_rows(feed_rows)
+    share_fg = remote(fg.at[0], fg.at[1], es.at[1], er.at[1], core)
+    share_fg.start()
+
+    @pl.loop(2, 7)
+    def _(i):
+        service(i)
+
+    kept[0].wait()
+    lone_in(0, 3)
+    share_fi.wait_recv()
+    share_fg.wait_recv()
+    saves = [
+        pltpu.make_async_copy(fi, fi_out, save.at[0]),
+        pltpu.make_async_copy(fg, fg_out, save.at[1]),
+        pltpu.make_async_copy(mod, mod_out, save.at[2]),
+    ]
+    for cp in saves:
+        cp.start()
+
+    def load_a(s):
+        return pltpu.make_async_copy(full.at[s, pl.ds(0, 3 * HEAD)], wa.at[lax.rem(s, 2)], ws.at[lax.rem(s, 2)])
+
+    load_o = pltpu.make_async_copy(full.at[:, pl.ds(3 * HEAD, HEAD)], ow, ls.at[3])
+    load_o.start()
+    load_a(0).start()
+
+    def save_head(s):
+        b = lax.rem(s, 2)
+        return [
+            pltpu.make_async_copy(qkv.at[b], qkv_out.at[s], qs.at[b, 0]),
+            pltpu.make_async_copy(norm.at[b], norm_out.at[s], qs.at[b, 1]),
+            pltpu.make_async_copy(stat.at[b], stat_out.at[s], qs.at[b, 2]),
+        ]
+
+    @pl.loop(0, 8)
+    def _(s):
+        b = lax.rem(s, 2)
+        load_a(s).wait()
+        pl.when(s < 7)(lambda: load_a(s + 1).start())
+
+        @pl.when(s > 1)
+        def _():
+            for cp in save_head(s - 2):
+                cp.wait()
+
+        bias_row = wide(mod_all[s, 6:7, :512])
+        bias_row = jnp.where(c == 0, bias_row[:, :256], bias_row[:, 256:])
+        bias = jnp.transpose(jnp.broadcast_to(bias_row, (128, 256)))[: 3 * HEAD, :1]
+        cos, sin = table[:HALF, :], table[HALF:, :]
+        for h in range(2):
+            raw = nt(wa[b], fi[h]) + bias
+            turned = []
+            for i in range(2):
+                v = raw[i * HEAD : (i + 1) * HEAD]
+                inv = lax.rsqrt(jnp.sum(v * v, axis=0, keepdims=True) * (1.0 / HD) + epsilon)
+                n = v * inv
+                norm[b, h, i * HEAD : (i + 1) * HEAD, :] = low(n)
+                stat[b, h, i : i + 1, :] = inv
+                turned.append(low(turn(n * gains[i * HEAD : (i + 1) * HEAD, :1], cos, sin)))
+            q, k = turned
+            v = low(raw[2 * HEAD :])
+            qkv[b, h, :HEAD, :] = q
+            qkv[b, h, HEAD : 2 * HEAD, :] = k
+            qkv[b, h, 2 * HEAD :, :] = v
+            for image in range(2):
+                cut = slice(image * PATCH, (image + 1) * PATCH)
+                e = jnp.exp(tn(k[:, cut], q[:, cut]) * FACTOR)
+                row_sum = jnp.sum(e, axis=0, keepdims=True)
+                stat[b, h, 2:3, cut] = jnp.log(row_sum)
+                p = low(e * (1.0 / row_sum))
+                mixed[h, pl.ds(pl.multiple_of(s * HEAD, 16), HEAD), cut] = low(nn(v[:, cut], p))
+        for cp in save_head(s):
+            cp.start()
+
+        @pl.when(lax.rem(s, 4) == 3)
+        def _():
+            service(7 + s // 4)
+
+    for s in (6, 7):
+        for cp in save_head(s):
+            cp.wait()
+    load_o.wait()
+    saves.append(pltpu.make_async_copy(mixed, mixed_out, save.at[3]))
+    saves[-1].start()
+
+    for image in range(2):
+        cut = slice(image * PATCH, (image + 1) * PATCH)
+        att_send[cut, :] = low(tn(mixed[1, :, cut], ow[...].reshape(8 * HEAD, D)))
+    share_att = remote(att_send, att_recv, es.at[2], er.at[2], core)
+    share_att.start()
+    for image in range(2):
+        cut = slice(image * PATCH, (image + 1) * PATCH)
+        att[cut, :] = tn(mixed[0, :, cut], ow[...].reshape(8 * HEAD, D))
+    share_att.wait_recv()
+
+    def second_rows(image, rows):
+        a = att[rows, :] + wide(att_recv[rows, :])
+        att[rows, :] = a
+        v = wide(tokens[rows, :]) + mod_row(image, 2) * a
+        n = v * lax.rsqrt(jnp.mean(v * v, axis=-1, keepdims=True) + epsilon)
+        si[0, rows, :] = low(n * (1.0 + mod_row(image, 4)) + mod_row(image, 3))
+
+    by_rows(second_rows)
+    share_si = remote(si.at[0], si.at[1], es.at[3], er.at[3], core)
+    share_si.start()
+    service(9)
+    lone_in(3, 6)
+    share_si.wait_recv()
+    saves += [
+        pltpu.make_async_copy(att, att_out, save.at[4]),
+        pltpu.make_async_copy(si, si_out, save.at[5]),
+    ]
+    saves[-2].start()
+    saves[-1].start()
+
+    def load_b(s):
+        return pltpu.make_async_copy(full.at[s, pl.ds(A_ROWS, B_ROWS)], wb.at[lax.rem(s, 2)], ws.at[2 + lax.rem(s, 2)])
+
+    def save_shard(s):
+        b = lax.rem(s, 2)
+        return [
+            pltpu.make_async_copy(gu.at[b], gu_out.at[s], hs.at[b, 0]),
+            pltpu.make_async_copy(hid.at[b], hid_out.at[s], hs.at[b, 1]),
+        ]
+
+    load_b(0).start()
+
+    @pl.loop(0, 8)
+    def _(s):
+        b = lax.rem(s, 2)
+        load_b(s).wait()
+        pl.when(s < 7)(lambda: load_b(s + 1).start())
+
+        @pl.when(s > 1)
+        def _():
+            for cp in save_shard(s - 2):
+                cp.wait()
+
+        for h in range(2):
+            both = nt(wb[b], si[h])
+            g, u = both[:SHARD_FF], both[SHARD_FF:]
+            gu[b, h] = low(both)
+            hid[b, h] = low(g * (1.0 / (1.0 + jnp.exp(-g))) * u)
+        for cp in save_shard(s):
+            cp.start()
+
+        pl.when(s == 3)(lambda: service(10))
+
+    lone_in(6, 7)
+    for s in (6, 7):
+        for cp in save_shard(s):
+            cp.wait()
+
+    @pl.loop(0, G_STAGES)
+    def _(g):
+        def sent(kind, rows):
+            copy(g, kind, own, t, rows, 0, x_side).wait_send()
+
+        sent(2, plane(g))
+        pl.when(z < 3)(lambda: sent(0, plane(g)))
+        pl.when(z > 0)(lambda: sent(1, plane(g)))
+        for k in range(4):
+            sent(21 + k, lone(g, x))
+        for j in (1, 2, 3):
+            @pl.when(z >= j)
+            def _():
+                pl.when(z < 3)(lambda: sent(1 + 2 * j, plane(g)))
+                sent(8 + j, plane(g))
+                sent(11 + j, lone(g, x))
+
+            @pl.when(z + j <= 3)
+            def _():
+                pl.when(z > 0)(lambda: sent(2 + 2 * j, plane(g)))
+                sent(14 + j, plane(g))
+                sent(17 + j, lone(g, x))
+
+    for cp in small + [share_fi, share_fg, share_att, share_si]:
+        cp.wait_send()
+    for g in groups:
+        remote(cond_in, cond_out.at[g], cs.at[0], cr.at[g], (g, t)).wait_recv()
+    kept[2].wait()
+    for cp in saves:
+        cp.wait()
+
+
+def forward(own, mod_in, cond_in, tokens, out_grad, ada, keep, gains, table):
+    dma = pltpu.SemaphoreType.DMA
+    vm = pltpu.VMEM
+    bf, f32 = jnp.bfloat16, jnp.float32
+    anywhere = pl.BlockSpec(memory_space=pl.ANY)
+    inside = pl.BlockSpec(memory_space=pltpu.VMEM)
+    R = tokens.shape[0]
+    outs = [
+        ((8, ROWS_ALL, D), bf), ((4,) + cond_in.shape, f32), ((16, D), f32),
+        ((2, R, D), bf), ((2, R, D), bf), ((2, R, D), bf), ((R, D), f32),
+        ((8, 2, 3 * HEAD, R), bf), ((8, 2, 2 * HEAD, R), bf), ((8, 2, 8, R), f32), ((2, 8 * HEAD, R), bf),
+        ((8, 2, B_ROWS, R), bf), ((8, 2, SHARD_FF, R), bf),
+    ]
+    return pl.pallas_call(
+        forward_kernel,
+        out_shape=tuple(jax.ShapeDtypeStruct(s, e) for s, e in outs),
+        in_specs=[anywhere] * 3 + [inside] * 6,
+        out_specs=(anywhere,) * len(outs),
+        scratch_shapes=[
+            vm((8, 16, D), bf), vm((16, D), f32),
+            vm((2, R, D), bf), vm((2, R, D), bf), vm((2, R, D), bf), vm((R, D), f32), vm((R, D), bf), vm((R, D), bf),
+            vm((2, 3 * HEAD, D), bf), vm((8, HEAD, D), bf), vm((2, 8 * HEAD, R), bf),
+            vm((2, 2, 3 * HEAD, R), bf), vm((2, 2, 2 * HEAD, R), bf), vm((2, 2, 8, R), f32),
+            vm((2, B_ROWS, D), bf), vm((2, 2, B_ROWS, R), bf), vm((2, 2, SHARD_FF, R), bf),
+            dma((G_STAGES, 25)), dma((G_STAGES, 8, 2)), dma((7,)), dma((8,)), dma((3,)), dma((4,)),
+            dma((4,)), dma((4,)), dma((4,)), dma((2, 3)), dma((2, 2)), dma((4,)), dma((6,)),
+        ],
+        compiler_params=pltpu.CompilerParams(
+            collective_id=0, has_side_effects=True, vmem_limit_bytes=60 * 2**20),
+        name="forward",
+    )(own, mod_in, cond_in, tokens, out_grad, ada, keep, gains, table)
+
+
+def reduce_kernel(part_in, pay, out, pay_all, part, xin, yin, zin, fin, xs, xr, ys, yr, zs, zr, fs, fr, ps, pr, ls):
+    x, c, z, y = place()
+    t = z * 2 + y
+    me = (x * 2 + c) * 8 + t
+    targets = [lax.rem(me + k, 32) for k in range(1, 32)]
+    greet([(o // 8, o % 8) for o in targets])
+    load = pltpu.make_async_copy(part_in, part, ls.at[0])
+    load.start()
+    keep = pltpu.make_async_copy(pay, pay_all.at[me], ls.at[1])
+    keep.start()
+
+    def pay_copy(k):
+        o = lax.rem(me + k, 32)
+        return pltpu.make_async_remote_copy(
+            src_ref=pay, dst_ref=pay_all.at[me], send_sem=ps.at[k], recv_sem=pr.at[k],
+            device_id=(o // 8, o % 8), device_id_type=MESH)
+
+    @pl.loop(1, 32)
+    def _(k):
+        pay_copy(k).start()
+
+    y_side, x_side, core = at(x, c, z, 1 - y), at(1 - x, c, z, y), at(x, 1 - c, z, y)
+    up, down = at(x, c, z + 1, y), at(x, c, z - 1, y)
+    keep.wait()
+    load.wait()
+
+    def lone(g, side):
+        return g * R_STAGE + side * (R_STAGE - R_LONE)
+
+    def plane(g):
+        return g * R_STAGE + x * R_LONE
+
+    PL = R_STAGE - R_LONE
+    MID = R_STAGE - 2 * R_LONE
+
+    def xcopy(g, side):
+        yy = 1 - y if side == 0 else y
+        return remote(
+            part.at[:, yy, rows_at(lone(g, 1 - x), R_LONE)], xin.at[:, yy, rows_at(g * R_LONE, R_LONE)],
+            xs.at[g, side], xr.at[g, side], x_side)
+
+    def ycopy(g):
+        return remote(
+            part.at[:, 1 - y, rows_at(plane(g), PL)], yin.at[:, rows_at(g * PL, PL)],
+            ys.at[g], yr.at[g], y_side)
+
+    def zcopy(g, to_z, way):
+        return remote(
+            part.at[to_z, y, rows_at(plane(g), PL)], zin.at[way, to_z, rows_at(g * PL, PL)],
+            zs.at[g, way, to_z], zr.at[g, way, to_z], up if way == 0 else down)
+
+    def fcopy(g, what):
+        if what == 0:
+            rows = rows_at(lone(g, x), R_LONE)
+            return remote(out.at[c, rows], out.at[c, rows], fs.at[g, 0], fr.at[g, 0], x_side)
+        rows = rows_at(g * R_STAGE + R_LONE, MID)
+        return remote(part.at[z, y, rows], fin.at[rows], fs.at[g, 1], fr.at[g, 1], x_side)
+
+    def add(zz, yy, first, rows, piece):
+        @pl.loop(0, rows // 16)
+        def _(i):
+            a = rows_at(first + i * 16, 16)
+            part[zz, yy, a, :] = (
+                part[zz, yy, a, :].astype(jnp.float32) + piece(i).astype(jnp.float32)).astype(jnp.bfloat16)
+
+    def x_stage(g, side):
+        yy = 1 - y if side == 0 else y
+        xcopy(g, side).wait_recv()
+
+        @pl.loop(0, 4)
+        def _(k):
+            add(k, yy, lone(g, x), R_LONE, lambda r: xin[k, yy, rows_at(g * R_LONE + r * 16, 16), :])
+
+        if side == 0:
+            ycopy(g).start()
+
+    def y_stage(g):
+        ycopy(g).wait_recv()
+
+        @pl.loop(0, 4)
+        def _(k):
+            add(k, y, plane(g), PL, lambda r: yin[k, rows_at(g * PL + r * 16, 16), :])
+
+    def take(g, way, to_z):
+        zcopy(g, to_z, way).wait_recv()
+        add(to_z, y, plane(g), PL, lambda r: zin[way, to_z, rows_at(g * PL + r * 16, 16), :])
+
+    def up_stage(g):
+        for j in (3, 2, 1):
+            @pl.when(z + j <= 3)
+            def _():
+                pl.when(z > 0)(lambda: take(g, 0, z + j))
+                zcopy(g, z + j, 0).start()
+
+    def down_stage(g):
+        for j in (3, 2, 1):
+            @pl.when(z >= j)
+            def _():
+                pl.when(z < 3)(lambda: take(g, 1, z - j))
+                zcopy(g, z - j, 1).start()
+
+    def own_stage(g):
+        pl.when(z > 0)(lambda: take(g, 0, z))
+        pl.when(z < 3)(lambda: take(g, 1, z))
+        rows = lone(g, x)
+        out[c, rows_at(rows, R_LONE), :] = part[z, y, rows_at(rows, R_LONE), :]
+        fcopy(g, 0).start()
+        fcopy(g, 1).start()
+
+    def f_stage(g):
+        fcopy(g, 0).wait_recv()
+        fcopy(g, 1).wait_recv()
+        first = g * R_STAGE + R_LONE
+
+        @pl.loop(0, MID // 16)
+        def _(i):
+            a = rows_at(first + i * 16, 16)
+            out[c, a, :] = (part[z, y, a, :].astype(jnp.float32) + fin[a, :].astype(jnp.float32)).astype(jnp.bfloat16)
+
+        rows = rows_at(g * R_STAGE, R_STAGE)
+        remote(out.at[c, rows], out.at[c, rows], fs.at[g, 2], fr.at[g, 2], core).start()
+
+    def x_send(g):
+        xcopy(g, 0).start()
+        xcopy(g, 1).start()
+
+    x_send(0)
+    x_send(1)
+
+    def service(i):
+        def on(g, act):
+            pl.when(jnp.logical_and(g >= 0, g < R_STAGES))(lambda: act(g))
+
+        on(i, lambda g: x_stage(g, 0))
+        on(i, lambda g: x_stage(g, 1))
+        on(i + 2, x_send)
+        on(i - 1, y_stage)
+        on(i - 1 - z, up_stage)
+        on(i - 4 + z, down_stage)
+        on(i - 4, own_stage)
+        on(i - 5, f_stage)
+
+    @pl.loop(0, R_STAGES + 5)
+    def _(i):
+        service(i)
+
+    @pl.loop(0, R_STAGES)
+    def _(g):
+        xcopy(g, 0).wait_send()
+        xcopy(g, 1).wait_send()
+        ycopy(g).wait_send()
+
+        for j in (3, 2, 1):
+            pl.when(z + j <= 3)(lambda: zcopy(g, z + j, 0).wait_send())
+            pl.when(z >= j)(lambda: zcopy(g, z - j, 1).wait_send())
+        fcopy(g, 0).wait_send()
+        fcopy(g, 1).wait_send()
+        rows = rows_at(g * R_STAGE, R_STAGE)
+        mine = remote(out.at[c, rows], out.at[c, rows], fs.at[g, 2], fr.at[g, 2], core)
+        mine.wait_send()
+        remote(out.at[c, rows], out.at[1 - c, rows], fs.at[g, 2], fr.at[g, 2], core).wait_recv()
+
+    @pl.loop(1, 32)
+    def _(k):
+        pay_copy(k).wait()
+
+
+def reduce_grads(part, pay):
+    vm = pltpu.VMEM
+    dma = pltpu.SemaphoreType.DMA
+    PL = R_STAGE - R_LONE
+    anywhere = pl.BlockSpec(memory_space=pl.ANY)
+    return pl.pallas_call(
+        reduce_kernel,
+        out_shape=(
+            jax.ShapeDtypeStruct((2, ROWS_ALL, D), jnp.bfloat16),
+            jax.ShapeDtypeStruct((32, PAY, D), jnp.bfloat16),
+        ),
+        in_specs=[anywhere, anywhere],
+        out_specs=(pl.BlockSpec(memory_space=pltpu.VMEM), anywhere),
+        scratch_shapes=[
+            vm((4, 2, ROWS_ALL, D), jnp.bfloat16),
+            vm((4, 2, R_STAGES * R_LONE, D), jnp.bfloat16),
+            vm((4, R_STAGES * PL, D), jnp.bfloat16),
+            vm((2, 4, R_STAGES * PL, D), jnp.bfloat16),
+            vm((ROWS_ALL, D), jnp.bfloat16),
+            dma((R_STAGES, 2)), dma((R_STAGES, 2)), dma((R_STAGES,)), dma((R_STAGES,)),
+            dma((R_STAGES, 2, 4)), dma((R_STAGES, 2, 4)), dma((R_STAGES, 3)), dma((R_STAGES, 3)),
+            dma((32,)), dma((32,)), dma((2,)),
+        ],
+        compiler_params=pltpu.CompilerParams(
+            collective_id=1, has_side_effects=True, vmem_limit_bytes=60 * 2**20),
+        name="reduce_grads",
+    )(part.reshape(4, 2, ROWS_ALL, D), pay)
+
+
+def normalize(vectors, axis=-1, count=None):
+    count = count or vectors.shape[axis]
+    inverse = lax.rsqrt(jnp.sum(vectors * vectors, axis=axis, keepdims=True) / count + epsilon)
     return (vectors * inverse, inverse)
 
 
-def normalize_back(grad, normed, inverse):
-    return inverse * (grad - normed * jnp.mean(grad * normed, axis=-1, keepdims=True))
+def normalize_back(grad, normed, inverse, axis=-1, count=None):
+    count = count or grad.shape[axis]
+    return inverse * (grad - normed * (jnp.sum(grad * normed, axis=axis, keepdims=True) / count))
+
+
+def silu_slope(values):
+    sigma = jax.nn.sigmoid(values)
+    return sigma * (1.0 + values * (1.0 - sigma))
+
+
+def pair_rows(heads):
+    lead, n = heads.shape[:-2], heads.shape[-1]
+    split = heads.reshape(lead + (2, 2, 18, n))
+    split = jnp.swapaxes(split, -4, -3).reshape(lead + (2, 36, n))
+    return jnp.pad(split, [(0, 0)] * len(lead) + [(0, 0), (0, 4), (0, 0)]).reshape(lead + (HEAD, n))
+
+
+def unpair_rows(rows):
+    lead, n = rows.shape[:-2], rows.shape[-1]
+    split = rows.reshape(lead + (2, HALF, n))[..., :36, :].reshape(lead + (2, 2, 18, n))
+    return jnp.swapaxes(split, -4, -3).reshape(lead + (HD, n))
+
+
+def pad_rows(rows):
+    return jnp.pad(rows, [(0, 0)] * (rows.ndim - 2) + [(0, 8), (0, 0)])
+
+
+def pair_tables():
+    pairs = HD // 4
+    theta = np.exp(-math.log(100.0) * np.arange(pairs, dtype=np.float32) / pairs)
+    spot = np.arange(PATCH)
+    angle = np.concatenate([theta[:, None] * (spot // GRID)[None], theta[:, None] * (spot % GRID)[None]])
+    pad = ((0, HALF - 36), (0, 0))
+    return (
+        np.pad(np.cos(angle), pad).astype(np.float32),
+        np.pad(np.sin(angle), pad).astype(np.float32),
+    )
+
+
+def rotate_pairs(v, cos, sin):
+    a, b = v[..., :HALF, :], v[..., HALF:, :]
+    return jnp.concatenate([a * cos - b * sin, b * cos + a * sin], axis=-2)
+
+
+def pack_weights(qkv_weight, out_weight, gate_up_weight, down_weight, c):
+    heads = lax.dynamic_slice_in_dim(qkv_weight, c * HD, HD, 2).transpose(1, 2, 0)
+    qk = pair_rows(heads[:2]).reshape(2 * HEAD, D)
+    v = pad_rows(heads[2])
+    o = pad_rows(lax.dynamic_slice_in_dim(out_weight, c * HD, HD, 0))
+    gu = lax.dynamic_slice_in_dim(gate_up_weight, c * SHARD_FF, SHARD_FF, 2)
+    gu = gu.transpose(1, 2, 0).reshape(B_ROWS, D)
+    dn = lax.dynamic_slice_in_dim(down_weight, c * SHARD_FF, SHARD_FF, 0)
+    return jnp.concatenate([qk, v, o, gu, dn], axis=0)
+
+
+def unpack_grads(both):
+    both = both.astype(jnp.float32)
+    qk = unpair_rows(both[:, : 2 * HEAD].reshape(2, 2, HEAD, D))
+    v = both[:, 2 * HEAD : 2 * HEAD + HD].reshape(2, 1, HD, D)
+    qkv = jnp.concatenate([qk, v], axis=1).transpose(3, 1, 0, 2).reshape(D, 3, 2 * HD)
+    o = both[:, 3 * HEAD : 3 * HEAD + HD].reshape(2 * HD, D)
+    gu = both[:, A_ROWS : A_ROWS + B_ROWS].reshape(2, 2, SHARD_FF, D)
+    gu = gu.transpose(3, 1, 0, 2).reshape(D, 2, 2 * SHARD_FF)
+    dn = both[:, A_ROWS + B_ROWS :].reshape(2 * SHARD_FF, D)
+    return qkv, o, gu, dn
+
+
+def fast(
+    tokens, labels, timesteps, image_counts, class_table, ada_weight, ada_bias,
+    qkv_weight, qkv_bias, qk_scale, out_weight, gate_up_weight, down_weight, out_grad,
+):
+    dot = lambda s, a, b: jnp.einsum(s, a, b, preferred_element_type=jnp.float32)
+    t = lax.axis_index("tensor")
+    c = lax.axis_index("dp") % 2
+    own = pack_weights(qkv_weight, out_weight, gate_up_weight, down_weight, c)
+    sib = lambda v: lax.ppermute(v, "dp", [(0, 1), (1, 0), (2, 3), (3, 2)])
+    both = lambda v: jnp.concatenate([v, sib(v)])
+    half = tokens.shape[0]
+    images = labels.shape[0]
+    meet = lambda v: v[:half] + sib(low(v[half:])).astype(jnp.float32)
+
+    columns_here = class_table.shape[1]
+    column = t * columns_here + jnp.arange(columns_here)
+    half_width = D // 2
+    frequency = jnp.exp(-math.log(10000.0) * (column % half_width).astype(jnp.float32) / half_width)
+    angles = timesteps.astype(jnp.float32)[:, None] * frequency[None, :]
+    time_embed = jnp.where(column[None, :] < half_width, jnp.cos(angles), jnp.sin(angles))
+    classes = jnp.arange(class_table.shape[0])
+    condition = dot("in,nc->ic", low(labels[:, None] == classes[None, :]), class_table) + time_embed
+    mod_part = dot("ic,ckd->ikd", low(jax.nn.silu(condition)), ada_weight)
+    heads = qkv_bias.reshape(3, 2, HD).swapaxes(0, 1)[..., None]
+    bias_row = jnp.concatenate([pair_rows(heads[:, :2]).reshape(2, -1), pad_rows(heads[:, 2])[..., 0]], axis=1)
+    bias_row = jnp.pad(bias_row, ((0, 0), (0, 16))).reshape(1, 1, -1)
+    bias_row = jnp.pad(bias_row, ((0, 0), (0, 0), (0, D - bias_row.size)))
+    bias_row = jnp.broadcast_to(bias_row, (images, 1, D))
+    mod_part = jnp.concatenate([low(mod_part), bias_row, jnp.zeros_like(bias_row)], axis=1)
+    cond_part = jnp.concatenate(
+        [condition, labels.astype(jnp.float32)[:, None], jnp.zeros((images, 256 - columns_here - 1), jnp.float32)], axis=1)
+    mod_images = images // 8
+    kept = (t * mod_images + jnp.arange(mod_images) < image_counts[0]).astype(jnp.float32)
+    ada = jnp.pad(ada_bias.astype(jnp.float32), ((0, 2), (0, 0)))
+    ada = jnp.tile(ada, (mod_images, 1))
+    gate_rows = jnp.array([0, 0, 1, 0, 0, 1, 0, 0], jnp.float32)
+    keep = jnp.where(gate_rows[None, :] > 0, kept[:, None], 1.0).reshape(-1, 1)
+    keep = jnp.broadcast_to(keep, ada.shape)
+    gain_rows = jnp.broadcast_to(pair_rows(qk_scale.astype(jnp.float32)[..., None]).reshape(2 * HEAD, 1), (2 * HEAD, 128))
+    cos, sin = pair_tables()
+    table = np.tile(np.concatenate([cos, sin]), (1, tokens.shape[0] // PATCH))
+    (weights, cond_all, mod, first_in, second_in, feed_grad, attention, qkv_t, norm_t, stat_t, mixed, gu_t, hidden) = forward(
+        own, mod_part.reshape(8, images, D), cond_part, tokens, out_grad, ada, keep, gain_rows, table)
+    cond_all = cond_all.reshape(4 * images, 256)
+    condition = cond_all[:, :columns_here]
+    labels_all = cond_all[:, columns_here].astype(jnp.int32)
+    chosen = low(labels_all[:, None] == classes[None, :])
+    cond_act = low(jax.nn.silu(condition))
+    first_image = lax.axis_index("dp") * images
+    mod = mod.reshape(mod_images, 8, D)
+    mod_rows = jnp.repeat(mod, PATCH, axis=0)
+    shift_one, scale_one, gate_one, shift_two, scale_two, gate_two = [mod_rows[:, i] for i in range(6)]
+    gains = pair_rows(qk_scale.astype(jnp.float32)[..., None])
+    cos, sin = np.tile(cos, (1, 4)), np.tile(sin, (1, 4))
+    flat = lambda v: v.swapaxes(-3, -2).reshape(v.shape[:-3] + (v.shape[-2], 1024))
+    qkv_t, norm_t, stat_t, gu_t, hidden = [flat(v) for v in (qkv_t, norm_t, stat_t, gu_t, hidden)]
+    mixed = flat(mixed).reshape(8, HEAD, 1024)
+    first_in, second_in, feed_grad = [v.reshape(1024, D) for v in (first_in, second_in, feed_grad)]
+    q_t, k_t, v_t = [qkv_t[:, i * HEAD : (i + 1) * HEAD] for i in range(3)]
+    q_norm, k_norm = [norm_t[:, i * HEAD : (i + 1) * HEAD].astype(jnp.float32) for i in range(2)]
+    q_inv, k_inv, logsum = [stat_t[:, i : i + 1] for i in range(3)]
+    g, u = [gu_t[:, i * SHARD_FF : (i + 1) * SHARD_FF].astype(jnp.float32) for i in range(2)]
+    act = jax.nn.silu(g)
+    factor = FACTOR
+    cut = lambda v: v.reshape(8, HEAD, 4, PATCH)
+    scores = dot("heiq,heik->hikq", cut(q_t), cut(k_t)) * factor
+    prob = jnp.exp(scores - logsum.reshape(8, 4, 1, PATCH))
+    prob_low = low(prob)
+    wo = weights[:, 3 * HEAD : 4 * HEAD]
+    wg = weights[:, A_ROWS : A_ROWS + SHARD_FF]
+    wu = weights[:, A_ROWS + SHARD_FF : A_ROWS + B_ROWS]
+    wd = weights[:, A_ROWS + B_ROWS :]
+    tokens_f = tokens.astype(jnp.float32)
+    first_norm, first_inverse = normalize(tokens_f)
+    after_attn = tokens_f + gate_one * attention
+    second_norm, second_inverse = normalize(after_attn)
+    feed = meet(dot("sfn,sfd->nd", hidden, wd))
+    result = low(after_attn + gate_two * feed)
+
+    grad_out = out_grad.astype(jnp.float32)
+    hidden_grad = dot("sfd,nd->sfn", wd, feed_grad)
+    g_grad = low(hidden_grad * u * silu_slope(g))
+    u_grad = low(hidden_grad * act)
+    d_part = low(dot("sfn,nd->sfd", hidden, feed_grad))
+    g_part = low(dot("sfn,nd->sfd", g_grad, second_in))
+    u_part = low(dot("sfn,nd->sfd", u_grad, second_in))
+    second_grad = meet(dot("sfn,sfd->nd", g_grad, wg) + dot("sfn,sfd->nd", u_grad, wu))
+    after_grad = grad_out + normalize_back(second_grad * (1.0 + scale_two), second_norm, second_inverse)
+    attn_grad = both(low(after_grad * gate_one))
+    mixed_grad = low(dot("hed,nd->hen", wo, attn_grad))
+    o_part = low(dot("hen,nd->hed", mixed, attn_grad))
+    v_grad = low(dot("hikq,heiq->heik", prob_low, cut(mixed_grad))).reshape(8, HEAD, 1024)
+    prob_grad = dot("heik,heiq->hikq", cut(v_t), cut(mixed_grad))
+    score_grad = low(prob * (prob_grad - jnp.sum(prob * prob_grad, axis=2, keepdims=True)))
+    q_back = dot("hikq,heik->heiq", score_grad, cut(k_t)).reshape(8, HEAD, 1024) * factor
+    k_back = dot("hikq,heiq->heik", score_grad, cut(q_t)).reshape(8, HEAD, 1024) * factor
+    q_back = rotate_pairs(q_back, cos, -sin)
+    k_back = rotate_pairs(k_back, cos, -sin)
+    scale_part = jnp.stack([jnp.sum(q_back * q_norm, axis=(0, 2)), jnp.sum(k_back * k_norm, axis=(0, 2))])
+    q_grad = low(normalize_back(q_back * gains[0], q_norm, q_inv, 1, HD))
+    k_grad = low(normalize_back(k_back * gains[1], k_norm, k_inv, 1, HD))
+    qkv_grad = jnp.concatenate([q_grad, k_grad, v_grad], axis=1)
+    bias_part = jnp.sum(qkv_grad.astype(jnp.float32), axis=2)
+    qkv_part = low(dot("hen,nd->hed", qkv_grad, first_in))
+    first_grad = meet(dot("hen,hed->nd", qkv_grad, weights[:, : 3 * HEAD]))
+    tokens_grad = after_grad + normalize_back(first_grad * (1.0 + scale_one), first_norm, first_inverse)
+
+    per_image = lambda v: jnp.sum(v.reshape(mod_images, PATCH, D), axis=1)
+    mod_grad = low(jnp.stack([
+        per_image(first_grad), per_image(first_grad * first_norm), per_image(after_grad * attention) * kept[:, None],
+        per_image(second_grad), per_image(second_grad * second_norm), per_image(grad_out * feed) * kept[:, None],
+    ], axis=1))
+    tail = jnp.concatenate([low(bias_part).reshape(-1), low(scale_part).reshape(-1)])
+    tail = jnp.pad(tail, (0, (PAY - 6 * mod_images) * D - tail.size)).reshape(-1, D)
+    pay = jnp.concatenate([mod_grad.reshape(6 * mod_images, D), tail], axis=0)
+    summed, pay_all = reduce_grads(jnp.concatenate([qkv_part, o_part, g_part, u_part, d_part], axis=1), pay)
+    qkv_weight_grad, out_weight_grad, gate_up_grad, down_grad = unpack_grads(summed)
+
+    mod_grad = pay_all[:, : 6 * mod_images].reshape(-1, 6, D)
+    tail = pay_all[:, 6 * mod_images :].reshape(32, -1).astype(jnp.float32)
+    bias_all = tail[:, : bias_part.size].reshape(32, 8, 3 * HEAD)
+    scale_all = tail[:, bias_part.size : bias_part.size + scale_part.size].reshape(32, 2, HEAD)
+    qk_scale_grad = unpair_rows(jnp.sum(scale_all, axis=0)[..., None])[..., 0]
+    bias_all = lax.dynamic_index_in_dim(bias_all, t, 1, keepdims=False).reshape(2, 2, 8, 3, HEAD)
+    bias_sum = jnp.sum(bias_all, axis=(0, 2))
+    qk_bias = unpair_rows(bias_sum[:, :2, :, None])[..., 0]
+    qkv_bias_grad = jnp.concatenate([qk_bias, bias_sum[:, 2:, :HD]], axis=1).transpose(1, 0, 2).reshape(3, 2 * HD)
+
+    ada_weight_grad = dot("ic,ikd->ckd", cond_act, mod_grad)
+    ada_bias_grad = jnp.sum(mod_grad.astype(jnp.float32), axis=0)
+    act_grad = dot("ikd,ckd->ic", mod_grad, ada_weight)
+    cond_grad_all = act_grad * silu_slope(condition)
+    table_grad = jnp.dot(chosen.astype(jnp.float32).T, cond_grad_all, precision=HIGH)
+    cond_grad = lax.dynamic_slice_in_dim(cond_grad_all, first_image, images, 0)
+    return (
+        result, tokens_grad, cond_grad, table_grad, ada_weight_grad, ada_bias_grad,
+        qkv_weight_grad, qkv_bias_grad, qk_scale_grad, out_weight_grad, gate_up_grad, down_grad,
+    )
 
 
 def rope_tables(count):
@@ -53,12 +868,7 @@
     )
 
 
-def silu_slope(values):
-    sigma = jax.nn.sigmoid(values)
-    return sigma * (1.0 + values * (1.0 - sigma))
-
-
-def local(
+def general(
     tokens,
     labels,
     timesteps,
@@ -307,8 +1117,9 @@
         P("tensor", None),
         P(("dp", "tensor"), None),
     )
+    plain = mesh.shape["dp"] != 4 or mesh.shape["tensor"] != 8
     return jax.shard_map(
-        local,
+        general if plain else fast,
         mesh=mesh,
         in_specs=placed,
         out_specs=(

time: 1710 us -> 627 us (0.37)
  waiting for transfers between devices: 1360 us -> 0.01 us
  Pallas kernels: 0 us -> 344 us
  matrix products: 154 us -> 97 us
  local copies, waits for them, and re-layouts: 69.1 us -> 120 us
  blocking collectives: 32 us -> 0 us
  other arithmetic: 77.1 us -> 53.9 us
    reduce_scatter x4 -> x0, waiting for transfers between devices: 609 us -> none  [the longest x1 163 us: local(): lax.psum_scatter(jnp.dot(hidden, down_weight, preferred_element_type=jnp....]
    all_gather x4 -> x0, waiting for transfers between devices: 533 us -> none  [the longest x1 137 us: local(): lax.all_gather(attention_grad, 'tensor', axis=0, tiled=True)]
    pallas_call x0 -> x2, Pallas kernels: none -> 344 us  [the longest x1 181 us: reduce_grads(): pl.pallas_call(reduce_kernel, out_shape=(jax.ShapeDtypeStruct((2, ROWS_AL...]
    psum x3 -> x0, waiting for transfers between devices: 216 us -> none  [the longest x1 79.3 us: local(): lax.psum(gate_up_grad.astype(jnp.bfloat16), 'dp').astype(jnp.float32)]
    dot_general x23 -> x21, matrix products: 141 us -> 97 us  [the longest x20 95.7 us: fast(): jnp.einsum(s, a, b, preferred_element_type=jnp.float32)]
    psum x2 -> x0, blocking collectives: 32 us -> none  [the longest x1 19.7 us: local(): lax.psum(scale_part.astype(jnp.bfloat16), 'tensor').astype(jnp.float32)]
    transpose x1 -> x10, local copies, waits for them, and re-layouts: 0.41 us -> 21.4 us  [the longest x2 12.4 us: fast(): v.swapaxes(-3, -2).reshape(v.shape[:-3] + (v.shape[-2], 1024))]
    slice x1 -> x18, local copies, waits for them, and re-layouts: 0.15 us -> 18.7 us  [the longest x1 6.61 us: fast(): gu_t[:, i * SHARD_FF:(i + 1) * SHARD_FF].astype(jnp.float32)]
  transfers between devices with their start and end apart: 11 -> 4, of which waited for: 11 -> 0; matrix products, arithmetic and copies ran while one was open for 4% -> 21% of each run, Pallas kernels for 0% -> 0%
where the time goes in v1:
time: 627 us; the launch traced here: 618 us
  Pallas kernels  344 us (55%)
  local copies, waits for them, and re-layouts  120 us (19%)
  matrix products  97 us (15%)
  other arithmetic  53.9 us (9%)
    pallas_call x1, Pallas kernels, reduce_grads(): pl.pallas_call(reduce_kernel, out_shape=(jax.ShapeDtypeStruct((2, ROWS_AL...  181 us
    pallas_call x1, Pallas kernels, forward(): pl.pallas_call(forward_kernel, out_shape=tuple((jax.ShapeDtypeStruct(s, e...  162 us
    dot_general x20, matrix products, fast(): jnp.einsum(s, a, b, preferred_element_type=jnp.float32)  95.7 us
    unnamed x130, local copies, waits for them, and re-layouts  38.6 us
  transfers between devices with their start and end apart: 4, of which 0 were waited for; matrix products, arithmetic and copies ran while one was open for 21% of the time, Pallas kernels for 0%

profile of v1, /device:TPU:0, one launch (start us, length us, event | category | flops | bytes accessed | tf_op | source)
XLA Modules:
  0.0 618.4 jit_solution(3128177517572347506)
XLA Ops:
  13.6 3.1 dynamic-slice_bitcast_fusion
  16.7 2.9 copy.119
  25.0 2.1 constant_dynamic-update-slice_fusion
  29.4 162.3 %forward.1 = (bf16[8,896,1152]{2,1,0:T(8,128)(2,1)}, f32[4,16,256]{2,1,0:T(8,128)}, f32[16,1152]{1,0:T(8,128)}, bf16[2,512,1152]{2,1,0:T(8,128)(2,1)}, bf16[2,51...) custom-call(bf16[896,1152]{1,0:T(8,128)(2,1)} %dynamic-slice_dynamic, ...), custom_call_target="tpu_custom_call" | custom-call | tf_op jit(solution)/shard_map/forward/pallas_call | solution.py:412
  191.6 2.3 copy.165
  193.9 6.5 %convolution_bitcast_fusion = f32[1024,1152]{1,0:T(8,128)S(1)} fusion(bf16[8,192,1024]{2,1,0:T(8,128)(2,1)S(1)} %bitcast.302, bf16[8,896,1152]{2,1,0:T(8,128)(2,1)} %get-tuple-element.30), kind=kOutput, calls=%fused_computation.28 | convolution fusion | flops 3623878656 | bytes 11403264 | tf_op jit(solution)/shard_map/sfn,sfd->nd/dot_general | solution.py:705
  200.4 2.1 copy-done.24
  203.6 8.6 %copy.126 = bf16[8,384,2,512]{1,3,2,0:T(8,128)(2,1)} copy(bf16[8,384,2,512]{3,1,2,0:T(8,128)(2,1)} %bitcast.289) | data formatting | bytes 12582912 | tf_op jit(solution)/shard_map/transpose | solution.py:755
  212.3 6.6 %fusion.112 = (bf16[8,192,1024]{1,2,0:T(8,128)(2,1)}, bf16[8,192,1024]{1,2,0:T(8,128)(2,1)}) fusion(bf16[8,384,1024]{1,2,0:T(8,128)(2,1)} %bitcast.272), kind=kLoop, calls=%fused_computation.223 | loop fusion | bytes 12582912 | tf_op jit(solution)/shard_map/slice | solution.py:762
  218.9 6.1 copy.157
  225.0 6.5 %copy.158 = bf16[8,192,1024]{2,1,0:T(8,128)(2,1)} copy(bf16[8,192,1024]{1,2,0:T(8,128)(2,1)} %get-tuple-element.94) | data formatting | bytes 6291456
  231.6 13.3 %fusion.6 = (bf16[8,192,1024]{2,1,0:T(8,128)(2,1)S(1)}, f32[8,192,1024]{2,1,0:T(8,128)}) fusion(bf16[8,192,1024]{2,1,0:T(8,128)(2,1)} %copy.158, bf16[8,192,1024]{2,1,0:T(8,128)(2,1)} %copy.157, bf16[1024,1152,1]{1,0,2:T(8,128)(2,1)} %bitcast.331, bf16[8,896,1152]{2,1,0:T(8,128)(2,1)} %get-tuple-element.30), kind=kOutput, calls=%fused_computation.13 | convolution fusion | flops 3642753024 | bytes 21626880 | tf_op jit(solution)/shard_map/sfd,nd->sfn/dot_general | solution.py:705
  244.8 7.7 %fusion.24 = f32[1024,1152,1]{1,0,2:T(8,128)S(1)} fusion(bf16[8,192,1024]{2,1,0:T(8,128)(2,1)S(1)} %get-tuple-element.112, bf16[8,896,1152]{2,1,0:T(8,128)(2,1)} %get-tuple-element.30), kind=kOutput, calls=%fused_computation.40 | convolution fusion | flops 3623878656 | bytes 11403264 | tf_op jit(solution)/shard_map/sfn,sfd->nd/dot_general | solution.py:705
  252.5 9.1 %bitcast_add_fusion = f32[1024,1152]{1,0:T(8,128)S(1)} fusion(f32[1024,1152,1]{1,0,2:T(8,128)S(1)} %fusion.24, bf16[8,896,1152]{2,1,0:T(8,128)(2,1)} %get-tuple-element.30, f32[8,192,1024]{2,1,0:T(8,128)} %get-tuple-element.113, bf16[8,192,1024]{2,1,0:T(8,128)(2,1)S(1)} %copy-done.29), kind=kOutput, calls=%fused_computation.19 | convolution fusion | flops 3636068352 | bytes 22413312 | tf_op jit(solution)/shard_map/sfn,sfd->nd/dot_general | solution.py:705
  263.1 7.7 %broadcast_in_dim.101 = f32[2,256,8,1152]{3,1,0,2:T(8,128)} broadcast(f32[2,8,1152]{2,0,1:T(2,128)S(1)} %copy.124), dimensions={0,2,3} | broadcast | bytes 18948096 | tf_op jit(solution)/shard_map/broadcast_in_dim | solution.py:751
  270.8 2.5 multiply_reduce_fusion.2
  275.3 2.1 fusion.113
  277.3 2.9 multiply_reduce_fusion.1
  280.3 5.0 fusion.111
  285.3 3.7 multiply_convert_fusion.1
  289.8 3.7 copy.141
  293.5 4.5 reshape_reshape.15
  298.0 3.6 copy.168
  301.9 3.2 fusion.70
  305.0 2.4 bitcast_reduce_fusion.1
  308.8 2.4 bitcast_reduce_fusion
  311.2 4.0 convolution_convert_fusion.5
  316.8 2.3 multiply_reduce_fusion
  319.2 2.3 multiply_convert_fusion
  330.1 4.5 fusion.37
  334.7 7.9 %fusion.16 = f32[1024,1152]{1,0:T(8,128)S(1)} fusion(bf16[8,896,1152]{2,1,0:T(8,128)(2,1)} %get-tuple-element.30, bf16[8,80,1024]{2,1,0:T(8,128)(2,1)S(1)} %bitcast.296, bf16[8,80,1024]{2,1,0:T(8,128)(2,1)S(1)} %get-tuple-element.103, bf16[8,80,1024]{2,1,0:T(8,128)(2,1)S(1)} %get-tuple-element.102), kind=kOutput, calls=%fused_computation.27 | convolution fusion | flops 4541644800 | bytes 13074432 | tf_op jit(solution)/shard_map/hen,hed->nd/dot_general | solution.py:705
  343.7 2.2 copy-done.46
  346.0 6.8 %fusion.10 = bf16[8,896,1152]{2,1,0:T(8,128)(2,1)} fusion(bf16[1024,1152,1]{1,0,2:T(8,128)(2,1)S(1)} %bitcast.334, bf16[8,80,1024]{2,1,0:T(8,128)(2,1)S(1)} %bitcast.297, bf16[8,80,1024]{2,1,0:T(8,128)(2,1)S(1)} %get-tuple-element.103, bf16[8,80,1024]{2,1,0:T(8,128)(2,1)S(1)} %get-tuple-element.102), kind=kOutput, calls=%fused_computation.18 | convolution fusion | flops 4543856640 | bytes 10715136 | tf_op jit(solution)/shard_map/hen,nd->hed/dot_general | solution.py:705
  352.8 4.8 fusion.29
  357.6 5.7 fusion.13
  363.3 6.8 %fusion.12 = bf16[8,896,1152]{2,1,0:T(8,128)(2,1)} fusion(bf16[8,896,1152]{2,1,0:T(8,128)(2,1)} %fusion.13, bf16[1024,1152,1]{1,0,2:T(8,128)(2,1)S(1)} %bitcast.333, f32[8,192,1024]{2,1,0:T(8,128)S(1)} %bitcast.336, bf16[8,192,1024]{2,1,0:T(8,128)(2,1)S(1)} %copy-done.30), kind=kOutput, calls=%fused_computation.22 | convolution fusion | flops 3636658176 | bytes 15335424 | tf_op jit(solution)/shard_map/sfn,nd->sfd/dot_general | solution.py:705
  370.9 8.7 %fusion.11 = bf16[8,896,1152]{2,1,0:T(8,128)(2,1)} fusion(bf16[8,896,1152]{2,1,0:T(8,128)(2,1)} %fusion.12, bf16[8,2,192,512]{3,2,1,0:T(8,128)(2,1)} %get-tuple-element.29, bf16[2,512,1152]{2,1,0:T(8,128)(2,1)} %get-tuple-element.31), kind=kOutput, calls=%fused_computation.20 | convolution fusion | flops 3625648128 | bytes 9043968 | tf_op jit(solution)/shard_map/sfn,nd->sfd/dot_general | solution.py:705
  379.6 2.7 bitcast_reduce_fusion.4
  383.2 181.3 %reduce_grads.1 = (bf16[2,896,1152]{2,1,0:T(8,128)(2,1)}, bf16[32,16,1152]{2,1,0:T(8,128)(2,1)}) custom-call(bf16[4,2,896,1152]{3,2,1,0:T(8,128)(2,1)} %bitcast.53.part_in, bf16[16,1152]{1,0:T(8,128)(2,1)} %pad_maximum_fusion.4.pay), custom_call_target="tpu_custom_call" | custom-call | tf_op jit(solution)/shard_map/reduce_grads/pallas_call | solution.py:604
  567.9 3.0 reshape.372
  570.9 2.3 convert_reduce_fusion
  579.2 2.7 fusion.81
  583.9 3.8 convert_element_type.197
  587.7 2.7 fusion.44
  594.1 2.2 copy.159
  598.1 2.1 copy.151
  600.2 7.4 %copy.153 = f32[1152,2,384]{2,1,0:T(2,128)} copy(f32[1152,2,384]{0,2,1:T(8,128)} %bitcast.281) | data formatting | bytes 7077888
  613.1 5.0 fusion.47
  (247 shorter events, 61.8 us)
Async XLA Ops:
  0.6 11.1 %copy-start = (bf16[144,6,1152]{2,0,1:T(8,128)(2,1)S(1)}, bf16[144,6,1152]{2,0,1:T(8,128)(2,1)}, u32[]{:S(2)}) copy-start(bf16[144,6,1152]{2,0,1:T(8,128)(2,1)} %param.24) | copy-start | bytes 5971972
  0.7 10.8 %copy-start.48 = (s32[16]{0:T(128)S(1)}, s32[16]{0:T(128)}, u32[]{:S(2)}) copy-start(s32[16]{0:T(128)} %param.20) | copy-start | bytes 196
  0.7 10.1 %copy-start.36 = (bf16[144,1152]{1,0:T(8,128)(2,1)S(1)}, bf16[144,1152]{1,0:T(8,128)(2,1)}, u32[]{:S(2)}) copy-start(bf16[144,1152]{1,0:T(8,128)(2,1)} %param.29) | copy-start | bytes 995332
  0.7 10.8 %copy-start.47 = (bf16[1000,144]{0,1:T(8,128)(2,1)S(1)}, bf16[1000,144]{0,1:T(8,128)(2,1)}, u32[]{:S(2)}) copy-start(bf16[1000,144]{0,1:T(8,128)(2,1)} %param.23) | copy-start | bytes 864004
  19.6 7.6 %copy-start.32 = (bf16[384,1152]{1,0:T(8,128)(2,1)S(1)}, bf16[384,1152]{1,0:T(8,128)(2,1)}, u32[]{:S(2)}) copy-start(bf16[384,1152]{1,0:T(8,128)(2,1)} %param.31) | copy-start | bytes 2654212
  19.6 8.4 %copy-start.44 = (f32[16]{0:T(128)S(1)}, f32[16]{0:T(128)}, u32[]{:S(2)}) copy-start(f32[16]{0:T(128)} %select_n.53) | copy-start | bytes 196
  19.6 9.1 %copy-start.43 = (f32[160]{0:T(256)S(1)}, f32[160]{0:T(256)}, u32[]{:S(2)}) copy-start(f32[160]{0:T(256)} %broadcast_in_dim.59) | copy-start | bytes 1924
  203.6 76.6 %collective-permute-start = (bf16[512,1152]{1,0:T(8,128)(2,1)}, bf16[512,1152]{1,0:T(8,128)(2,1)}, u32[]{:S(2)}, u32[]{:S(2)}) collective-permute-start(bf16[512,1152]{1,0:T(8,128)(2,1)} %slice.355), channel_id=1, source_target_pairs={{0,8},{8,0},{16,24},{24,16},{1,9},{9,1},{17,25},{25,17},{2,10},{10... | collective-permute-start | bytes 3538952 | tf_op jit(solution)/shard_map/ppermute | solution.py:709
  244.8 7.7 %copy-start.49 = (bf16[8,192,1024]{2,1,0:T(8,128)(2,1)}, bf16[8,192,1024]{2,1,0:T(8,128)(2,1)S(1)}, u32[]{:S(2)}) copy-start(bf16[8,192,1024]{2,1,0:T(8,128)(2,1)S(1)} %get-tuple-element.112) | copy-start | bytes 9437188
  244.8 7.7 %copy-start.29 = (bf16[8,192,1024]{2,1,0:T(8,128)(2,1)S(1)}, bf16[8,192,1024]{2,1,0:T(8,128)(2,1)}, u32[]{:S(2)}) copy-start(bf16[8,192,1024]{2,1,0:T(8,128)(2,1)} %copy.158) | copy-start | bytes 9437188
  252.5 10.1 %copy-start.28 = (bf16[8,2,240,512]{3,2,1,0:T(8,128)(2,1)S(1)}, bf16[8,2,240,512]{3,2,1,0:T(8,128)(2,1)}, u32[]{:S(2)}) copy-start(bf16[8,2,240,512]{3,2,1,0:T(8,128)(2,1)} %get-tuple-element.34) | copy-start | bytes 11796484
  261.6 18.6 %copy-start.9 = (f32[1024,1152]{1,0:T(8,128)}, f32[1024,1152]{1,0:T(8,128)S(1)}, u32[]{:S(2)}) copy-start(f32[1024,1152]{1,0:T(8,128)S(1)} %bitcast_add_fusion) | copy-start | bytes 14155780
  261.8 15.6 %collective-permute-start.1 = (bf16[512,1152]{1,0:T(8,128)(2,1)S(1)}, bf16[512,1152]{1,0:T(8,128)(2,1)S(1)}, u32[]{:S(2)}, u32[]{:S(2)}) collective-permute-start(bf16[512,1152]{1,0:T(8,128)(2,1)S(1)} %slice.354), channel_id=1, source_target_pairs={{0,8},{8,0},{16,24},{24,16},{1,9},{9,1},{17,25},{25,17},{2,10},{10... | collective-permute-start | bytes 3538952 | tf_op jit(solution)/shard_map/ppermute | solution.py:709
  263.1 7.7 %copy-start.4 = (bf16[512,1152]{1,0:T(8,128)(2,1)S(1)}, bf16[512,1152]{1,0:T(8,128)(2,1)}, u32[]{:S(2)}) copy-start(bf16[512,1152]{1,0:T(8,128)(2,1)} %tokens.1) | copy-start | bytes 3538948
  263.1 7.7 %copy-start.21 = (f32[512,1152]{1,0:T(8,128)S(1)}, f32[512,1152]{1,0:T(8,128)}, u32[]{:S(2)}) copy-start(f32[512,1152]{1,0:T(8,128)} %get-tuple-element.28) | copy-start | bytes 7077892
  270.8 9.4 %slice-start.2 = ((s8[4718592]{0:T(1024)(128)(4,1)}), s8[4194304]{0:T(1024)(128)(4,1)S(1)}, s32[]{:S(2)}) async-start(s8[4718592]{0:T(1024)(128)(4,1)} %bitcast.287), calls=%async_computation.2 | async-start | bytes 8388608
  273.4 6.9 %copy-start.1 = (f32[512,1152]{1,0:T(8,128)}, f32[512,1152]{1,0:T(8,128)S(1)}, u32[]{:S(2)}) copy-start(f32[512,1152]{1,0:T(8,128)S(1)} %get-tuple-element.91) | copy-start | bytes 7077892
  275.2 5.0 slice-start.3
  277.3 2.9 copy-start.17
  277.3 2.9 copy-start.19
  285.3 3.7 copy-start.6
  285.3 4.3 copy-start.39
  289.1 22.1 %collective-permute-start.2 = (bf16[512,1152]{1,0:T(8,128)(2,1)}, bf16[512,1152]{1,0:T(8,128)(2,1)}, u32[]{:S(2)}, u32[]{:S(2)}) collective-permute-start(bf16[512,1152]{1,0:T(8,128)(2,1)} %multiply_convert_fusion.1), channel_id=1, source_target_pairs={{0,8},{8,0},{16,24},{24,16},{1,9},{9,1},{17,25},{25,17},{2,10},{10... | collective-permute-start | bytes 3538952 | tf_op jit(solution)/shard_map/ppermute | solution.py:709
  298.0 3.6 copy-start.35
  301.8 3.2 copy-start.2
  301.8 3.2 copy-start.18
  305.0 2.5 copy-start.22
  319.2 2.3 copy-start.12
  327.6 2.1 copy-start.13
  327.6 2.4 copy-start.16
  330.1 4.5 copy-start.27
  342.6 10.2 %copy-start.10 = (f32[1024,1152]{1,0:T(8,128)}, f32[1024,1152]{1,0:T(8,128)S(1)}, u32[]{:S(2)}) copy-start(f32[1024,1152]{1,0:T(8,128)S(1)} %fusion.16) | copy-start | bytes 14155780
  342.6 3.4 copy-start.46
  343.7 35.9 %collective-permute-start.3 = (bf16[512,1152]{1,0:T(8,128)(2,1)}, bf16[512,1152]{1,0:T(8,128)(2,1)}, u32[]{:S(2)}, u32[]{:S(2)}) collective-permute-start(bf16[512,1152]{1,0:T(8,128)(2,1)} %slice.353), channel_id=1, source_target_pairs={{0,8},{8,0},{16,24},{24,16},{1,9},{9,1},{17,25},{25,17},{2,10},{10... | collective-permute-start | bytes 3538952 | tf_op jit(solution)/shard_map/ppermute | solution.py:709
  346.0 6.8 %copy-start.31 = (bf16[8,80,1024]{2,1,0:T(8,128)(2,1)S(1)}, bf16[8,80,1024]{2,1,0:T(8,128)(2,1)}, u32[]{:S(2)}) copy-start(bf16[8,80,1024]{2,1,0:T(8,128)(2,1)} %reshape_reshape.15) | copy-start | bytes 3932164
  352.8 4.8 copy-start.45
  352.8 4.8 copy-start.50
  352.8 10.5 %slice-start.5 = ((s8[6291456]{0:T(1024)(128)(4,1)}), s8[4194304]{0:T(1024)(128)(4,1)S(1)}, s32[]{:S(2)}) async-start(s8[6291456]{0:T(1024)(128)(4,1)} %bitcast.335), calls=%async_computation.5 | async-start | bytes 8388608
  357.6 5.7 copy-start.30
  357.6 5.7 slice-start.6
  379.6 2.7 copy-start.42
  567.8 7.4 %copy-start.40 = (f32[2,3,80]{2,1,0:T(4,128)}, f32[2,3,80]{2,1,0:T(4,128)S(1)}, u32[]{:S(2)}) copy-start(f32[2,3,80]{2,1,0:T(4,128)S(1)} %reduce_sum.197) | copy-start | bytes 5764
  570.9 4.4 copy-start.3
  581.8 5.9 slice-start
  583.9 3.8 slice-start.1
  587.7 3.6 slice-start.4
  594.1 4.0 copy-start.11
  610.7 2.4 copy-start.7
  (14 other events, 21.4 us)

commit v2 on v1

--- a/solution.py
+++ b/solution.py
@@ -25,9 +25,7 @@
 D = 1152
 
 G_STAGE, G_LONE = 128, 48
-R_STAGE, R_LONE = 64, 16
 G_STAGES = ROWS_ALL // G_STAGE
-R_STAGES = ROWS_ALL // R_STAGE
 PAY = 16
 
 
@@ -429,94 +427,129 @@
     )(own, mod_in, cond_in, tokens, out_grad, ada, keep, gains, table)
 
 
-def reduce_kernel(part_in, pay, out, pay_all, part, xin, yin, zin, fin, xs, xr, ys, yr, zs, zr, fs, fr, ps, pr, ls):
+R_STAGE, R_LONE = 64, 16
+R_STAGES = ROWS_ALL // R_STAGE
+R_PLANE = R_STAGE - R_LONE
+R_MID = R_STAGE - 2 * R_LONE
+X_RING, Y_RING, Z_RING = 8, 4, 6
+D_STAGES = C_ROWS // R_STAGE
+GU_STAGES = B_ROWS // R_STAGE
+
+
+def backward_kernel(
+    full, fi_in, si_in, fg_in, att_in, qkv_in, norm_in, stat_in, mixed_in, gu_in, hid_in,
+    tokens, out_grad, mod, keep, gains, table,
+    result_out, tokens_out, grads, pay_all,
+    part, xin, yin, zin, fin, buf_a, buf_b, acc, after, att, sent, came, came_feed, result,
+    wd, wb, wa, hid, gu, qkv, norm, stat, mixed, dqkv, gain_sum, payf, pay,
+    xs, xr, ys, yr, zs, zr, fs, fr, es, er, ps, pr, ls, lw, x_free, y_free, z_free,
+):
     x, c, z, y = place()
     t = z * 2 + y
-    me = (x * 2 + c) * 8 + t
-    targets = [lax.rem(me + k, 32) for k in range(1, 32)]
-    greet([(o // 8, o % 8) for o in targets])
-    load = pltpu.make_async_copy(part_in, part, ls.at[0])
-    load.start()
-    keep = pltpu.make_async_copy(pay, pay_all.at[me], ls.at[1])
-    keep.start()
-
-    def pay_copy(k):
-        o = lax.rem(me + k, 32)
-        return pltpu.make_async_remote_copy(
-            src_ref=pay, dst_ref=pay_all.at[me], send_sem=ps.at[k], recv_sem=pr.at[k],
-            device_id=(o // 8, o % 8), device_id_type=MESH)
-
-    @pl.loop(1, 32)
-    def _(k):
-        pay_copy(k).start()
-
+    d = x * 2 + c
     y_side, x_side, core = at(x, c, z, 1 - y), at(1 - x, c, z, y), at(x, 1 - c, z, y)
     up, down = at(x, c, z + 1, y), at(x, c, z - 1, y)
-    keep.wait()
-    load.wait()
+    spot = x * 8 + t
+    mates = []
+    for k in range(1, 16):
+        o = lax.rem(spot + k, 16)
+        mates.append(((o // 8) * 2 + c, lax.rem(o, 8)))
+    greet(mates + [core])
+
+    loads = [
+        pltpu.make_async_copy(fg_in, buf_a, ls.at[0]),
+        pltpu.make_async_copy(si_in, buf_b, ls.at[1]),
+        pltpu.make_async_copy(att_in, att, ls.at[2]),
+    ]
+    for cp in loads:
+        cp.start()
+
+    def base(g):
+        return (R_STAGES - 1 - g) * R_STAGE
 
     def lone(g, side):
-        return g * R_STAGE + side * (R_STAGE - R_LONE)
+        return rows_at(base(g) + side * (R_STAGE - R_LONE), R_LONE)
 
     def plane(g):
-        return g * R_STAGE + x * R_LONE
-
-    PL = R_STAGE - R_LONE
-    MID = R_STAGE - 2 * R_LONE
+        return rows_at(base(g) + x * R_LONE, R_PLANE)
+
+    def side_y(side):
+        return 1 - y if side == 0 else y
 
     def xcopy(g, side):
-        yy = 1 - y if side == 0 else y
+        yy = side_y(side)
         return remote(
-            part.at[:, yy, rows_at(lone(g, 1 - x), R_LONE)], xin.at[:, yy, rows_at(g * R_LONE, R_LONE)],
-            xs.at[g, side], xr.at[g, side], x_side)
+            part.at[:, yy, lone(g, 1 - x)], xin.at[lax.rem(g, X_RING), :, yy], xs.at[g, side], xr.at[g, side], x_side)
 
     def ycopy(g):
+        return remote(part.at[:, 1 - y, plane(g)], yin.at[lax.rem(g, Y_RING)], ys.at[g], yr.at[g], y_side)
+
+    def zcopy(g, to_z, way):
+        spot = to_z - (z + 1) if way == 0 else 4 - to_z
         return remote(
-            part.at[:, 1 - y, rows_at(plane(g), PL)], yin.at[:, rows_at(g * PL, PL)],
-            ys.at[g], yr.at[g], y_side)
-
-    def zcopy(g, to_z, way):
-        return remote(
-            part.at[to_z, y, rows_at(plane(g), PL)], zin.at[way, to_z, rows_at(g * PL, PL)],
+            part.at[to_z, y, plane(g)], zin.at[lax.rem(g, Z_RING), spot],
             zs.at[g, way, to_z], zr.at[g, way, to_z], up if way == 0 else down)
 
     def fcopy(g, what):
         if what == 0:
-            rows = rows_at(lone(g, x), R_LONE)
-            return remote(out.at[c, rows], out.at[c, rows], fs.at[g, 0], fr.at[g, 0], x_side)
-        rows = rows_at(g * R_STAGE + R_LONE, MID)
-        return remote(part.at[z, y, rows], fin.at[rows], fs.at[g, 1], fr.at[g, 1], x_side)
-
-    def add(zz, yy, first, rows, piece):
-        @pl.loop(0, rows // 16)
+            return remote(part.at[z, y, lone(g, x)], grads.at[c, lone(g, x)], fs.at[g, 0], fr.at[g, 0], x_side)
+        if what == 1:
+            mid = rows_at(base(g) + R_LONE, R_MID)
+            return remote(part.at[z, y, mid], fin.at[rows_at(g * R_MID, R_MID)], fs.at[g, 1], fr.at[g, 1], x_side)
+        if what == 2:
+            return remote(part.at[z, y, plane(g)], grads.at[c, plane(g)], fs.at[g, 2], fr.at[g, 2], core)
+        return remote(grads.at[c, lone(g, 1 - x)], grads.at[c, lone(g, 1 - x)], fs.at[g, 3], fr.at[g, 3], core)
+
+    def own_copy(g):
+        return pltpu.make_async_copy(part.at[z, y, plane(g)], grads.at[c, plane(g)], fs.at[g, 4])
+
+    def add(zz, yy, rows, size, piece):
+        @pl.loop(0, size // 16)
         def _(i):
-            a = rows_at(first + i * 16, 16)
-            part[zz, yy, a, :] = (
-                part[zz, yy, a, :].astype(jnp.float32) + piece(i).astype(jnp.float32)).astype(jnp.bfloat16)
-
-    def x_stage(g, side):
-        yy = 1 - y if side == 0 else y
-        xcopy(g, side).wait_recv()
+            a = rows_at(rows + i * 16, 16)
+            part[zz, yy, a, :] = low(wide(part[zz, yy, a, :]) + wide(piece(rows_at(i * 16, 16))))
+
+    def x_send(g, side):
+        if side == 0:
+            pl.when(g >= X_RING)(lambda: pl.semaphore_wait(x_free, 1))
+        xcopy(g, side).start()
+
+    def x_stage(g):
+        b = lax.rem(g, X_RING)
+        for side in (0, 1):
+            yy = side_y(side)
+            xcopy(g, side).wait_recv()
+
+            @pl.loop(0, 4)
+            def _(k):
+                add(k, yy, base(g) + x * (R_STAGE - R_LONE), R_LONE, lambda r: xin[b, k, yy, r, :])
+
+            if side == 0:
+                pl.when(g >= Y_RING)(lambda: pl.semaphore_wait(y_free, 1))
+                ycopy(g).start()
+        pl.when(g + X_RING < R_STAGES)(
+            lambda: pl.semaphore_signal(x_free, inc=1, device_id=x_side, device_id_type=MESH))
+
+    def y_stage(g):
+        b = lax.rem(g, Y_RING)
+        ycopy(g).wait_recv()
 
         @pl.loop(0, 4)
         def _(k):
-            add(k, yy, lone(g, x), R_LONE, lambda r: xin[k, yy, rows_at(g * R_LONE + r * 16, 16), :])
-
-        if side == 0:
-            ycopy(g).start()
-
-    def y_stage(g):
-        ycopy(g).wait_recv()
-
-        @pl.loop(0, 4)
-        def _(k):
-            add(k, y, plane(g), PL, lambda r: yin[k, rows_at(g * PL + r * 16, 16), :])
+            add(k, y, base(g) + x * R_LONE, R_PLANE, lambda r: yin[b, k, r, :])
+
+        pl.when(g + Y_RING < R_STAGES)(
+            lambda: pl.semaphore_signal(y_free, inc=1, device_id=y_side, device_id_type=MESH))
 
     def take(g, way, to_z):
-        zcopy(g, to_z, way).wait_recv()
-        add(to_z, y, plane(g), PL, lambda r: zin[way, to_z, rows_at(g * PL + r * 16, 16), :])
+        b = lax.rem(g, Z_RING)
+        spot = to_z - z if way == 0 else 4 - to_z
+        remote(
+            part.at[to_z, y, plane(g)], zin.at[b, spot], zs.at[g, way, to_z], zr.at[g, way, to_z], y_side).wait_recv()
+        add(to_z, y, base(g) + x * R_LONE, R_PLANE, lambda r: zin[b, spot, r, :])
 
     def up_stage(g):
+        pl.when(jnp.logical_and(g >= Z_RING, z < 3))(lambda: pl.semaphore_wait(z_free.at[0], 1))
         for j in (3, 2, 1):
             @pl.when(z + j <= 3)
             def _():
@@ -524,6 +557,7 @@
                 zcopy(g, z + j, 0).start()
 
     def down_stage(g):
+        pl.when(jnp.logical_and(g >= Z_RING, z > 0))(lambda: pl.semaphore_wait(z_free.at[1], 1))
         for j in (3, 2, 1):
             @pl.when(z >= j)
             def _():
@@ -533,45 +567,306 @@
     def own_stage(g):
         pl.when(z > 0)(lambda: take(g, 0, z))
         pl.when(z < 3)(lambda: take(g, 1, z))
-        rows = lone(g, x)
-        out[c, rows_at(rows, R_LONE), :] = part[z, y, rows_at(rows, R_LONE), :]
+
+        @pl.when(g + Z_RING < R_STAGES)
+        def _():
+            pl.when(z > 0)(
+                lambda: pl.semaphore_signal(z_free.at[0], inc=1, device_id=down, device_id_type=MESH))
+            pl.when(z < 3)(
+                lambda: pl.semaphore_signal(z_free.at[1], inc=1, device_id=up, device_id_type=MESH))
+
         fcopy(g, 0).start()
         fcopy(g, 1).start()
 
     def f_stage(g):
+        fcopy(g, 1).wait()
+        mid = base(g) + R_LONE
+
+        @pl.loop(0, R_MID // 16)
+        def _(i):
+            a = rows_at(mid + i * 16, 16)
+            part[z, y, a, :] = low(wide(part[z, y, a, :]) + wide(fin[rows_at(g * R_MID + i * 16, 16), :]))
+
+        own_copy(g).start()
+        fcopy(g, 2).start()
         fcopy(g, 0).wait_recv()
-        fcopy(g, 1).wait_recv()
-        first = g * R_STAGE + R_LONE
-
-        @pl.loop(0, MID // 16)
-        def _(i):
-            a = rows_at(first + i * 16, 16)
-            out[c, a, :] = (part[z, y, a, :].astype(jnp.float32) + fin[a, :].astype(jnp.float32)).astype(jnp.bfloat16)
-
-        rows = rows_at(g * R_STAGE, R_STAGE)
-        remote(out.at[c, rows], out.at[c, rows], fs.at[g, 2], fr.at[g, 2], core).start()
-
-    def x_send(g):
-        xcopy(g, 0).start()
-        xcopy(g, 1).start()
-
-    x_send(0)
-    x_send(1)
+        fcopy(g, 3).start()
 
     def service(i):
         def on(g, act):
             pl.when(jnp.logical_and(g >= 0, g < R_STAGES))(lambda: act(g))
 
-        on(i, lambda g: x_stage(g, 0))
-        on(i, lambda g: x_stage(g, 1))
-        on(i + 2, x_send)
+        on(i, x_stage)
         on(i - 1, y_stage)
         on(i - 1 - z, up_stage)
         on(i - 4 + z, down_stage)
         on(i - 4, own_stage)
         on(i - 5, f_stage)
 
-    @pl.loop(0, R_STAGES + 5)
+    def send_stages(first, last, side):
+        @pl.loop(first, last)
+        def _(g):
+            x_send(g, side)
+
+    def shard(k):
+        return lax.rem(k, 4), jnp.where(k < 4, 1 - y, y)
+
+    def slot(k):
+        zz, yy = shard(k)
+        return zz * 2 + yy
+
+    def stream(pairs):
+        def fetch(k):
+            b = lax.rem(k, 2)
+            return [pltpu.make_async_copy(src(slot(k)), buf.at[b], lw.at[n, b]) for src, buf, n in pairs]
+
+        def begin(k):
+            for cp in fetch(k):
+                cp.start()
+
+        def turn_to(k):
+            for cp in fetch(k):
+                cp.wait()
+            pl.when(k < 7)(lambda: begin(k + 1))
+
+        return begin, turn_to
+
+    def mod_row(image, k):
+        return mod[pl.ds(image * 8 + k, 1), :]
+
+    def by_rows(act):
+        for image in range(2):
+            @pl.loop(0, PATCH // CHUNK)
+            def _(i):
+                act(image, rows_at(image * PATCH + i * CHUNK, CHUNK))
+
+    def count(image, k, v):
+        payf[pl.ds(image * 8 + k, 1), :] += jnp.sum(v, axis=0, keepdims=True)
+
+    def clear(ref):
+        @pl.loop(0, ref.shape[0] // 16)
+        def _(i):
+            ref[rows_at(i * 16, 16), :] = jnp.zeros((16, D), jnp.float32)
+
+    def gather_sum(h, left, right):
+        for image in range(2):
+            cut = slice(image * PATCH, (image + 1) * PATCH)
+            rows = slice(h * 512 + image * PATCH, h * 512 + (image + 1) * PATCH)
+            acc[rows, :] += tn(left[:, cut], right)
+
+    def share_half(number, landing):
+        @pl.loop(0, 512 // CHUNK)
+        def _(i):
+            sent[rows_at(i * CHUNK, CHUNK), :] = low(acc[rows_at(512 + i * CHUNK, CHUNK), :])
+
+        cp = remote(sent, landing, es.at[number], er.at[number], core)
+        cp.start()
+        return cp
+
+    payf[...] = jnp.zeros_like(payf)
+    gain_sum[...] = jnp.zeros_like(gain_sum)
+    clear(acc)
+    begin_d, turn_d = stream([(lambda s: hid_in.at[s], hid, 0)])
+    begin_g, turn_g = stream([
+        (lambda s: full.at[s, pl.ds(A_ROWS + B_ROWS, C_ROWS)], wd, 1),
+        (lambda s: full.at[s, pl.ds(A_ROWS, B_ROWS)], wb, 2),
+        (lambda s: gu_in.at[s], gu, 3),
+    ])
+    begin_a, turn_a = stream([
+        (lambda s: full.at[s, pl.ds(0, A_ROWS)], wa, 4),
+        (lambda s: qkv_in.at[s], qkv, 5),
+        (lambda s: norm_in.at[s], norm, 6),
+        (lambda s: stat_in.at[s], stat, 7),
+        (lambda s: mixed_in.at[:, rows_at(s * HEAD, HEAD)], mixed, 8),
+    ])
+    begin_f, turn_f = stream([
+        (lambda s: hid_in.at[s], hid, 0),
+        (lambda s: full.at[s, pl.ds(A_ROWS + B_ROWS, C_ROWS)], wd, 1),
+    ])
+    begin_d(0)
+    begin_g(0)
+    loads[0].wait()
+
+    @pl.loop(0, 8)
+    def _(k):
+        b = lax.rem(k, 2)
+        zz, yy = shard(k)
+        turn_d(k)
+        grad = nn(hid[b, 0], buf_a[0]) + nn(hid[b, 1], buf_a[1])
+        part[zz, yy, A_ROWS + B_ROWS :, :] = low(grad)
+        pl.when(k == 3)(lambda: send_stages(0, D_STAGES, 0))
+
+    send_stages(0, D_STAGES, 1)
+    loads[1].wait()
+
+    @pl.loop(0, 8)
+    def _(k):
+        b = lax.rem(k, 2)
+        zz, yy = shard(k)
+        turn_g(k)
+        grads_here = []
+        for h in range(2):
+            hg = nt(wd[b], buf_a[h])
+            g, u = wide(gu[b, h, :SHARD_FF]), wide(gu[b, h, SHARD_FF:])
+            sig = 1.0 / (1.0 + jnp.exp(-g))
+            act = g * sig
+            both = low(jnp.concatenate([hg * u * (sig + act * (1.0 - sig)), hg * act], axis=0))
+            grads_here.append(both)
+            gather_sum(h, both, wb[b])
+        part[zz, yy, A_ROWS : A_ROWS + B_ROWS, :] = low(
+            nn(grads_here[0], buf_b[0]) + nn(grads_here[1], buf_b[1]))
+
+        @pl.when(k == 3)
+        def _():
+            service(0)
+            send_stages(D_STAGES, 6, 0)
+
+    send_stages(D_STAGES, 6, 1)
+    share_second = share_half(0, came)
+    service(1)
+    begin_a(0)
+    load_fi = pltpu.make_async_copy(fi_in, buf_a, ls.at[0])
+    load_fi.start()
+    send_stages(6, 8, 0)
+    send_stages(6, 8, 1)
+    loads[2].wait()
+    share_second.wait_recv()
+
+    def after_rows(image, rows):
+        a = att[rows, :]
+        v = wide(tokens[rows, :]) + mod_row(image, 2) * a
+        inv = lax.rsqrt(jnp.mean(v * v, axis=-1, keepdims=True) + epsilon)
+        n = v * inv
+        sg = acc[rows, :] + wide(came[rows, :])
+        dn = sg * (1.0 + mod_row(image, 4))
+        ag = wide(out_grad[rows, :]) + inv * (dn - n * jnp.mean(dn * n, axis=-1, keepdims=True))
+        after[rows, :] = ag
+        buf_b[0, rows, :] = low(ag * mod_row(image, 2))
+        count(image, 2, ag * a)
+        count(image, 3, sg)
+        count(image, 4, sg * n)
+
+    by_rows(after_rows)
+    share_ag = remote(buf_b.at[0], buf_b.at[1], es.at[1], er.at[1], core)
+    share_ag.start()
+    service(2)
+    clear(acc)
+    load_fi.wait()
+    share_ag.wait_recv()
+
+    @pl.loop(0, 8)
+    def _(k):
+        b = lax.rem(k, 2)
+        zz, yy = shard(k)
+        turn_a(k)
+        cos, sin = table[:HALF, :PATCH], table[HALF:, :PATCH]
+        part[zz, yy, 3 * HEAD : A_ROWS, :] = low(nn(mixed[b, 0], buf_b[0]) + nn(mixed[b, 1], buf_b[1]))
+        for h in range(2):
+            mg_all = low(nt(wa[b, 3 * HEAD :], buf_b[h]))
+            for image in range(2):
+                cut = slice(image * PATCH, (image + 1) * PATCH)
+                q, kk, v = [qkv[b, h, i * HEAD : (i + 1) * HEAD, cut] for i in range(3)]
+                mg = mg_all[:, cut]
+                p = jnp.exp(tn(kk, q) * FACTOR - stat[b, h, 2:3, cut])
+                dqkv[h, 2 * HEAD :, cut] = low(nt(mg, low(p)))
+                pg = tn(v, mg)
+                sg = low(p * (pg - jnp.sum(p * pg, axis=0, keepdims=True)))
+                backs = (nn(kk, sg), nt(q, sg))
+                for i in range(2):
+                    rows = slice(i * HEAD, (i + 1) * HEAD)
+                    back = turn(backs[i] * FACTOR, cos, -sin)
+                    n = wide(norm[b, h, rows, cut])
+                    gain_sum[rows, :] += back * n
+                    dn = back * gains[rows, :1]
+                    mean = jnp.sum(dn * n, axis=0, keepdims=True) * (1.0 / HD)
+                    dqkv[h, rows, cut] = low(stat[b, h, i : i + 1, cut] * (dn - n * mean))
+            gather_sum(h, dqkv[h], wa[b, : 3 * HEAD])
+        part[zz, yy, : 3 * HEAD, :] = low(nn(dqkv[0], buf_a[0]) + nn(dqkv[1], buf_a[1]))
+        ones = jnp.ones((8, 512), jnp.bfloat16)
+        sums = nt(ones, dqkv[0]) + nt(ones, dqkv[1])
+        s = slot(k)
+        payf[pl.ds(6 + s // 4, 1), pl.ds(pl.multiple_of(lax.rem(s, 4) * 256, 128), 3 * HEAD)] = sums[:1]
+
+        @pl.when(lax.rem(k, 3) == 2)
+        def _():
+            service(3 + k // 3)
+
+        pl.when(k == 3)(lambda: send_stages(8, 9, 0))
+
+    send_stages(8, 9, 1)
+    share_second.wait_send()
+    begin_f(0)
+    share_first = share_half(2, came)
+    service(5)
+    send_stages(9, 12, 0)
+    send_stages(9, 12, 1)
+    share_first.wait_recv()
+
+    def first_rows(image, rows):
+        v = wide(tokens[rows, :])
+        inv = lax.rsqrt(jnp.mean(v * v, axis=-1, keepdims=True) + epsilon)
+        n = v * inv
+        fgd = acc[rows, :] + wide(came[rows, :])
+        dn = fgd * (1.0 + mod_row(image, 1))
+        count(image, 0, fgd)
+        count(image, 1, fgd * n)
+        acc[rows, :] = after[rows, :] + inv * (dn - n * jnp.mean(dn * n, axis=-1, keepdims=True))
+
+    by_rows(first_rows)
+    save_tokens = pltpu.make_async_copy(acc.at[pl.ds(0, 512)], tokens_out, ls.at[3])
+    save_tokens.start()
+    service(6)
+    save_tokens.wait()
+    clear(acc)
+
+    @pl.loop(0, 8)
+    def _(k):
+        b = lax.rem(k, 2)
+        turn_f(k)
+        for h in range(2):
+            gather_sum(h, hid[b, h], wd[b])
+
+    share_first.wait_send()
+    share_feed = share_half(3, came_feed)
+    service(7)
+    send_stages(12, 14, 0)
+    send_stages(12, 14, 1)
+    share_feed.wait_recv()
+
+    def result_rows(image, rows):
+        feed = acc[rows, :] + wide(came_feed[rows, :])
+        v = wide(tokens[rows, :]) + mod_row(image, 2) * att[rows, :]
+        result[rows, :] = low(v + mod_row(image, 5) * feed)
+        count(image, 5, wide(out_grad[rows, :]) * feed)
+
+    by_rows(result_rows)
+    save_result = pltpu.make_async_copy(result, result_out, ls.at[4])
+    save_result.start()
+    lanes = gain_sum[:, :128] + gain_sum[:, 128:]
+    lanes = jnp.concatenate([lanes, jnp.zeros((96, 128), jnp.float32)], axis=0)
+    payf[14:15, :256] = jnp.sum(jnp.transpose(lanes), axis=0, keepdims=True)
+    pay[...] = low(payf[...] * keep[...])
+    me = d * 8 + t
+    keep_pay = pltpu.make_async_copy(pay, pay_all.at[me], ls.at[5])
+    keep_pay.start()
+    pays = [remote(pay, pay_all.at[me], ps.at[k], pr.at[k], o) for k, o in enumerate(mates)]
+    for cp in pays:
+        cp.start()
+
+    @pl.loop(8, 14)
+    def _(i):
+        service(i)
+
+    keep_pay.wait()
+    for cp in pays:
+        cp.wait()
+    swaps = []
+    for xx in range(2):
+        rows = pl.ds(pl.multiple_of((xx * 2 + c) * 8, 8), 8)
+        swaps.append(remote(pay_all.at[rows], pay_all.at[rows], ps.at[15 + xx], pr.at[15 + xx], core))
+        swaps[-1].start()
+
+    @pl.loop(14, R_STAGES + 5)
     def _(i):
         service(i)
 
@@ -580,49 +875,53 @@
         xcopy(g, 0).wait_send()
         xcopy(g, 1).wait_send()
         ycopy(g).wait_send()
-
         for j in (3, 2, 1):
             pl.when(z + j <= 3)(lambda: zcopy(g, z + j, 0).wait_send())
             pl.when(z >= j)(lambda: zcopy(g, z - j, 1).wait_send())
         fcopy(g, 0).wait_send()
-        fcopy(g, 1).wait_send()
-        rows = rows_at(g * R_STAGE, R_STAGE)
-        mine = remote(out.at[c, rows], out.at[c, rows], fs.at[g, 2], fr.at[g, 2], core)
-        mine.wait_send()
-        remote(out.at[c, rows], out.at[1 - c, rows], fs.at[g, 2], fr.at[g, 2], core).wait_recv()
-
-    @pl.loop(1, 32)
-    def _(k):
-        pay_copy(k).wait()
-
-
-def reduce_grads(part, pay):
+        own_copy(g).wait()
+        fcopy(g, 2).wait()
+        fcopy(g, 3).wait()
+
+    for cp in swaps:
+        cp.wait()
+    share_ag.wait_send()
+    share_feed.wait_send()
+    save_result.wait()
+
+
+def backward(saved, tokens, out_grad, mod, keep, gains, table):
+    dma = pltpu.SemaphoreType.DMA
+    regular = pltpu.SemaphoreType.REGULAR
     vm = pltpu.VMEM
-    dma = pltpu.SemaphoreType.DMA
-    PL = R_STAGE - R_LONE
+    bf, f32 = jnp.bfloat16, jnp.float32
     anywhere = pl.BlockSpec(memory_space=pl.ANY)
+    inside = pl.BlockSpec(memory_space=pltpu.VMEM)
+    R = tokens.shape[0]
+    outs = [((R, D), bf), ((R, D), f32), ((2, ROWS_ALL, D), bf), ((32, PAY, D), bf)]
     return pl.pallas_call(
-        reduce_kernel,
-        out_shape=(
-            jax.ShapeDtypeStruct((2, ROWS_ALL, D), jnp.bfloat16),
-            jax.ShapeDtypeStruct((32, PAY, D), jnp.bfloat16),
-        ),
-        in_specs=[anywhere, anywhere],
-        out_specs=(pl.BlockSpec(memory_space=pltpu.VMEM), anywhere),
+        backward_kernel,
+        out_shape=tuple(jax.ShapeDtypeStruct(s, e) for s, e in outs),
+        in_specs=[anywhere] * len(saved) + [inside] * 6,
+        out_specs=(anywhere,) * len(outs),
         scratch_shapes=[
-            vm((4, 2, ROWS_ALL, D), jnp.bfloat16),
-            vm((4, 2, R_STAGES * R_LONE, D), jnp.bfloat16),
-            vm((4, R_STAGES * PL, D), jnp.bfloat16),
-            vm((2, 4, R_STAGES * PL, D), jnp.bfloat16),
-            vm((ROWS_ALL, D), jnp.bfloat16),
+            vm((4, 2, ROWS_ALL, D), bf), vm((X_RING, 4, 2, R_LONE, D), bf), vm((Y_RING, 4, R_PLANE, D), bf),
+            vm((Z_RING, 5, R_PLANE, D), bf), vm((R_STAGES * R_MID, D), bf),
+            vm((2, R, D), bf), vm((2, R, D), bf), vm((2 * R, D), f32), vm((R, D), f32), vm((R, D), f32),
+            vm((R, D), bf), vm((R, D), bf), vm((R, D), bf), vm((R, D), bf),
+            vm((2, C_ROWS, D), bf), vm((2, B_ROWS, D), bf), vm((2, A_ROWS, D), bf),
+            vm((2, 2, SHARD_FF, R), bf), vm((2, 2, B_ROWS, R), bf), vm((2, 2, 3 * HEAD, R), bf),
+            vm((2, 2, 2 * HEAD, R), bf), vm((2, 2, 8, R), f32), vm((2, 2, HEAD, R), bf),
+            vm((2, 3 * HEAD, R), bf), vm((2 * HEAD, PATCH), f32), vm((16, D), f32), vm((16, D), bf),
             dma((R_STAGES, 2)), dma((R_STAGES, 2)), dma((R_STAGES,)), dma((R_STAGES,)),
-            dma((R_STAGES, 2, 4)), dma((R_STAGES, 2, 4)), dma((R_STAGES, 3)), dma((R_STAGES, 3)),
-            dma((32,)), dma((32,)), dma((2,)),
+            dma((R_STAGES, 2, 4)), dma((R_STAGES, 2, 4)), dma((R_STAGES, 5)), dma((R_STAGES, 4)),
+            dma((4,)), dma((4,)), dma((17,)), dma((17,)), dma((6,)), dma((9, 2)),
+            regular, regular, regular((2,)),
         ],
         compiler_params=pltpu.CompilerParams(
-            collective_id=1, has_side_effects=True, vmem_limit_bytes=60 * 2**20),
-        name="reduce_grads",
-    )(part.reshape(4, 2, ROWS_ALL, D), pay)
+            collective_id=1, has_side_effects=True, vmem_limit_bytes=62 * 2**20),
+        name="backward",
+    )(*saved, tokens, out_grad, mod, keep, gains, table)
 
 
 def normalize(vectors, axis=-1, count=None):
@@ -706,12 +1005,7 @@
     t = lax.axis_index("tensor")
     c = lax.axis_index("dp") % 2
     own = pack_weights(qkv_weight, out_weight, gate_up_weight, down_weight, c)
-    sib = lambda v: lax.ppermute(v, "dp", [(0, 1), (1, 0), (2, 3), (3, 2)])
-    both = lambda v: jnp.concatenate([v, sib(v)])
-    half = tokens.shape[0]
     images = labels.shape[0]
-    meet = lambda v: v[:half] + sib(low(v[half:])).astype(jnp.float32)
-
     columns_here = class_table.shape[1]
     column = t * columns_here + jnp.arange(columns_here)
     half_width = D // 2
@@ -747,79 +1041,13 @@
     chosen = low(labels_all[:, None] == classes[None, :])
     cond_act = low(jax.nn.silu(condition))
     first_image = lax.axis_index("dp") * images
-    mod = mod.reshape(mod_images, 8, D)
-    mod_rows = jnp.repeat(mod, PATCH, axis=0)
-    shift_one, scale_one, gate_one, shift_two, scale_two, gate_two = [mod_rows[:, i] for i in range(6)]
-    gains = pair_rows(qk_scale.astype(jnp.float32)[..., None])
-    cos, sin = np.tile(cos, (1, 4)), np.tile(sin, (1, 4))
-    flat = lambda v: v.swapaxes(-3, -2).reshape(v.shape[:-3] + (v.shape[-2], 1024))
-    qkv_t, norm_t, stat_t, gu_t, hidden = [flat(v) for v in (qkv_t, norm_t, stat_t, gu_t, hidden)]
-    mixed = flat(mixed).reshape(8, HEAD, 1024)
-    first_in, second_in, feed_grad = [v.reshape(1024, D) for v in (first_in, second_in, feed_grad)]
-    q_t, k_t, v_t = [qkv_t[:, i * HEAD : (i + 1) * HEAD] for i in range(3)]
-    q_norm, k_norm = [norm_t[:, i * HEAD : (i + 1) * HEAD].astype(jnp.float32) for i in range(2)]
-    q_inv, k_inv, logsum = [stat_t[:, i : i + 1] for i in range(3)]
-    g, u = [gu_t[:, i * SHARD_FF : (i + 1) * SHARD_FF].astype(jnp.float32) for i in range(2)]
-    act = jax.nn.silu(g)
-    factor = FACTOR
-    cut = lambda v: v.reshape(8, HEAD, 4, PATCH)
-    scores = dot("heiq,heik->hikq", cut(q_t), cut(k_t)) * factor
-    prob = jnp.exp(scores - logsum.reshape(8, 4, 1, PATCH))
-    prob_low = low(prob)
-    wo = weights[:, 3 * HEAD : 4 * HEAD]
-    wg = weights[:, A_ROWS : A_ROWS + SHARD_FF]
-    wu = weights[:, A_ROWS + SHARD_FF : A_ROWS + B_ROWS]
-    wd = weights[:, A_ROWS + B_ROWS :]
-    tokens_f = tokens.astype(jnp.float32)
-    first_norm, first_inverse = normalize(tokens_f)
-    after_attn = tokens_f + gate_one * attention
-    second_norm, second_inverse = normalize(after_attn)
-    feed = meet(dot("sfn,sfd->nd", hidden, wd))
-    result = low(after_attn + gate_two * feed)
-
-    grad_out = out_grad.astype(jnp.float32)
-    hidden_grad = dot("sfd,nd->sfn", wd, feed_grad)
-    g_grad = low(hidden_grad * u * silu_slope(g))
-    u_grad = low(hidden_grad * act)
-    d_part = low(dot("sfn,nd->sfd", hidden, feed_grad))
-    g_part = low(dot("sfn,nd->sfd", g_grad, second_in))
-    u_part = low(dot("sfn,nd->sfd", u_grad, second_in))
-    second_grad = meet(dot("sfn,sfd->nd", g_grad, wg) + dot("sfn,sfd->nd", u_grad, wu))
-    after_grad = grad_out + normalize_back(second_grad * (1.0 + scale_two), second_norm, second_inverse)
-    attn_grad = both(low(after_grad * gate_one))
-    mixed_grad = low(dot("hed,nd->hen", wo, attn_grad))
-    o_part = low(dot("hen,nd->hed", mixed, attn_grad))
-    v_grad = low(dot("hikq,heiq->heik", prob_low, cut(mixed_grad))).reshape(8, HEAD, 1024)
-    prob_grad = dot("heik,heiq->hikq", cut(v_t), cut(mixed_grad))
-    score_grad = low(prob * (prob_grad - jnp.sum(prob * prob_grad, axis=2, keepdims=True)))
-    q_back = dot("hikq,heik->heiq", score_grad, cut(k_t)).reshape(8, HEAD, 1024) * factor
-    k_back = dot("hikq,heiq->heik", score_grad, cut(q_t)).reshape(8, HEAD, 1024) * factor
-    q_back = rotate_pairs(q_back, cos, -sin)
-    k_back = rotate_pairs(k_back, cos, -sin)
-    scale_part = jnp.stack([jnp.sum(q_back * q_norm, axis=(0, 2)), jnp.sum(k_back * k_norm, axis=(0, 2))])
-    q_grad = low(normalize_back(q_back * gains[0], q_norm, q_inv, 1, HD))
-    k_grad = low(normalize_back(k_back * gains[1], k_norm, k_inv, 1, HD))
-    qkv_grad = jnp.concatenate([q_grad, k_grad, v_grad], axis=1)
-    bias_part = jnp.sum(qkv_grad.astype(jnp.float32), axis=2)
-    qkv_part = low(dot("hen,nd->hed", qkv_grad, first_in))
-    first_grad = meet(dot("hen,hed->nd", qkv_grad, weights[:, : 3 * HEAD]))
-    tokens_grad = after_grad + normalize_back(first_grad * (1.0 + scale_one), first_norm, first_inverse)
-
-    per_image = lambda v: jnp.sum(v.reshape(mod_images, PATCH, D), axis=1)
-    mod_grad = low(jnp.stack([
-        per_image(first_grad), per_image(first_grad * first_norm), per_image(after_grad * attention) * kept[:, None],
-        per_image(second_grad), per_image(second_grad * second_norm), per_image(grad_out * feed) * kept[:, None],
-    ], axis=1))
-    tail = jnp.concatenate([low(bias_part).reshape(-1), low(scale_part).reshape(-1)])
-    tail = jnp.pad(tail, (0, (PAY - 6 * mod_images) * D - tail.size)).reshape(-1, D)
-    pay = jnp.concatenate([mod_grad.reshape(6 * mod_images, D), tail], axis=0)
-    summed, pay_all = reduce_grads(jnp.concatenate([qkv_part, o_part, g_part, u_part, d_part], axis=1), pay)
+    saved = (weights, first_in, second_in, feed_grad, attention, qkv_t, norm_t, stat_t, mixed, gu_t, hidden)
+    result, tokens_grad, summed, pay_all = backward(saved, tokens, out_grad, mod, keep, gain_rows, table)
     qkv_weight_grad, out_weight_grad, gate_up_grad, down_grad = unpack_grads(summed)
-
-    mod_grad = pay_all[:, : 6 * mod_images].reshape(-1, 6, D)
-    tail = pay_all[:, 6 * mod_images :].reshape(32, -1).astype(jnp.float32)
-    bias_all = tail[:, : bias_part.size].reshape(32, 8, 3 * HEAD)
-    scale_all = tail[:, bias_part.size : bias_part.size + scale_part.size].reshape(32, 2, HEAD)
+    pay_all = pay_all.reshape(32, mod_images, 8, D)
+    mod_grad = pay_all[:, :, :6].reshape(-1, 6, D)
+    bias_all = pay_all[:, 0, 6:, : 4 * 256].astype(jnp.float32).reshape(32, 8, 256)[..., : 3 * HEAD]
+    scale_all = pay_all[:, 1, 6, : 2 * HEAD].astype(jnp.float32).reshape(32, 2, HEAD)
     qk_scale_grad = unpair_rows(jnp.sum(scale_all, axis=0)[..., None])[..., 0]
     bias_all = lax.dynamic_index_in_dim(bias_all, t, 1, keepdims=False).reshape(2, 2, 8, 3, HEAD)
     bias_sum = jnp.sum(bias_all, axis=(0, 2))

time: 627 us -> 435 us (0.69); the launches traced: 618 us -> 433 us
  matrix products: 97 us -> 7.59 us
  local copies, waits for them, and re-layouts: 120 us -> 44.8 us
  other arithmetic: 53.9 us -> 9.72 us
  Pallas kernels: 344 us -> 370 us
    dot_general x20 -> x4, matrix products: 95.7 us -> 6.3 us  [fast(): jnp.einsum(s, a, b, preferred_element_type=jnp.float32)]
    pallas_call x1, Pallas kernels: 181 us -> 207 us  [backward(): pl.pallas_call(backward_kernel, out_shape=tuple((jax.ShapeDtypeStruct(s,...]
    reduce_sum x9 -> x0, other arithmetic: 18.1 us -> none  [the longest x4 7.7 us: fast(): per_image = lambda v: jnp.sum(v.reshape(mod_images, PATCH, D), axis=1)]
    unnamed x130 -> x35, local copies, waits for them, and re-layouts: 38.6 us -> 20.6 us
    slice x8 -> x0, local copies, waits for them, and re-layouts: 12.9 us -> none  [the longest x1 6.61 us: fast(): gu_t[:, i * SHARD_FF:(i + 1) * SHARD_FF].astype(jnp.float32)]
    transpose x2 -> x0, local copies, waits for them, and re-layouts: 12.4 us -> none  [fast(): v.swapaxes(-3, -2).reshape(v.shape[:-3] + (v.shape[-2], 1024))]
    convert_element_type x4 -> x0, other arithmetic: 11.7 us -> none  [the longest x3 10.5 us: low(): return v.astype(jnp.bfloat16)]
    reshape x9 -> x0, local copies, waits for them, and re-layouts: 11.7 us -> none  [the longest x3 6.38 us: fast(): v.swapaxes(-3, -2).reshape(v.shape[:-3] + (v.shape[-2], 1024))]
  transfers between devices with their start and end apart: 4 -> 0, of which waited for: 0 -> 0; matrix products, arithmetic and copies ran while one was open for 21% -> 0% of each run, Pallas kernels for 0% -> 0%
where the time goes in v2:
time: 435 us; the launch traced here: 433 us
  Pallas kernels  370 us (85%)
  local copies, waits for them, and re-layouts  44.8 us (10%)
  other arithmetic  9.72 us (2%)
  matrix products  7.59 us (2%)
    pallas_call x1, Pallas kernels, backward(): pl.pallas_call(backward_kernel, out_shape=tuple((jax.ShapeDtypeStruct(s,...  207 us
    pallas_call x1, Pallas kernels, forward(): pl.pallas_call(forward_kernel, out_shape=tuple((jax.ShapeDtypeStruct(s, e...  162 us
    unnamed x35, local copies, waits for them, and re-layouts  20.6 us

profile of v2, /device:TPU:0, one launch (start us, length us, event | category | flops | bytes accessed | tf_op | source)
XLA Modules:
  0.0 433.4 jit_solution(4517225274763827731)
XLA Ops:
  1.5 0.7 convert_element_type.72
  2.1 0.7 broadcast_select_fusion
  2.9 0.7 convert_bitcast_fusion
  3.8 0.8 reshape.159
  4.6 0.7 reshape_broadcast_in_dim.10
  6.0 1.2 convolution_add_fusion
  7.2 0.7 maximum_maximum_fusion.1.cond_in
  7.9 0.7 pad_convert_fusion
  8.6 0.6 broadcast_bitcast_fusion.ada
  9.3 0.7 broadcast_in_dim.81.keep
  10.0 0.7 broadcast_in_dim.84.gains
  10.7 1.6 constant_dynamic-slice_fusion.1
  12.8 0.8 copy.74
  13.6 0.7 slice_bitcast_fusion.1
  14.9 0.8 pad.39.clone
  15.7 1.9 dynamic-slice_bitcast_fusion
  17.6 2.9 copy.72
  20.4 1.1 constant_dynamic-update-slice_fusion.1
  21.5 0.9 pad_dynamic-update-slice_fusion.1
  22.5 0.9 pad_dynamic-update-slice_fusion
  23.4 1.3 constant_dynamic-update-slice_fusion
  24.8 1.3 copy-done.5
  26.1 162.3 %forward.1 = (bf16[8,896,1152]{2,1,0:T(8,128)(2,1)}, f32[4,16,256]{2,1,0:T(8,128)}, f32[16,1152]{1,0:T(8,128)}, bf16[2,512,1152]{2,1,0:T(8,128)(2,1)}, bf16[2,51...) custom-call(bf16[896,1152]{1,0:T(8,128)(2,1)} %copy-done.5, ...), custom_call_target="tpu_custom_call" | custom-call | tf_op jit(solution)/shard_map/forward/pallas_call | solution.py:410
  188.4 207.3 %backward.1 = (bf16[512,1152]{1,0:T(8,128)(2,1)}, f32[512,1152]{1,0:T(8,128)}, bf16[2,896,1152]{2,1,0:T(8,128)(2,1)}, bf16[32,16,1152]{2,1,0:T(8,128)(2,1)}) custom-call(bf16[8,896,1152]{2,1,0:T(8,128)(2,1)} %get-tuple-element.29.full, bf16[2,512,1152]{2,1,0:T(8,128)(2,1)} %get-tuple-element.30.fi_in, bf16[2,512,1152]{2,1,0:T(8,128)(2,1)} %get-tuple-element.31.si_in, ...), custom_call_target="tpu_custom_call" | custom-call | tf_op jit(solution)/shard_map/backward/pallas_call | solution.py:902
  395.7 0.9 fusion.8
  396.6 1.0 fusion.6
  397.8 0.6 squeeze_reshape.7
  398.4 2.2 convert_reduce_fusion
  400.7 2.1 fusion
  402.7 0.6 constant_dynamic-slice_fusion
  404.1 0.7 reshape.174
  404.8 1.3 fusion.4
  406.1 1.9 slice.101
  407.9 1.2 slice.91
  409.1 0.7 copy.89
  409.8 0.7 copy.79
  410.5 0.8 copy-done.2
  411.3 1.3 slice.103
  412.9 2.0 copy.85
  414.9 7.4 %copy.87 = f32[1152,2,384]{2,1,0:T(2,128)} copy(f32[1152,2,384]{0,2,1:T(8,128)} %bitcast.98) | data formatting | bytes 7077888
  422.3 2.7 fusion.1
  425.0 0.7 copy-done.3
  426.3 0.7 copy.80
  427.0 1.2 pad_maximum_fusion
  428.2 1.4 copy.86
  430.0 1.0 copy.107
  431.0 1.1 copy-done.6
  432.0 1.4 copy.108
  (70 shorter events, 4.2 us)
Async XLA Ops:
  0.6 11.6 %copy-start = (bf16[144,6,1152]{2,0,1:T(8,128)(2,1)S(1)}, bf16[144,6,1152]{2,0,1:T(8,128)(2,1)}, u32[]{:S(2)}) copy-start(bf16[144,6,1152]{2,0,1:T(8,128)(2,1)} %param.21) | copy-start | bytes 5971972
  7.2 6.4 %copy-start.9 = (bf16[1152,3,144]{0,2,1:T(8,128)(2,1)S(1)}, bf16[1152,3,144]{0,2,1:T(8,128)(2,1)}, u32[]{:S(2)}) copy-start(bf16[1152,3,144]{0,2,1:T(8,128)(2,1)} %param.23) | copy-start | bytes 2985988
  13.6 2.1 copy-start.8
  20.4 4.3 copy-start.10
  24.8 1.3 copy-start.5
  398.4 4.9 %copy-start.4 = (bf16[32,16,1152]{2,1,0:T(8,128)(2,1)S(1)}, bf16[32,16,1152]{2,1,0:T(8,128)(2,1)}, u32[]{:S(2)}) copy-start(bf16[32,16,1152]{2,1,0:T(8,128)(2,1)} %get-tuple-element.43) | copy-start | bytes 3538948
  409.1 2.2 copy-start.2
  414.9 7.4 %copy-start.11 = (f32[4,16,256]{2,1,0:T(8,128)S(1)}, f32[4,16,256]{2,1,0:T(8,128)}, u32[]{:S(2)}) copy-start(f32[4,16,256]{2,1,0:T(8,128)} %get-tuple-element.44) | copy-start | bytes 196612
  422.3 3.4 copy-start.3
  428.2 1.8 copy-start.7
  429.9 2.1 copy-start.6
  429.9 3.5 copy-start.1

commit v3 on v2

--- a/solution.py
+++ b/solution.py
@@ -14,19 +14,32 @@
 HIGH = lax.Precision.HIGHEST
 MESH = pl.DeviceIdType.MESH
 epsilon = 1e-06
-
-HEAD = 80
-HALF = 40
+D = 1152
+
+QKV = 3 * HD
+A_ROWS = 4 * HD
 SHARD_FF = 192
-A_ROWS = 4 * HEAD
 B_ROWS = 2 * SHARD_FF
 C_ROWS = SHARD_FF
 ROWS_ALL = A_ROWS + B_ROWS + C_ROWS
-D = 1152
-
-G_STAGE, G_LONE = 128, 48
+HEAD = 80
+O_FIRST = A_ROWS - HEAD
+QKV_ROWS = 224
+CHUNK = 64
+FACTOR = HD ** (-0.5)
+PAY = 16
+
+G_STAGE, G_LONE = 96, 32
 G_STAGES = ROWS_ALL // G_STAGE
-PAY = 16
+A_STAGES = A_ROWS // G_STAGE
+AB_STAGES = (A_ROWS + B_ROWS) // G_STAGE
+
+R_STAGE = 48
+R_STAGES = ROWS_ALL // R_STAGE
+D_STAGES = C_ROWS // R_STAGE
+GU_STAGES = (C_ROWS + B_ROWS) // R_STAGE
+X_RING, Y_RING, Z_RING = 8, 6, 8
+AHEAD = 2
 
 
 def place():
@@ -71,8 +84,19 @@
 
 
 def turn(v, cos, sin):
-    a, b = v[:HALF], v[HALF:]
-    return jnp.concatenate([a * cos - b * sin, b * cos + a * sin], axis=0)
+    other = jnp.concatenate([v[18:36], v[:18], v[54:72], v[36:54]], axis=0)
+    return v * cos + other * sin
+
+
+def fill(v):
+    return jnp.concatenate([v, jnp.zeros((HEAD - HD, v.shape[1]), v.dtype)], axis=0)
+
+
+def columns(rows):
+    k, n = rows.shape
+    rows = jnp.concatenate([rows, jnp.zeros((k, 128 - n), jnp.float32)], axis=1)
+    rows = jnp.concatenate([rows, jnp.zeros((128 - k, 128), jnp.float32)], axis=0)
+    return jnp.transpose(rows)
 
 
 def remote(src, dst, ss, rs, to):
@@ -80,14 +104,12 @@
         src_ref=src, dst_ref=dst, send_sem=ss, recv_sem=rs, device_id=to, device_id_type=MESH)
 
 
-CHUNK = 64
-FACTOR = HD ** (-0.5)
-
-
 def forward_kernel(
-    own, mod_in, cond_in, tokens, out_grad, ada, keep, gains, table,
+    counts, qkv_w, out_w, gu_w, down_w, condition, labels, ada_w, ada_b, bias_w, tokens, out_grad, gains, table,
     full, cond_out, mod_out, fi_out, si_out, fg_out, att_out, qkv_out, norm_out, stat_out, mixed_out, gu_out, hid_out,
-    mod_all, mod, fi, si, fg, att, att_send, att_recv, wa, ow, mixed, qkv, norm, stat, wb, gu, hid,
+    dd_out,
+    own, mod_in, mod_send, cond_in, mod_all, mod, fi, si, fg, att, att_send, att_recv, wa, ow, mixed, qkv, norm, stat, wb, gu,
+    hid, dd,
     send, recv, ms, mr, cs, cr, es, er, ls, qs, hs, ws, save,
 ):
     x, c, z, y = place()
@@ -95,23 +117,21 @@
     d = x * 2 + c
     peers = [lax.rem(t + k, 8) for k in range(1, 8)]
     groups = [lax.rem(d + k, 4) for k in range(1, 4)]
+    load_gu = pltpu.make_async_copy(gu_w, own.at[pl.ds(A_ROWS, B_ROWS)], ls.at[4])
+    load_gu.start()
+    load_down = pltpu.make_async_copy(
+        down_w.at[rows_at(c * C_ROWS, C_ROWS)], own.at[pl.ds(A_ROWS + B_ROWS, C_ROWS)], ls.at[5])
+    load_down.start()
+    for head in range(2):
+        @pl.when(c == head)
+        def _():
+            cut = slice(head * HD, (head + 1) * HD)
+            own[:A_ROWS, :] = low(jnp.concatenate(
+                [wide(qkv_w[0, cut]), wide(qkv_w[1, cut]), wide(qkv_w[2, cut]), wide(out_w[cut])], axis=0))
+
     greet([(d, p) for p in peers] + [(g, t) for g in groups])
     y_side, x_side, core = at(x, c, z, 1 - y), at(1 - x, c, z, y), at(x, 1 - c, z, y)
     up, down = at(x, c, z + 1, y), at(x, c, z - 1, y)
-    small = []
-    for k, p in enumerate(peers):
-        small.append(remote(mod_in.at[p], mod_all.at[t], ms.at[k], mr.at[t], (d, p)))
-    for k, g in enumerate(groups):
-        small.append(remote(cond_in, cond_out.at[d], cs.at[k], cr.at[d], (g, t)))
-    for cp in small:
-        cp.start()
-    kept = [
-        pltpu.make_async_copy(own, full.at[t], ls.at[0]),
-        pltpu.make_async_copy(mod_in.at[t], mod_all.at[t], ls.at[1]),
-        pltpu.make_async_copy(cond_in, cond_out.at[d], ls.at[2]),
-    ]
-    for cp in kept:
-        cp.start()
 
     def plane(g):
         return rows_at(g * G_STAGE + x * G_LONE, G_STAGE - G_LONE)
@@ -187,13 +207,50 @@
 
     service(0)
 
+    cond_in[...] = jnp.zeros_like(cond_in)
+    cond_in[:, :144] = condition[...]
+    cond_in[:, 144:145] = wide(labels[...])
+    mod_in[...] = jnp.zeros_like(mod_in)
+    v = condition[...]
+    act = low(v * (1.0 / (1.0 + jnp.exp(-v))))
+    for k in range(6):
+        share = nn(act, ada_w[k])
+        for image in range(16):
+            mod_in[image // 2, image % 2 * 8 + k : image % 2 * 8 + k + 1, :] = share[image : image + 1]
+    for p in range(8):
+        for k, row in enumerate((6, 7, 14)):
+            mod_in[p, row : row + 1, :144] = wide(bias_w[k : k + 1, :])
+    mod_send[...] = low(mod_in[...])
+    small = []
     for k, p in enumerate(peers):
-        remote(mod_in.at[p], mod_all.at[p], ms.at[0], mr.at[p], (d, p)).wait_recv()
-    kept[1].wait()
-    total = ada[...]
-    for s in range(8):
-        total = total + wide(mod_all[s])
-    mod[...] = total * keep[...]
+        small.append(remote(mod_send.at[p], mod_all.at[t], ms.at[k], mr.at[t], (d, p)))
+    for k, g in enumerate(groups):
+        small.append(remote(cond_in, cond_out.at[d], cs.at[k], cr.at[d], (g, t)))
+    for cp in small:
+        cp.start()
+    kept = [
+        pltpu.make_async_copy(mod_send.at[t], mod_all.at[t], ls.at[1]),
+        pltpu.make_async_copy(cond_in, cond_out.at[d], ls.at[2]),
+    ]
+    for cp in kept:
+        cp.start()
+    load_gu.wait()
+    load_down.wait()
+    kept.append(pltpu.make_async_copy(own, full.at[t], ls.at[0]))
+    kept[2].start()
+    service(1)
+
+    for p in peers:
+        remote(mod_send.at[p], mod_all.at[p], ms.at[0], mr.at[p], (d, p)).wait_recv()
+    kept[0].wait()
+    for image in range(2):
+        total = jnp.concatenate([wide(ada_b[...]), jnp.zeros((2, D), jnp.float32)], axis=0)
+        for s in range(8):
+            total = total + wide(mod_all[s])[image * 8 : image * 8 + 8]
+        real = jnp.where(t * 2 + image < counts[0], 1.0, 0.0)
+        row = lax.broadcasted_iota(jnp.int32, (8, D), 0)
+        gate = jnp.logical_or(row == 2, row == 5)
+        mod[image * 8 : image * 8 + 8, :] = jnp.where(gate, total * real, total)
 
     def first_rows(image, rows):
         v = wide(tokens[rows, :])
@@ -203,7 +260,6 @@
     by_rows(first_rows)
     share_fi = remote(fi.at[0], fi.at[1], es.at[0], er.at[0], core)
     share_fi.start()
-    service(1)
 
     def feed_rows(image, rows):
         fg[0, rows, :] = low(wide(out_grad[rows, :]) * mod_row(image, 5))
@@ -212,12 +268,12 @@
     share_fg = remote(fg.at[0], fg.at[1], es.at[1], er.at[1], core)
     share_fg.start()
 
-    @pl.loop(2, 7)
+    @pl.loop(2, A_STAGES + 4)
     def _(i):
         service(i)
 
-    kept[0].wait()
-    lone_in(0, 3)
+    kept[2].wait()
+    lone_in(0, A_STAGES)
     share_fi.wait_recv()
     share_fg.wait_recv()
     saves = [
@@ -229,11 +285,12 @@
         cp.start()
 
     def load_a(s):
-        return pltpu.make_async_copy(full.at[s, pl.ds(0, 3 * HEAD)], wa.at[lax.rem(s, 2)], ws.at[lax.rem(s, 2)])
-
-    load_o = pltpu.make_async_copy(full.at[:, pl.ds(3 * HEAD, HEAD)], ow, ls.at[3])
+        return pltpu.make_async_copy(full.at[s, pl.ds(0, QKV_ROWS)], wa.at[lax.rem(s, 2)], ws.at[lax.rem(s, 2)])
+
+    load_o = pltpu.make_async_copy(full.at[:, pl.ds(O_FIRST, HEAD)], ow, ls.at[3])
     load_o.start()
     load_a(0).start()
+    gain_cols = columns(wide(gains[...]))
 
     def save_head(s):
         b = lax.rem(s, 2)
@@ -254,38 +311,35 @@
             for cp in save_head(s - 2):
                 cp.wait()
 
-        bias_row = wide(mod_all[s, 6:7, :512])
-        bias_row = jnp.where(c == 0, bias_row[:, :256], bias_row[:, 256:])
-        bias = jnp.transpose(jnp.broadcast_to(bias_row, (128, 256)))[: 3 * HEAD, :1]
-        cos, sin = table[:HALF, :], table[HALF:, :]
+        bias_rows = wide(mod_all[s, :, :256])
+        bias_rows = jnp.concatenate([bias_rows[6:8, :144], bias_rows[14:15, :144]], axis=0)
+        bias = columns(jnp.where(c == 0, bias_rows[:, :HD], bias_rows[:, HD:]))
+        cos, sin = table[:HD, :], table[HD:, :]
         for h in range(2):
-            raw = nt(wa[b], fi[h]) + bias
-            turned = []
+            raw = nt(wa[b], fi[h])
             for i in range(2):
-                v = raw[i * HEAD : (i + 1) * HEAD]
+                v = raw[i * HD : (i + 1) * HD] + bias[:HD, i : i + 1]
                 inv = lax.rsqrt(jnp.sum(v * v, axis=0, keepdims=True) * (1.0 / HD) + epsilon)
                 n = v * inv
-                norm[b, h, i * HEAD : (i + 1) * HEAD, :] = low(n)
+                norm[b, h, i * HEAD : (i + 1) * HEAD, :] = low(fill(n))
                 stat[b, h, i : i + 1, :] = inv
-                turned.append(low(turn(n * gains[i * HEAD : (i + 1) * HEAD, :1], cos, sin)))
-            q, k = turned
-            v = low(raw[2 * HEAD :])
-            qkv[b, h, :HEAD, :] = q
-            qkv[b, h, HEAD : 2 * HEAD, :] = k
+                qkv[b, h, i * HEAD : (i + 1) * HEAD, :] = low(fill(turn(n * gain_cols[:HD, i : i + 1], cos, sin)))
+            v = low(fill(raw[2 * HD : 3 * HD] + bias[:HD, 2:3]))
             qkv[b, h, 2 * HEAD :, :] = v
             for image in range(2):
                 cut = slice(image * PATCH, (image + 1) * PATCH)
-                e = jnp.exp(tn(k[:, cut], q[:, cut]) * FACTOR)
+                e = jnp.exp(tn(qkv[b, h, HEAD : 2 * HEAD, cut], qkv[b, h, :HEAD, cut]) * FACTOR)
                 row_sum = jnp.sum(e, axis=0, keepdims=True)
                 stat[b, h, 2:3, cut] = jnp.log(row_sum)
                 p = low(e * (1.0 / row_sum))
-                mixed[h, pl.ds(pl.multiple_of(s * HEAD, 16), HEAD), cut] = low(nn(v[:, cut], p))
+                m = nn(v[:, cut], p)
+                m = jnp.concatenate([m[HD:], m[:HD]], axis=0)
+                mixed[h, pl.ds(pl.multiple_of(s * HEAD, 16), HEAD), cut] = low(m)
         for cp in save_head(s):
             cp.start()
 
-        @pl.when(lax.rem(s, 4) == 3)
-        def _():
-            service(7 + s // 4)
+        pl.when(s == 3)(lambda: service(A_STAGES + 4))
+        pl.when(s == 7)(lambda: service(A_STAGES + 5))
 
     for s in (6, 7):
         for cp in save_head(s):
@@ -314,8 +368,12 @@
     by_rows(second_rows)
     share_si = remote(si.at[0], si.at[1], es.at[3], er.at[3], core)
     share_si.start()
-    service(9)
-    lone_in(3, 6)
+
+    @pl.loop(A_STAGES + 6, AB_STAGES + 4)
+    def _(i):
+        service(i)
+
+    lone_in(A_STAGES, AB_STAGES)
     share_si.wait_recv()
     saves += [
         pltpu.make_async_copy(att, att_out, save.at[4]),
@@ -332,6 +390,7 @@
         return [
             pltpu.make_async_copy(gu.at[b], gu_out.at[s], hs.at[b, 0]),
             pltpu.make_async_copy(hid.at[b], hid_out.at[s], hs.at[b, 1]),
+            pltpu.make_async_copy(dd.at[b], dd_out.at[s], hs.at[b, 2]),
         ]
 
     load_b(0).start()
@@ -352,12 +411,14 @@
             g, u = both[:SHARD_FF], both[SHARD_FF:]
             gu[b, h] = low(both)
             hid[b, h] = low(g * (1.0 / (1.0 + jnp.exp(-g))) * u)
+        dd[b] = low(nn(hid[b, 0], fg[0]) + nn(hid[b, 1], fg[1]))
         for cp in save_shard(s):
             cp.start()
 
-        pl.when(s == 3)(lambda: service(10))
-
-    lone_in(6, 7)
+        pl.when(s == 3)(lambda: service(AB_STAGES + 4))
+
+    service(AB_STAGES + 5)
+    lone_in(AB_STAGES, G_STAGES)
     for s in (6, 7):
         for cp in save_shard(s):
             cp.wait()
@@ -389,59 +450,52 @@
         cp.wait_send()
     for g in groups:
         remote(cond_in, cond_out.at[g], cs.at[0], cr.at[g], (g, t)).wait_recv()
-    kept[2].wait()
+    kept[1].wait()
     for cp in saves:
         cp.wait()
 
 
-def forward(own, mod_in, cond_in, tokens, out_grad, ada, keep, gains, table):
+def forward(counts, qkv_w, out_w, gu_w, down_w, condition, labels, ada_w, ada_b, bias_w, tokens, out_grad, gains, table):
     dma = pltpu.SemaphoreType.DMA
     vm = pltpu.VMEM
     bf, f32 = jnp.bfloat16, jnp.float32
     anywhere = pl.BlockSpec(memory_space=pl.ANY)
     inside = pl.BlockSpec(memory_space=pltpu.VMEM)
+    scalar = pl.BlockSpec(memory_space=pltpu.SMEM)
     R = tokens.shape[0]
     outs = [
-        ((8, ROWS_ALL, D), bf), ((4,) + cond_in.shape, f32), ((16, D), f32),
+        ((8, ROWS_ALL, D), bf), ((4, 16, 256), f32), ((16, D), f32),
         ((2, R, D), bf), ((2, R, D), bf), ((2, R, D), bf), ((R, D), f32),
         ((8, 2, 3 * HEAD, R), bf), ((8, 2, 2 * HEAD, R), bf), ((8, 2, 8, R), f32), ((2, 8 * HEAD, R), bf),
-        ((8, 2, B_ROWS, R), bf), ((8, 2, SHARD_FF, R), bf),
+        ((8, 2, B_ROWS, R), bf), ((8, 2, SHARD_FF, R), bf), ((8, C_ROWS, D), bf),
     ]
     return pl.pallas_call(
         forward_kernel,
         out_shape=tuple(jax.ShapeDtypeStruct(s, e) for s, e in outs),
-        in_specs=[anywhere] * 3 + [inside] * 6,
+        in_specs=[scalar, inside, inside, anywhere, anywhere] + [inside] * 9,
         out_specs=(anywhere,) * len(outs),
         scratch_shapes=[
-            vm((8, 16, D), bf), vm((16, D), f32),
+            vm((ROWS_ALL, D), bf), vm((8, 16, D), f32), vm((8, 16, D), bf), vm((16, 256), f32), vm((8, 16, D), bf),
+            vm((16, D), f32),
             vm((2, R, D), bf), vm((2, R, D), bf), vm((2, R, D), bf), vm((R, D), f32), vm((R, D), bf), vm((R, D), bf),
-            vm((2, 3 * HEAD, D), bf), vm((8, HEAD, D), bf), vm((2, 8 * HEAD, R), bf),
+            vm((2, QKV_ROWS, D), bf), vm((8, HEAD, D), bf), vm((2, 8 * HEAD, R), bf),
             vm((2, 2, 3 * HEAD, R), bf), vm((2, 2, 2 * HEAD, R), bf), vm((2, 2, 8, R), f32),
-            vm((2, B_ROWS, D), bf), vm((2, 2, B_ROWS, R), bf), vm((2, 2, SHARD_FF, R), bf),
+            vm((2, B_ROWS, D), bf), vm((2, 2, B_ROWS, R), bf), vm((2, 2, SHARD_FF, R), bf), vm((2, C_ROWS, D), bf),
             dma((G_STAGES, 25)), dma((G_STAGES, 8, 2)), dma((7,)), dma((8,)), dma((3,)), dma((4,)),
-            dma((4,)), dma((4,)), dma((4,)), dma((2, 3)), dma((2, 2)), dma((4,)), dma((6,)),
+            dma((4,)), dma((4,)), dma((6,)), dma((2, 3)), dma((2, 3)), dma((4,)), dma((6,)),
         ],
         compiler_params=pltpu.CompilerParams(
             collective_id=0, has_side_effects=True, vmem_limit_bytes=60 * 2**20),
         name="forward",
-    )(own, mod_in, cond_in, tokens, out_grad, ada, keep, gains, table)
-
-
-R_STAGE, R_LONE = 64, 16
-R_STAGES = ROWS_ALL // R_STAGE
-R_PLANE = R_STAGE - R_LONE
-R_MID = R_STAGE - 2 * R_LONE
-X_RING, Y_RING, Z_RING = 8, 4, 6
-D_STAGES = C_ROWS // R_STAGE
-GU_STAGES = B_ROWS // R_STAGE
+    )(counts, qkv_w, out_w, gu_w, down_w, condition, labels, ada_w, ada_b, bias_w, tokens, out_grad, gains, table)
 
 
 def backward_kernel(
-    full, fi_in, si_in, fg_in, att_in, qkv_in, norm_in, stat_in, mixed_in, gu_in, hid_in,
-    tokens, out_grad, mod, keep, gains, table,
+    full, fi_in, si_in, fg_in, att_in, qkv_in, norm_in, stat_in, mixed_in, gu_in, hid_in, dd_in,
+    counts, tokens, out_grad, mod, gains, table,
     result_out, tokens_out, grads, pay_all,
     part, xin, yin, zin, fin, buf_a, buf_b, acc, after, att, sent, came, came_feed, result,
-    wd, wb, wa, hid, gu, qkv, norm, stat, mixed, dqkv, gain_sum, payf, pay,
+    wd, wb, wa, hid, gu, qkv, norm, stat, mixed, dqkv, dlow, gain_sum, payf, pay,
     xs, xr, ys, yr, zs, zr, fs, fr, es, er, ps, pr, ls, lw, x_free, y_free, z_free,
 ):
     x, c, z, y = place()
@@ -461,112 +515,120 @@
         pltpu.make_async_copy(si_in, buf_b, ls.at[1]),
         pltpu.make_async_copy(att_in, att, ls.at[2]),
     ]
+    load_dd = pltpu.make_async_copy(
+        dd_in, part.at[:, :, pl.ds(A_ROWS + B_ROWS, C_ROWS)], ls.at[6])
+    load_dd.start()
     for cp in loads:
         cp.start()
 
-    def base(g):
-        return (R_STAGES - 1 - g) * R_STAGE
-
-    def lone(g, side):
-        return rows_at(base(g) + side * (R_STAGE - R_LONE), R_LONE)
-
-    def plane(g):
-        return rows_at(base(g) + x * R_LONE, R_PLANE)
+    def rows_of(g):
+        return rows_at((R_STAGES - 1 - g) * R_STAGE, R_STAGE)
 
     def side_y(side):
         return 1 - y if side == 0 else y
+
+    def lone_z(g, yy):
+        return jnp.where(yy == lax.rem(x + g, 2), 1, 2)
 
     def xcopy(g, side):
         yy = side_y(side)
         return remote(
-            part.at[:, yy, lone(g, 1 - x)], xin.at[lax.rem(g, X_RING), :, yy], xs.at[g, side], xr.at[g, side], x_side)
-
-    def ycopy(g):
-        return remote(part.at[:, 1 - y, plane(g)], yin.at[lax.rem(g, Y_RING)], ys.at[g], yr.at[g], y_side)
-
-    def zcopy(g, to_z, way):
-        spot = to_z - (z + 1) if way == 0 else 4 - to_z
+            part.at[3 - lone_z(g, yy), yy, rows_of(g)], xin.at[lax.rem(g, X_RING), side],
+            xs.at[g, side], xr.at[g, side], x_side)
+
+    def ycopy(g, k):
+        yy = 1 - y
+        zz = (0, 3, lone_z(g, yy))[k]
+        return remote(part.at[zz, yy, rows_of(g)], yin.at[lax.rem(g, Y_RING), k], ys.at[g, k], yr.at[g, k], y_side)
+
+    def zcopy(g, way, k):
+        zz = (3 - 3 * way) if k == 0 else lone_z(g, y)
         return remote(
-            part.at[to_z, y, plane(g)], zin.at[lax.rem(g, Z_RING), spot],
-            zs.at[g, way, to_z], zr.at[g, way, to_z], up if way == 0 else down)
-
-    def fcopy(g, what):
-        if what == 0:
-            return remote(part.at[z, y, lone(g, x)], grads.at[c, lone(g, x)], fs.at[g, 0], fr.at[g, 0], x_side)
-        if what == 1:
-            mid = rows_at(base(g) + R_LONE, R_MID)
-            return remote(part.at[z, y, mid], fin.at[rows_at(g * R_MID, R_MID)], fs.at[g, 1], fr.at[g, 1], x_side)
-        if what == 2:
-            return remote(part.at[z, y, plane(g)], grads.at[c, plane(g)], fs.at[g, 2], fr.at[g, 2], core)
-        return remote(grads.at[c, lone(g, 1 - x)], grads.at[c, lone(g, 1 - x)], fs.at[g, 3], fr.at[g, 3], core)
+            part.at[zz, y, rows_of(g)], zin.at[lax.rem(g, Z_RING), way * 2 + k],
+            zs.at[g, way * 2 + k], zr.at[g, way * 2 + k], up if way == 0 else down)
+
+    def plane_sum(g):
+        return remote(part.at[z, y, rows_of(g)], fin.at[rows_of(g)], fs.at[g, 0], fr.at[g, 0], x_side)
+
+    def finished(g):
+        return remote(part.at[z, y, rows_of(g)], grads.at[c, rows_of(g)], fs.at[g, 0], fr.at[g, 0], x_side)
+
+    def core_copy(g, here):
+        src = part.at[z, y, rows_of(g)] if here else grads.at[c, rows_of(g)]
+        return remote(src, grads.at[c, rows_of(g)], fs.at[g, 1], fr.at[g, 1], core)
 
     def own_copy(g):
-        return pltpu.make_async_copy(part.at[z, y, plane(g)], grads.at[c, plane(g)], fs.at[g, 4])
-
-    def add(zz, yy, rows, size, piece):
-        @pl.loop(0, size // 16)
+        return pltpu.make_async_copy(part.at[z, y, rows_of(g)], grads.at[c, rows_of(g)], fs.at[g, 2])
+
+    def add(zz, yy, g, piece):
+        first = (R_STAGES - 1 - g) * R_STAGE
+
+        @pl.loop(0, R_STAGE // 16)
         def _(i):
-            a = rows_at(rows + i * 16, 16)
+            a = rows_at(first + i * 16, 16)
             part[zz, yy, a, :] = low(wide(part[zz, yy, a, :]) + wide(piece(rows_at(i * 16, 16))))
 
-    def x_send(g, side):
+    def send(g, side):
         if side == 0:
             pl.when(g >= X_RING)(lambda: pl.semaphore_wait(x_free, 1))
+            pl.when(g >= Y_RING)(lambda: pl.semaphore_wait(y_free, 1))
         xcopy(g, side).start()
+        if side == 0:
+            ycopy(g, 0).start()
+            ycopy(g, 1).start()
 
     def x_stage(g):
         b = lax.rem(g, X_RING)
         for side in (0, 1):
             yy = side_y(side)
             xcopy(g, side).wait_recv()
-
-            @pl.loop(0, 4)
-            def _(k):
-                add(k, yy, base(g) + x * (R_STAGE - R_LONE), R_LONE, lambda r: xin[b, k, yy, r, :])
-
+            add(lone_z(g, yy), yy, g, lambda r: xin[b, side, r, :])
             if side == 0:
-                pl.when(g >= Y_RING)(lambda: pl.semaphore_wait(y_free, 1))
-                ycopy(g).start()
+                ycopy(g, 2).start()
         pl.when(g + X_RING < R_STAGES)(
             lambda: pl.semaphore_signal(x_free, inc=1, device_id=x_side, device_id_type=MESH))
 
     def y_stage(g):
         b = lax.rem(g, Y_RING)
-        ycopy(g).wait_recv()
-
-        @pl.loop(0, 4)
-        def _(k):
-            add(k, y, base(g) + x * R_LONE, R_PLANE, lambda r: yin[b, k, r, :])
-
+        for k in range(3):
+            ycopy(g, k).wait_recv()
+            add((0, 3, lone_z(g, y))[k], y, g, lambda r: yin[b, k, r, :])
         pl.when(g + Y_RING < R_STAGES)(
             lambda: pl.semaphore_signal(y_free, inc=1, device_id=y_side, device_id_type=MESH))
 
-    def take(g, way, to_z):
-        b = lax.rem(g, Z_RING)
-        spot = to_z - z if way == 0 else 4 - to_z
-        remote(
-            part.at[to_z, y, plane(g)], zin.at[b, spot], zs.at[g, way, to_z], zr.at[g, way, to_z], y_side).wait_recv()
-        add(to_z, y, base(g) + x * R_LONE, R_PLANE, lambda r: zin[b, spot, r, :])
-
-    def up_stage(g):
-        pl.when(jnp.logical_and(g >= Z_RING, z < 3))(lambda: pl.semaphore_wait(z_free.at[0], 1))
-        for j in (3, 2, 1):
-            @pl.when(z + j <= 3)
-            def _():
-                pl.when(z > 0)(lambda: take(g, 0, z + j))
-                zcopy(g, z + j, 0).start()
-
-    def down_stage(g):
-        pl.when(jnp.logical_and(g >= Z_RING, z > 0))(lambda: pl.semaphore_wait(z_free.at[1], 1))
-        for j in (3, 2, 1):
-            @pl.when(z >= j)
-            def _():
-                pl.when(z < 3)(lambda: take(g, 1, z - j))
-                zcopy(g, z - j, 1).start()
+    def take(g, way, k):
+        zcopy(g, way, k).wait_recv()
+        zz = (3 - 3 * way) if k == 0 else lone_z(g, y)
+        add(zz, y, g, lambda r: zin[lax.rem(g, Z_RING), way * 2 + k, r, :])
+
+    def z_stage(g, way):
+        further = z < 3 if way == 0 else z > 0
+        first = z == 0 if way == 0 else z == 3
+
+        @pl.when(further)
+        def _():
+            pl.when(g >= Z_RING)(lambda: pl.semaphore_wait(z_free.at[way], 1))
+            pl.when(jnp.logical_not(first))(lambda: take(g, way, 0))
+            zcopy(g, way, 0).start()
+
+        lone = lone_z(g, y)
+
+        @pl.when(z < lone if way == 0 else z > lone)
+        def _():
+            pl.when(jnp.logical_not(first))(lambda: take(g, way, 1))
+            zcopy(g, way, 1).start()
 
     def own_stage(g):
-        pl.when(z > 0)(lambda: take(g, 0, z))
-        pl.when(z < 3)(lambda: take(g, 1, z))
+        pl.when(z == 3)(lambda: take(g, 0, 0))
+        pl.when(z == 0)(lambda: take(g, 1, 0))
+
+        @pl.when(z == lone_z(g, y))
+        def _():
+            take(g, 0, 1)
+            take(g, 1, 1)
+            finished(g).start()
+
+        pl.when(jnp.logical_or(z == 0, z == 3))(lambda: plane_sum(g).start())
 
         @pl.when(g + Z_RING < R_STAGES)
         def _():
@@ -575,38 +637,46 @@
             pl.when(z < 3)(
                 lambda: pl.semaphore_signal(z_free.at[1], inc=1, device_id=up, device_id_type=MESH))
 
-        fcopy(g, 0).start()
-        fcopy(g, 1).start()
-
     def f_stage(g):
-        fcopy(g, 1).wait()
-        mid = base(g) + R_LONE
-
-        @pl.loop(0, R_MID // 16)
-        def _(i):
-            a = rows_at(mid + i * 16, 16)
-            part[z, y, a, :] = low(wide(part[z, y, a, :]) + wide(fin[rows_at(g * R_MID + i * 16, 16), :]))
-
-        own_copy(g).start()
-        fcopy(g, 2).start()
-        fcopy(g, 0).wait_recv()
-        fcopy(g, 3).start()
-
-    def service(i):
+        ends = jnp.logical_or(z == 0, z == 3)
+        here = z == lone_z(g, y)
+
+        @pl.when(ends)
+        def _():
+            plane_sum(g).wait()
+            add(z, y, g, lambda r: fin[rows_at((R_STAGES - 1 - g) * R_STAGE + r.start, 16), :])
+
+        @pl.when(jnp.logical_or(ends, here))
+        def _():
+            own_copy(g).start()
+            core_copy(g, True).start()
+
+        @pl.when(z == 3 - lone_z(g, y))
+        def _():
+            finished(g).wait_recv()
+            core_copy(g, False).start()
+
+    def service(i, ready):
         def on(g, act):
             pl.when(jnp.logical_and(g >= 0, g < R_STAGES))(lambda: act(g))
 
         on(i, x_stage)
         on(i - 1, y_stage)
-        on(i - 1 - z, up_stage)
-        on(i - 4 + z, down_stage)
+        on(i - 1 - z, lambda g: z_stage(g, 0))
+        on(i - 4 + z, lambda g: z_stage(g, 1))
         on(i - 4, own_stage)
         on(i - 5, f_stage)
 
-    def send_stages(first, last, side):
+        @pl.when(i + AHEAD < ready)
+        def _():
+            send(i + AHEAD, 0)
+            send(i + AHEAD, 1)
+
+    def send_stages(first, last):
         @pl.loop(first, last)
         def _(g):
-            x_send(g, side)
+            send(g, 0)
+            send(g, 1)
 
     def shard(k):
         return lax.rem(k, 4), jnp.where(k < 4, 1 - y, y)
@@ -666,7 +736,6 @@
     payf[...] = jnp.zeros_like(payf)
     gain_sum[...] = jnp.zeros_like(gain_sum)
     clear(acc)
-    begin_d, turn_d = stream([(lambda s: hid_in.at[s], hid, 0)])
     begin_g, turn_g = stream([
         (lambda s: full.at[s, pl.ds(A_ROWS + B_ROWS, C_ROWS)], wd, 1),
         (lambda s: full.at[s, pl.ds(A_ROWS, B_ROWS)], wb, 2),
@@ -683,20 +752,10 @@
         (lambda s: hid_in.at[s], hid, 0),
         (lambda s: full.at[s, pl.ds(A_ROWS + B_ROWS, C_ROWS)], wd, 1),
     ])
-    begin_d(0)
     begin_g(0)
+    load_dd.wait()
+    send_stages(0, AHEAD)
     loads[0].wait()
-
-    @pl.loop(0, 8)
-    def _(k):
-        b = lax.rem(k, 2)
-        zz, yy = shard(k)
-        turn_d(k)
-        grad = nn(hid[b, 0], buf_a[0]) + nn(hid[b, 1], buf_a[1])
-        part[zz, yy, A_ROWS + B_ROWS :, :] = low(grad)
-        pl.when(k == 3)(lambda: send_stages(0, D_STAGES, 0))
-
-    send_stages(0, D_STAGES, 1)
     loads[1].wait()
 
     @pl.loop(0, 8)
@@ -716,19 +775,14 @@
         part[zz, yy, A_ROWS : A_ROWS + B_ROWS, :] = low(
             nn(grads_here[0], buf_b[0]) + nn(grads_here[1], buf_b[1]))
 
-        @pl.when(k == 3)
-        def _():
-            service(0)
-            send_stages(D_STAGES, 6, 0)
-
-    send_stages(D_STAGES, 6, 1)
+        pl.when(lax.rem(k, 2) == 1)(lambda: service(k // 2, D_STAGES))
+
+    send_stages(D_STAGES, D_STAGES + AHEAD)
     share_second = share_half(0, came)
-    service(1)
+    service(D_STAGES, GU_STAGES)
     begin_a(0)
     load_fi = pltpu.make_async_copy(fi_in, buf_a, ls.at[0])
     load_fi.start()
-    send_stages(6, 8, 0)
-    send_stages(6, 8, 1)
     loads[2].wait()
     share_second.wait_recv()
 
@@ -749,57 +803,57 @@
     by_rows(after_rows)
     share_ag = remote(buf_b.at[0], buf_b.at[1], es.at[1], er.at[1], core)
     share_ag.start()
-    service(2)
+    service(D_STAGES + 1, GU_STAGES)
     clear(acc)
     load_fi.wait()
     share_ag.wait_recv()
+
+    gain_cols = columns(wide(gains[...]))
 
     @pl.loop(0, 8)
     def _(k):
         b = lax.rem(k, 2)
         zz, yy = shard(k)
         turn_a(k)
-        cos, sin = table[:HALF, :PATCH], table[HALF:, :PATCH]
-        part[zz, yy, 3 * HEAD : A_ROWS, :] = low(nn(mixed[b, 0], buf_b[0]) + nn(mixed[b, 1], buf_b[1]))
+        cos, sin = table[:HD, :PATCH], table[HD:, :PATCH]
+        out_part = nn(mixed[b, 0], buf_b[0]) + nn(mixed[b, 1], buf_b[1])
         for h in range(2):
-            mg_all = low(nt(wa[b, 3 * HEAD :], buf_b[h]))
+            mg_all = nt(wa[b, O_FIRST:], buf_b[h])
+            mg_all = low(fill(mg_all[HEAD - HD :]))
+            dqkv[h, 3 * HD :, :] = jnp.zeros((QKV_ROWS - 3 * HD, 512), jnp.float32)
             for image in range(2):
                 cut = slice(image * PATCH, (image + 1) * PATCH)
                 q, kk, v = [qkv[b, h, i * HEAD : (i + 1) * HEAD, cut] for i in range(3)]
                 mg = mg_all[:, cut]
                 p = jnp.exp(tn(kk, q) * FACTOR - stat[b, h, 2:3, cut])
-                dqkv[h, 2 * HEAD :, cut] = low(nt(mg, low(p)))
+                dqkv[h, 2 * HD : 3 * HD, cut] = nt(mg, low(p))[:HD]
                 pg = tn(v, mg)
                 sg = low(p * (pg - jnp.sum(p * pg, axis=0, keepdims=True)))
                 backs = (nn(kk, sg), nt(q, sg))
                 for i in range(2):
-                    rows = slice(i * HEAD, (i + 1) * HEAD)
-                    back = turn(backs[i] * FACTOR, cos, -sin)
-                    n = wide(norm[b, h, rows, cut])
+                    rows = slice(i * HD, (i + 1) * HD)
+                    back = turn(backs[i][:HD] * FACTOR, cos, -sin)
+                    n = wide(norm[b, h, i * HEAD : (i + 1) * HEAD, cut])[:HD]
                     gain_sum[rows, :] += back * n
-                    dn = back * gains[rows, :1]
+                    dn = back * gain_cols[:HD, i : i + 1]
                     mean = jnp.sum(dn * n, axis=0, keepdims=True) * (1.0 / HD)
-                    dqkv[h, rows, cut] = low(stat[b, h, i : i + 1, cut] * (dn - n * mean))
-            gather_sum(h, dqkv[h], wa[b, : 3 * HEAD])
-        part[zz, yy, : 3 * HEAD, :] = low(nn(dqkv[0], buf_a[0]) + nn(dqkv[1], buf_a[1]))
+                    dqkv[h, rows, cut] = stat[b, h, i : i + 1, cut] * (dn - n * mean)
+            dlow[h] = low(dqkv[h])
+            gather_sum(h, dlow[h], wa[b, :QKV_ROWS])
+        qkv_part = nn(dlow[0], buf_a[0]) + nn(dlow[1], buf_a[1])
+        part[zz, yy, :A_ROWS, :] = low(jnp.concatenate([qkv_part[:QKV], out_part[HEAD - HD :]], axis=0))
         ones = jnp.ones((8, 512), jnp.bfloat16)
-        sums = nt(ones, dqkv[0]) + nt(ones, dqkv[1])
+        sums = nt(ones, dlow[0]) + nt(ones, dlow[1])
         s = slot(k)
-        payf[pl.ds(6 + s // 4, 1), pl.ds(pl.multiple_of(lax.rem(s, 4) * 256, 128), 3 * HEAD)] = sums[:1]
-
-        @pl.when(lax.rem(k, 3) == 2)
-        def _():
-            service(3 + k // 3)
-
-        pl.when(k == 3)(lambda: send_stages(8, 9, 0))
-
-    send_stages(8, 9, 1)
+        payf[pl.ds(6 + s // 4, 1), pl.ds(pl.multiple_of(lax.rem(s, 4) * 256, 128), QKV)] = sums[:1, :QKV]
+
+        pl.when(lax.rem(k, 3) != 0)(lambda: service(D_STAGES + 1 + k - k // 3, GU_STAGES))
+
+    send_stages(GU_STAGES, GU_STAGES - 1 + AHEAD)
     share_second.wait_send()
     begin_f(0)
     share_first = share_half(2, came)
-    service(5)
-    send_stages(9, 12, 0)
-    send_stages(9, 12, 1)
+    service(GU_STAGES - 1, R_STAGES)
     share_first.wait_recv()
 
     def first_rows(image, rows):
@@ -815,7 +869,7 @@
     by_rows(first_rows)
     save_tokens = pltpu.make_async_copy(acc.at[pl.ds(0, 512)], tokens_out, ls.at[3])
     save_tokens.start()
-    service(6)
+    service(GU_STAGES, R_STAGES)
     save_tokens.wait()
     clear(acc)
 
@@ -828,9 +882,7 @@
 
     share_first.wait_send()
     share_feed = share_half(3, came_feed)
-    service(7)
-    send_stages(12, 14, 0)
-    send_stages(12, 14, 1)
+    service(GU_STAGES + 1, R_STAGES)
     share_feed.wait_recv()
 
     def result_rows(image, rows):
@@ -843,9 +895,14 @@
     save_result = pltpu.make_async_copy(result, result_out, ls.at[4])
     save_result.start()
     lanes = gain_sum[:, :128] + gain_sum[:, 128:]
-    lanes = jnp.concatenate([lanes, jnp.zeros((96, 128), jnp.float32)], axis=0)
+    lanes = jnp.concatenate([lanes, jnp.zeros((256 - 2 * HD, 128), jnp.float32)], axis=0)
     payf[14:15, :256] = jnp.sum(jnp.transpose(lanes), axis=0, keepdims=True)
-    pay[...] = low(payf[...] * keep[...])
+    for image in range(2):
+        real = jnp.where(t * 2 + image < counts[0], 1.0, 0.0)
+        for k in (2, 5):
+            row = slice(image * 8 + k, image * 8 + k + 1)
+            payf[row, :] = payf[row, :] * real
+    pay[...] = low(payf[...])
     me = d * 8 + t
     keep_pay = pltpu.make_async_copy(pay, pay_all.at[me], ls.at[5])
     keep_pay.start()
@@ -853,9 +910,9 @@
     for cp in pays:
         cp.start()
 
-    @pl.loop(8, 14)
+    @pl.loop(GU_STAGES + 2, GU_STAGES + 6)
     def _(i):
-        service(i)
+        service(i, R_STAGES)
 
     keep_pay.wait()
     for cp in pays:
@@ -866,22 +923,24 @@
         swaps.append(remote(pay_all.at[rows], pay_all.at[rows], ps.at[15 + xx], pr.at[15 + xx], core))
         swaps[-1].start()
 
-    @pl.loop(14, R_STAGES + 5)
+    @pl.loop(GU_STAGES + 6, R_STAGES + 5)
     def _(i):
-        service(i)
+        service(i, R_STAGES)
 
     @pl.loop(0, R_STAGES)
     def _(g):
-        xcopy(g, 0).wait_send()
-        xcopy(g, 1).wait_send()
-        ycopy(g).wait_send()
-        for j in (3, 2, 1):
-            pl.when(z + j <= 3)(lambda: zcopy(g, z + j, 0).wait_send())
-            pl.when(z >= j)(lambda: zcopy(g, z - j, 1).wait_send())
-        fcopy(g, 0).wait_send()
-        own_copy(g).wait()
-        fcopy(g, 2).wait()
-        fcopy(g, 3).wait()
+        for side in (0, 1):
+            xcopy(g, side).wait_send()
+        for k in range(3):
+            ycopy(g, k).wait_send()
+        lone = lone_z(g, y)
+        pl.when(z < 3)(lambda: zcopy(g, 0, 0).wait_send())
+        pl.when(z > 0)(lambda: zcopy(g, 1, 0).wait_send())
+        pl.when(z < lone)(lambda: zcopy(g, 0, 1).wait_send())
+        pl.when(z > lone)(lambda: zcopy(g, 1, 1).wait_send())
+        pl.when(z == lone)(lambda: finished(g).wait_send())
+        pl.when(z != 3 - lone)(lambda: own_copy(g).wait())
+        core_copy(g, True).wait()
 
     for cp in swaps:
         cp.wait()
@@ -890,7 +949,7 @@
     save_result.wait()
 
 
-def backward(saved, tokens, out_grad, mod, keep, gains, table):
+def backward(saved, counts, tokens, out_grad, mod, gains, table):
     dma = pltpu.SemaphoreType.DMA
     regular = pltpu.SemaphoreType.REGULAR
     vm = pltpu.VMEM
@@ -902,26 +961,27 @@
     return pl.pallas_call(
         backward_kernel,
         out_shape=tuple(jax.ShapeDtypeStruct(s, e) for s, e in outs),
-        in_specs=[anywhere] * len(saved) + [inside] * 6,
+        in_specs=[anywhere] * len(saved) + [pl.BlockSpec(memory_space=pltpu.SMEM)] + [inside] * 5,
         out_specs=(anywhere,) * len(outs),
         scratch_shapes=[
-            vm((4, 2, ROWS_ALL, D), bf), vm((X_RING, 4, 2, R_LONE, D), bf), vm((Y_RING, 4, R_PLANE, D), bf),
-            vm((Z_RING, 5, R_PLANE, D), bf), vm((R_STAGES * R_MID, D), bf),
+            vm((4, 2, ROWS_ALL, D), bf), vm((X_RING, 2, R_STAGE, D), bf), vm((Y_RING, 3, R_STAGE, D), bf),
+            vm((Z_RING, 4, R_STAGE, D), bf), vm((ROWS_ALL, D), bf),
             vm((2, R, D), bf), vm((2, R, D), bf), vm((2 * R, D), f32), vm((R, D), f32), vm((R, D), f32),
             vm((R, D), bf), vm((R, D), bf), vm((R, D), bf), vm((R, D), bf),
             vm((2, C_ROWS, D), bf), vm((2, B_ROWS, D), bf), vm((2, A_ROWS, D), bf),
             vm((2, 2, SHARD_FF, R), bf), vm((2, 2, B_ROWS, R), bf), vm((2, 2, 3 * HEAD, R), bf),
             vm((2, 2, 2 * HEAD, R), bf), vm((2, 2, 8, R), f32), vm((2, 2, HEAD, R), bf),
-            vm((2, 3 * HEAD, R), bf), vm((2 * HEAD, PATCH), f32), vm((16, D), f32), vm((16, D), bf),
-            dma((R_STAGES, 2)), dma((R_STAGES, 2)), dma((R_STAGES,)), dma((R_STAGES,)),
-            dma((R_STAGES, 2, 4)), dma((R_STAGES, 2, 4)), dma((R_STAGES, 5)), dma((R_STAGES, 4)),
-            dma((4,)), dma((4,)), dma((17,)), dma((17,)), dma((6,)), dma((9, 2)),
+            vm((2, QKV_ROWS, R), f32), vm((2, QKV_ROWS, R), bf), vm((2 * HD, PATCH), f32), vm((16, D), f32),
+            vm((16, D), bf),
+            dma((R_STAGES, 2)), dma((R_STAGES, 2)), dma((R_STAGES, 3)), dma((R_STAGES, 3)),
+            dma((R_STAGES, 4)), dma((R_STAGES, 4)), dma((R_STAGES, 3)), dma((R_STAGES, 2)),
+            dma((4,)), dma((4,)), dma((17,)), dma((17,)), dma((7,)), dma((9, 2)),
             regular, regular, regular((2,)),
         ],
         compiler_params=pltpu.CompilerParams(
             collective_id=1, has_side_effects=True, vmem_limit_bytes=62 * 2**20),
         name="backward",
-    )(*saved, tokens, out_grad, mod, keep, gains, table)
+    )(*saved, counts, tokens, out_grad, mod, gains, table)
 
 
 def normalize(vectors, axis=-1, count=None):
@@ -940,61 +1000,23 @@
     return sigma * (1.0 + values * (1.0 - sigma))
 
 
-def pair_rows(heads):
-    lead, n = heads.shape[:-2], heads.shape[-1]
-    split = heads.reshape(lead + (2, 2, 18, n))
-    split = jnp.swapaxes(split, -4, -3).reshape(lead + (2, 36, n))
-    return jnp.pad(split, [(0, 0)] * len(lead) + [(0, 0), (0, 4), (0, 0)]).reshape(lead + (HEAD, n))
-
-
-def unpair_rows(rows):
-    lead, n = rows.shape[:-2], rows.shape[-1]
-    split = rows.reshape(lead + (2, HALF, n))[..., :36, :].reshape(lead + (2, 2, 18, n))
-    return jnp.swapaxes(split, -4, -3).reshape(lead + (HD, n))
-
-
-def pad_rows(rows):
-    return jnp.pad(rows, [(0, 0)] * (rows.ndim - 2) + [(0, 8), (0, 0)])
-
-
-def pair_tables():
+def pair_tables(count):
     pairs = HD // 4
     theta = np.exp(-math.log(100.0) * np.arange(pairs, dtype=np.float32) / pairs)
-    spot = np.arange(PATCH)
-    angle = np.concatenate([theta[:, None] * (spot // GRID)[None], theta[:, None] * (spot % GRID)[None]])
-    pad = ((0, HALF - 36), (0, 0))
-    return (
-        np.pad(np.cos(angle), pad).astype(np.float32),
-        np.pad(np.sin(angle), pad).astype(np.float32),
-    )
-
-
-def rotate_pairs(v, cos, sin):
-    a, b = v[..., :HALF, :], v[..., HALF:, :]
-    return jnp.concatenate([a * cos - b * sin, b * cos + a * sin], axis=-2)
-
-
-def pack_weights(qkv_weight, out_weight, gate_up_weight, down_weight, c):
-    heads = lax.dynamic_slice_in_dim(qkv_weight, c * HD, HD, 2).transpose(1, 2, 0)
-    qk = pair_rows(heads[:2]).reshape(2 * HEAD, D)
-    v = pad_rows(heads[2])
-    o = pad_rows(lax.dynamic_slice_in_dim(out_weight, c * HD, HD, 0))
-    gu = lax.dynamic_slice_in_dim(gate_up_weight, c * SHARD_FF, SHARD_FF, 2)
-    gu = gu.transpose(1, 2, 0).reshape(B_ROWS, D)
-    dn = lax.dynamic_slice_in_dim(down_weight, c * SHARD_FF, SHARD_FF, 0)
-    return jnp.concatenate([qk, v, o, gu, dn], axis=0)
+    spot = np.arange(count) % PATCH
+    a, b = theta[:, None] * (spot // GRID)[None], theta[:, None] * (spot % GRID)[None]
+    cos = np.concatenate([np.cos(a), np.cos(a), np.cos(b), np.cos(b)])
+    sin = np.concatenate([-np.sin(a), np.sin(a), -np.sin(b), np.sin(b)])
+    return np.concatenate([cos, sin]).astype(np.float32)
 
 
 def unpack_grads(both):
-    both = both.astype(jnp.float32)
-    qk = unpair_rows(both[:, : 2 * HEAD].reshape(2, 2, HEAD, D))
-    v = both[:, 2 * HEAD : 2 * HEAD + HD].reshape(2, 1, HD, D)
-    qkv = jnp.concatenate([qk, v], axis=1).transpose(3, 1, 0, 2).reshape(D, 3, 2 * HD)
-    o = both[:, 3 * HEAD : 3 * HEAD + HD].reshape(2 * HD, D)
+    qkv = both[:, :QKV].reshape(2, 3, HD, D).swapaxes(0, 1).reshape(3, 2 * HD, D)
+    o = both[:, QKV:A_ROWS].reshape(2 * HD, D)
     gu = both[:, A_ROWS : A_ROWS + B_ROWS].reshape(2, 2, SHARD_FF, D)
     gu = gu.transpose(3, 1, 0, 2).reshape(D, 2, 2 * SHARD_FF)
     dn = both[:, A_ROWS + B_ROWS :].reshape(2 * SHARD_FF, D)
-    return qkv, o, gu, dn
+    return [wide(v) for v in (qkv.transpose(2, 0, 1), o, gu, dn)]
 
 
 def fast(
@@ -1004,7 +1026,6 @@
     dot = lambda s, a, b: jnp.einsum(s, a, b, preferred_element_type=jnp.float32)
     t = lax.axis_index("tensor")
     c = lax.axis_index("dp") % 2
-    own = pack_weights(qkv_weight, out_weight, gate_up_weight, down_weight, c)
     images = labels.shape[0]
     columns_here = class_table.shape[1]
     column = t * columns_here + jnp.arange(columns_here)
@@ -1014,51 +1035,36 @@
     time_embed = jnp.where(column[None, :] < half_width, jnp.cos(angles), jnp.sin(angles))
     classes = jnp.arange(class_table.shape[0])
     condition = dot("in,nc->ic", low(labels[:, None] == classes[None, :]), class_table) + time_embed
-    mod_part = dot("ic,ckd->ikd", low(jax.nn.silu(condition)), ada_weight)
-    heads = qkv_bias.reshape(3, 2, HD).swapaxes(0, 1)[..., None]
-    bias_row = jnp.concatenate([pair_rows(heads[:, :2]).reshape(2, -1), pad_rows(heads[:, 2])[..., 0]], axis=1)
-    bias_row = jnp.pad(bias_row, ((0, 0), (0, 16))).reshape(1, 1, -1)
-    bias_row = jnp.pad(bias_row, ((0, 0), (0, 0), (0, D - bias_row.size)))
-    bias_row = jnp.broadcast_to(bias_row, (images, 1, D))
-    mod_part = jnp.concatenate([low(mod_part), bias_row, jnp.zeros_like(bias_row)], axis=1)
-    cond_part = jnp.concatenate(
-        [condition, labels.astype(jnp.float32)[:, None], jnp.zeros((images, 256 - columns_here - 1), jnp.float32)], axis=1)
-    mod_images = images // 8
-    kept = (t * mod_images + jnp.arange(mod_images) < image_counts[0]).astype(jnp.float32)
-    ada = jnp.pad(ada_bias.astype(jnp.float32), ((0, 2), (0, 0)))
-    ada = jnp.tile(ada, (mod_images, 1))
-    gate_rows = jnp.array([0, 0, 1, 0, 0, 1, 0, 0], jnp.float32)
-    keep = jnp.where(gate_rows[None, :] > 0, kept[:, None], 1.0).reshape(-1, 1)
-    keep = jnp.broadcast_to(keep, ada.shape)
-    gain_rows = jnp.broadcast_to(pair_rows(qk_scale.astype(jnp.float32)[..., None]).reshape(2 * HEAD, 1), (2 * HEAD, 128))
-    cos, sin = pair_tables()
-    table = np.tile(np.concatenate([cos, sin]), (1, tokens.shape[0] // PATCH))
-    (weights, cond_all, mod, first_in, second_in, feed_grad, attention, qkv_t, norm_t, stat_t, mixed, gu_t, hidden) = forward(
-        own, mod_part.reshape(8, images, D), cond_part, tokens, out_grad, ada, keep, gain_rows, table)
-    cond_all = cond_all.reshape(4 * images, 256)
+    gu = lax.dynamic_slice_in_dim(gate_up_weight, c * SHARD_FF, SHARD_FF, 2)
+    gu = gu.transpose(1, 2, 0).reshape(B_ROWS, D)
+    table = pair_tables(tokens.shape[0])
+    (weights, cond_all, mod, first_in, second_in, feed_grad, attention, qkv_t, norm_t, stat_t, mixed, gu_t, hidden,
+     down_part) = forward(
+        image_counts, qkv_weight.transpose(1, 2, 0), out_weight, gu, down_weight, condition, labels[:, None],
+        ada_weight.transpose(1, 0, 2), ada_bias, qkv_bias, tokens, out_grad, qk_scale, table)
+    saved = (weights, first_in, second_in, feed_grad, attention, qkv_t, norm_t, stat_t, mixed, gu_t, hidden,
+             down_part.reshape(4, 2, C_ROWS, D))
+    result, tokens_grad, summed, pay_all = backward(saved, image_counts, tokens, out_grad, mod, qk_scale, table)
+    qkv_weight_grad, out_weight_grad, gate_up_grad, down_grad = unpack_grads(summed)
+
+    cond_all = cond_all.reshape(4 * images, -1)
     condition = cond_all[:, :columns_here]
-    labels_all = cond_all[:, columns_here].astype(jnp.int32)
-    chosen = low(labels_all[:, None] == classes[None, :])
+    chosen = low(cond_all[:, columns_here].astype(jnp.int32)[:, None] == classes[None, :])
     cond_act = low(jax.nn.silu(condition))
     first_image = lax.axis_index("dp") * images
-    saved = (weights, first_in, second_in, feed_grad, attention, qkv_t, norm_t, stat_t, mixed, gu_t, hidden)
-    result, tokens_grad, summed, pay_all = backward(saved, tokens, out_grad, mod, keep, gain_rows, table)
-    qkv_weight_grad, out_weight_grad, gate_up_grad, down_grad = unpack_grads(summed)
-    pay_all = pay_all.reshape(32, mod_images, 8, D)
+    pay_all = pay_all.reshape(32, 2, 8, D)
     mod_grad = pay_all[:, :, :6].reshape(-1, 6, D)
-    bias_all = pay_all[:, 0, 6:, : 4 * 256].astype(jnp.float32).reshape(32, 8, 256)[..., : 3 * HEAD]
-    scale_all = pay_all[:, 1, 6, : 2 * HEAD].astype(jnp.float32).reshape(32, 2, HEAD)
-    qk_scale_grad = unpair_rows(jnp.sum(scale_all, axis=0)[..., None])[..., 0]
-    bias_all = lax.dynamic_index_in_dim(bias_all, t, 1, keepdims=False).reshape(2, 2, 8, 3, HEAD)
+    scale_all = wide(pay_all[:, 1, 6, : 2 * HD])
+    qk_scale_grad = jnp.sum(scale_all, axis=0).reshape(2, HD)
+    bias_all = wide(pay_all[:, 0, 6:, : 4 * 256]).reshape(32, 8, 256)[..., :QKV]
+    bias_all = lax.dynamic_index_in_dim(bias_all, t, 1, keepdims=False).reshape(2, 2, 8, 3, HD)
     bias_sum = jnp.sum(bias_all, axis=(0, 2))
-    qk_bias = unpair_rows(bias_sum[:, :2, :, None])[..., 0]
-    qkv_bias_grad = jnp.concatenate([qk_bias, bias_sum[:, 2:, :HD]], axis=1).transpose(1, 0, 2).reshape(3, 2 * HD)
-
+    qkv_bias_grad = bias_sum.swapaxes(0, 1).reshape(3, 2 * HD)
     ada_weight_grad = dot("ic,ikd->ckd", cond_act, mod_grad)
-    ada_bias_grad = jnp.sum(mod_grad.astype(jnp.float32), axis=0)
+    ada_bias_grad = jnp.sum(wide(mod_grad), axis=0)
     act_grad = dot("ikd,ckd->ic", mod_grad, ada_weight)
     cond_grad_all = act_grad * silu_slope(condition)
-    table_grad = jnp.dot(chosen.astype(jnp.float32).T, cond_grad_all, precision=HIGH)
+    table_grad = jnp.dot(wide(chosen).T, cond_grad_all, precision=HIGH)
     cond_grad = lax.dynamic_slice_in_dim(cond_grad_all, first_image, images, 0)
     return (
         result, tokens_grad, cond_grad, table_grad, ada_weight_grad, ada_bias_grad,

time: 435 us -> 367 us (0.84)
  Pallas kernels: 370 us -> 327 us
  local copies, waits for them, and re-layouts: 44.8 us -> 21.8 us
    pallas_call x1, Pallas kernels: 207 us -> 173 us  [backward(): pl.pallas_call(backward_kernel, out_shape=tuple((jax.ShapeDtypeStruct(s,...]
    unnamed x35 -> x16, local copies, waits for them, and re-layouts: 20.6 us -> 9.42 us
    pallas_call x1, Pallas kernels: 162 us -> 153 us  [forward(): pl.pallas_call(forward_kernel, out_shape=tuple((jax.ShapeDtypeStruct(s, e...]
where the time goes in v3:
time: 367 us
  Pallas kernels  327 us (89%)
  local copies, waits for them, and re-layouts  21.8 us (6%)
  matrix products  9.21 us (3%)
  other arithmetic  7.32 us (2%)
    pallas_call x1, Pallas kernels, backward(): pl.pallas_call(backward_kernel, out_shape=tuple((jax.ShapeDtypeStruct(s,...  173 us
    pallas_call x1, Pallas kernels, forward(): pl.pallas_call(forward_kernel, out_shape=tuple((jax.ShapeDtypeStruct(s, e...  153 us
    unnamed x16, local copies, waits for them, and re-layouts  9.42 us
    dot_general x3, matrix products, fast(): jnp.einsum(s, a, b, preferred_element_type=jnp.float32)  7.93 us

profile of v3, /device:TPU:0, one launch (start us, length us, event | category | flops | bytes accessed | tf_op | source)
XLA Modules:
  0.0 366.6 jit_solution(12436143378058185609)
XLA Ops:
  0.6 0.0 copy-start
  1.5 0.7 convert_element_type.72
  2.1 1.3 copy.53.labels
  3.5 1.8 convolution_add_fusion.condition
  5.3 0.0 copy-done
  5.3 1.9 dynamic-slice_bitcast_fusion
  7.2 2.9 copy.52
  10.0 153.5 %forward.1 = (bf16[8,864,1152]{2,1,0:T(8,128)(2,1)}, f32[4,16,256]{2,1,0:T(8,128)}, f32[16,1152]{1,0:T(8,128)}, bf16[2,512,1152]{2,1,0:T(8,128)(2,1)}, bf16[2,51...) custom-call(s32[1]{0:T(128)S(6)} %copy.68.counts, ...), custom_call_target="tpu_custom_call" | custom-call | tf_op jit(solution)/shard_map/forward/pallas_call | solution.py:472
  163.5 0.0 copy-start.4
  163.5 173.2 %backward.1 = (bf16[512,1152]{1,0:T(8,128)(2,1)}, f32[512,1152]{1,0:T(8,128)}, bf16[2,864,1152]{2,1,0:T(8,128)(2,1)}, bf16[32,16,1152]{2,1,0:T(8,128)(2,1)}) custom-call(bf16[8,864,1152]{2,1,0:T(8,128)(2,1)} %get-tuple-element.30.full, bf16[2,512,1152]{2,1,0:T(8,128)(2,1)} %get-tuple-element.31.fi_in, bf16[2,512,1152]{2,1,0:T(8,128)(2,1)} %get-tuple-element.32.si_in, ...), custom_call_target="tpu_custom_call" | custom-call | tf_op jit(solution)/shard_map/backward/pallas_call | solution.py:961
  336.7 0.9 fusion.8
  337.7 1.0 fusion.6
  338.7 0.6 reshape.98
  339.3 2.2 convert_reduce_fusion
  341.5 0.0 copy-done.4
  341.5 2.1 fusion
  343.5 0.6 constant_dynamic-slice_fusion
  344.1 1.2 slice_bitcast_fusion
  345.3 0.1 convert_element_type.82
  345.4 0.1 fusion.7
  345.5 0.1 reshape.96
  345.6 0.7 reshape.97
  346.3 1.0 slice.41
  347.3 0.9 bitcast_convert_fusion.1
  348.2 1.3 fusion.4
  349.5 0.0 copy-start.2
  349.5 1.4 slice.43
  350.9 1.4 bitcast_convert_fusion
  352.3 0.0 copy-done.2
  352.3 0.1 slice.36
  352.4 0.1 slice.42
  352.5 0.1 convert_bitcast_fusion
  352.7 1.4 copy.55
  354.1 0.2 copy.58
  354.3 4.7 %copy.59 = f32[1152,2,384]{2,1,0:T(2,128)} copy(f32[1152,2,384]{0,2,1:T(8,128)S(1)} %bitcast.45) | data formatting | bytes 7077888
  359.0 0.0 copy-start.5
  359.0 4.1 %fusion.1 = f32[144,6,1152]{2,0,1:T(8,128)} fusion(bf16[64,6,1152]{2,1,0:T(8,128)(2,1)} %bitcast.51, f32[64,256]{1,0:T(8,128)} %bitcast.61), kind=kOutput, calls=%fused_computation.7 | convolution fusion | flops 127448064 | bytes 4931584 | tf_op jit(solution)/shard_map/ic,ikd->ckd/dot_general | solution.py:1026
  363.1 0.0 copy-done.5
  363.1 0.0 copy-start.3
  363.1 0.0 copy-start.1
  363.1 1.0 copy.69
  364.1 1.1 copy-done.3
  365.2 1.4 copy.70
  366.6 0.0 copy-done.1
  (4 shorter events, 0.1 us)
Async XLA Ops:
  0.6 4.6 %copy-start = (bf16[1152,2,384]{2,1,0:T(2,128)(2,1)S(1)}, bf16[1152,2,384]{2,1,0:T(2,128)(2,1)}, u32[]{:S(2)}) copy-start(bf16[1152,2,384]{2,1,0:T(2,128)(2,1)} %param.26) | copy-start | bytes 5308420
  163.5 178.0 %copy-start.4 = (bf16[144,6,1152]{2,0,1:T(8,128)(2,1)S(1)}, bf16[144,6,1152]{2,0,1:T(8,128)(2,1)}, u32[]{:S(2)}) copy-start(bf16[144,6,1152]{2,0,1:T(8,128)(2,1)} %param.20) | copy-start | bytes 5971972
  349.5 2.8 copy-start.2
  359.0 4.1 %copy-start.5 = (bf16[512,1152]{1,0:T(8,128)(2,1)S(1)}, bf16[512,1152]{1,0:T(8,128)(2,1)}, u32[]{:S(2)}) copy-start(bf16[512,1152]{1,0:T(8,128)(2,1)} %get-tuple-element.108) | copy-start | bytes 3538948
  363.1 2.1 copy-start.3
  363.1 3.5 copy-start.1

commit v4 on v3

--- a/solution.py
+++ b/solution.py
@@ -19,9 +19,12 @@
 QKV = 3 * HD
 A_ROWS = 4 * HD
 SHARD_FF = 192
+HALF_FF = SHARD_FF // 2
 B_ROWS = 2 * SHARD_FF
 C_ROWS = SHARD_FF
 ROWS_ALL = A_ROWS + B_ROWS + C_ROWS
+B_FIRST = A_ROWS
+C_FIRST = A_ROWS + B_ROWS
 HEAD = 80
 O_FIRST = A_ROWS - HEAD
 QKV_ROWS = 224
@@ -29,10 +32,12 @@
 FACTOR = HD ** (-0.5)
 PAY = 16
 
-G_STAGE, G_LONE = 96, 32
+G_STAGE, G_LONE = 48, 16
 G_STAGES = ROWS_ALL // G_STAGE
+G_TURNED = (3, 9, 15)
 A_STAGES = A_ROWS // G_STAGE
-AB_STAGES = (A_ROWS + B_ROWS) // G_STAGE
+HALF_STAGES = (A_ROWS + SHARD_FF) // G_STAGE
+AB_STAGES = C_FIRST // G_STAGE
 
 R_STAGE = 48
 R_STAGES = ROWS_ALL // R_STAGE
@@ -105,23 +110,32 @@
 
 
 def forward_kernel(
-    counts, qkv_w, out_w, gu_w, down_w, condition, labels, ada_w, ada_b, bias_w, tokens, out_grad, gains, table,
+    counts, qkv_hbm, out_hbm, gu_w, down_w, condition, labels, ada_hbm, ada_b, bias_w, tokens_hbm, out_grad_hbm, gains, table,
     full, cond_out, mod_out, fi_out, si_out, fg_out, att_out, qkv_out, norm_out, stat_out, mixed_out, gu_out, hid_out,
     dd_out,
-    own, mod_in, mod_send, cond_in, mod_all, mod, fi, si, fg, att, att_send, att_recv, wa, ow, mixed, qkv, norm, stat, wb, gu,
+    qkv_w, out_w, ada_w, tokens, out_grad, own, mod_in, mod_send, cond_in, mod_all, mod, fi, si, fg, att, att_send, att_recv, wa, ow, mixed, qkv, norm, stat, wb, gu,
     hid, dd,
-    send, recv, ms, mr, cs, cr, es, er, ls, qs, hs, ws, save,
+    send, recv, ms, mr, cs, cr, es, er, ls, qs, hs, ws, save, fs,
 ):
     x, c, z, y = place()
     t = z * 2 + y
     d = x * 2 + c
     peers = [lax.rem(t + k, 8) for k in range(1, 8)]
     groups = [lax.rem(d + k, 4) for k in range(1, 4)]
-    load_gu = pltpu.make_async_copy(gu_w, own.at[pl.ds(A_ROWS, B_ROWS)], ls.at[4])
+    fetch = [
+        pltpu.make_async_copy(src, dst, fs.at[i])
+        for i, (src, dst) in enumerate(
+            [(qkv_hbm, qkv_w), (out_hbm, out_w), (ada_hbm, ada_w), (tokens_hbm, tokens), (out_grad_hbm, out_grad)])
+    ]
+    for cp in fetch:
+        cp.start()
+    load_gu = pltpu.make_async_copy(gu_w, own.at[pl.ds(B_FIRST, B_ROWS)], ls.at[4])
     load_gu.start()
     load_down = pltpu.make_async_copy(
-        down_w.at[rows_at(c * C_ROWS, C_ROWS)], own.at[pl.ds(A_ROWS + B_ROWS, C_ROWS)], ls.at[5])
+        down_w.at[rows_at(c * C_ROWS, C_ROWS)], own.at[pl.ds(C_FIRST, C_ROWS)], ls.at[5])
     load_down.start()
+    fetch[0].wait()
+    fetch[1].wait()
     for head in range(2):
         @pl.when(c == head)
         def _():
@@ -145,6 +159,15 @@
     def arrived(g, slot, rows, path):
         copy(g, 0, own, slot, rows, path, x_side).wait_recv()
 
+    def turned(g):
+        found = g == G_TURNED[0]
+        for other in G_TURNED[1:]:
+            found = jnp.logical_or(found, g == other)
+        return found
+
+    def straight(g):
+        return jnp.logical_not(turned(g))
+
     def issue(g):
         copy(g, 2, own, t, plane(g), 0, y_side).start()
         pl.when(z < 3)(lambda: copy(g, 0, own, t, plane(g), 0, up).start())
@@ -155,22 +178,33 @@
             slot = (z - j) * 2 + y
             arrived(g, slot, plane(g), 0)
             pl.when(z < 3)(lambda: copy(g, 1 + 2 * j, full.at[slot], slot, plane(g), 0, up).start())
-            copy(g, 8 + j, full.at[slot], slot, plane(g), 0, y_side).start()
+            pl.when(straight(g))(lambda: copy(g, 8 + j, full.at[slot], slot, plane(g), 0, y_side).start())
             copy(g, 11 + j, full.at[slot], slot, lone(g, x), 1, x_side).start()
 
         def above():
             slot = (z + j) * 2 + y
             arrived(g, slot, plane(g), 0)
             pl.when(z > 0)(lambda: copy(g, 2 + 2 * j, full.at[slot], slot, plane(g), 0, down).start())
-            copy(g, 14 + j, full.at[slot], slot, plane(g), 0, y_side).start()
+            pl.when(straight(g))(lambda: copy(g, 14 + j, full.at[slot], slot, plane(g), 0, y_side).start())
             copy(g, 17 + j, full.at[slot], slot, lone(g, x), 1, x_side).start()
 
         pl.when(z >= j)(below)
         pl.when(z + j <= 3)(above)
 
-    def along_y(g, zz):
+    def along_y(g, j, above):
+        zz = z + j if above else z - j
         slot = zz * 2 + 1 - y
         arrived(g, slot, plane(g), 0)
+
+        @pl.when(turned(g))
+        def _():
+            if j == 0 or not above:
+                kind = 25 if j == 0 else 8 + j
+                pl.when(z < 3)(lambda: copy(g, kind, full.at[slot], slot, plane(g), 0, up).start())
+            if j == 0 or above:
+                kind = 26 if j == 0 else 14 + j
+                pl.when(z > 0)(lambda: copy(g, kind, full.at[slot], slot, plane(g), 0, down).start())
+
         copy(g, 21 + zz, full.at[slot], slot, lone(g, x), 1, x_side).start()
 
     def service(i):
@@ -180,15 +214,15 @@
         on(i, issue)
         for j in (1, 2, 3):
             on(i - j, lambda g: along_z(g, j))
-        on(i - 1, lambda g: along_y(g, z))
+        on(i - 1, lambda g: along_y(g, 0, False))
         for j in (1, 2, 3):
             @pl.when(z >= j)
             def _():
-                on(i - j - 1, lambda g: along_y(g, z - j))
+                on(i - j - 1, lambda g: along_y(g, j, False))
 
             @pl.when(z + j <= 3)
             def _():
-                on(i - j - 1, lambda g: along_y(g, z + j))
+                on(i - j - 1, lambda g: along_y(g, j, True))
 
     def lone_in(first, last):
         @pl.loop(first, last)
@@ -211,15 +245,21 @@
     cond_in[:, :144] = condition[...]
     cond_in[:, 144:145] = wide(labels[...])
     mod_in[...] = jnp.zeros_like(mod_in)
+    for p in range(8):
+        for k, row in enumerate((6, 7, 14)):
+            mod_in[p, row : row + 1, :144] = wide(bias_w[k : k + 1, :])
+    load_gu.wait()
+    load_down.wait()
+    kept = [pltpu.make_async_copy(own, full.at[t], ls.at[0])]
+    kept[0].start()
+    fetch[2].wait()
+    service(1)
     v = condition[...]
     act = low(v * (1.0 / (1.0 + jnp.exp(-v))))
     for k in range(6):
         share = nn(act, ada_w[k])
         for image in range(16):
             mod_in[image // 2, image % 2 * 8 + k : image % 2 * 8 + k + 1, :] = share[image : image + 1]
-    for p in range(8):
-        for k, row in enumerate((6, 7, 14)):
-            mod_in[p, row : row + 1, :144] = wide(bias_w[k : k + 1, :])
     mod_send[...] = low(mod_in[...])
     small = []
     for k, p in enumerate(peers):
@@ -228,21 +268,19 @@
         small.append(remote(cond_in, cond_out.at[d], cs.at[k], cr.at[d], (g, t)))
     for cp in small:
         cp.start()
-    kept = [
+    kept += [
         pltpu.make_async_copy(mod_send.at[t], mod_all.at[t], ls.at[1]),
         pltpu.make_async_copy(cond_in, cond_out.at[d], ls.at[2]),
     ]
-    for cp in kept:
-        cp.start()
-    load_gu.wait()
-    load_down.wait()
-    kept.append(pltpu.make_async_copy(own, full.at[t], ls.at[0]))
+    kept[1].start()
     kept[2].start()
-    service(1)
-
+    service(2)
+    fetch[3].wait()
+    fetch[4].wait()
+    service(3)
     for p in peers:
         remote(mod_send.at[p], mod_all.at[p], ms.at[0], mr.at[p], (d, p)).wait_recv()
-    kept[0].wait()
+    kept[1].wait()
     for image in range(2):
         total = jnp.concatenate([wide(ada_b[...]), jnp.zeros((2, D), jnp.float32)], axis=0)
         for s in range(8):
@@ -251,28 +289,29 @@
         row = lax.broadcasted_iota(jnp.int32, (8, D), 0)
         gate = jnp.logical_or(row == 2, row == 5)
         mod[image * 8 : image * 8 + 8, :] = jnp.where(gate, total * real, total)
+    service(4)
 
     def first_rows(image, rows):
         v = wide(tokens[rows, :])
         n = v * lax.rsqrt(jnp.mean(v * v, axis=-1, keepdims=True) + epsilon)
         fi[0, rows, :] = low(n * (1.0 + mod_row(image, 1)) + mod_row(image, 0))
 
+    def feed_rows(image, rows):
+        fg[0, rows, :] = low(wide(out_grad[rows, :]) * mod_row(image, 5))
+
     by_rows(first_rows)
     share_fi = remote(fi.at[0], fi.at[1], es.at[0], er.at[0], core)
     share_fi.start()
-
-    def feed_rows(image, rows):
-        fg[0, rows, :] = low(wide(out_grad[rows, :]) * mod_row(image, 5))
-
+    service(5)
     by_rows(feed_rows)
     share_fg = remote(fg.at[0], fg.at[1], es.at[1], er.at[1], core)
     share_fg.start()
 
-    @pl.loop(2, A_STAGES + 4)
+    @pl.loop(6, A_STAGES + 4)
     def _(i):
         service(i)
 
-    kept[2].wait()
+    kept[0].wait()
     lone_in(0, A_STAGES)
     share_fi.wait_recv()
     share_fg.wait_recv()
@@ -338,8 +377,8 @@
         for cp in save_head(s):
             cp.start()
 
-        pl.when(s == 3)(lambda: service(A_STAGES + 4))
-        pl.when(s == 7)(lambda: service(A_STAGES + 5))
+        pl.when(jnp.logical_or(lax.rem(s, 5) == 0, jnp.logical_or(lax.rem(s, 5) == 2, s == 3)))(
+            lambda: service(A_STAGES + 4 + (s + 1) // 2))
 
     for s in (6, 7):
         for cp in save_head(s):
@@ -356,6 +395,7 @@
     for image in range(2):
         cut = slice(image * PATCH, (image + 1) * PATCH)
         att[cut, :] = tn(mixed[0, :, cut], ow[...].reshape(8 * HEAD, D))
+    service(A_STAGES + 9)
     share_att.wait_recv()
 
     def second_rows(image, rows):
@@ -368,12 +408,8 @@
     by_rows(second_rows)
     share_si = remote(si.at[0], si.at[1], es.at[3], er.at[3], core)
     share_si.start()
-
-    @pl.loop(A_STAGES + 6, AB_STAGES + 4)
-    def _(i):
-        service(i)
-
-    lone_in(A_STAGES, AB_STAGES)
+    service(A_STAGES + 10)
+
     share_si.wait_recv()
     saves += [
         pltpu.make_async_copy(att, att_out, save.at[4]),
@@ -382,46 +418,58 @@
     saves[-2].start()
     saves[-1].start()
 
-    def load_b(s):
-        return pltpu.make_async_copy(full.at[s, pl.ds(A_ROWS, B_ROWS)], wb.at[lax.rem(s, 2)], ws.at[2 + lax.rem(s, 2)])
-
-    def save_shard(s):
-        b = lax.rem(s, 2)
+    def load_b(half, p):
+        b = lax.rem(p, 2)
+        return pltpu.make_async_copy(
+            full.at[pl.ds(p * 2, 2), pl.ds(B_FIRST + half * SHARD_FF, SHARD_FF)], wb.at[b], ws.at[2 + b])
+
+    def save_pair(half, p):
+        b = lax.rem(p, 2)
+        both = pl.ds(p * 2, 2)
         return [
-            pltpu.make_async_copy(gu.at[b], gu_out.at[s], hs.at[b, 0]),
-            pltpu.make_async_copy(hid.at[b], hid_out.at[s], hs.at[b, 1]),
-            pltpu.make_async_copy(dd.at[b], dd_out.at[s], hs.at[b, 2]),
+            pltpu.make_async_copy(gu.at[b], gu_out.at[both, half], hs.at[b, 0]),
+            pltpu.make_async_copy(hid.at[b], hid_out.at[both, half], hs.at[b, 1]),
+            pltpu.make_async_copy(dd.at[b], dd_out.at[both, half], hs.at[b, 2]),
         ]
 
-    load_b(0).start()
-
-    @pl.loop(0, 8)
-    def _(s):
-        b = lax.rem(s, 2)
-        load_b(s).wait()
-        pl.when(s < 7)(lambda: load_b(s + 1).start())
-
-        @pl.when(s > 1)
-        def _():
-            for cp in save_shard(s - 2):
+    for half in range(2):
+        lone_in(A_STAGES + half * (HALF_STAGES - A_STAGES), HALF_STAGES + half * (HALF_STAGES - A_STAGES))
+        load_b(half, 0).start()
+
+        @pl.loop(0, 4)
+        def _(p):
+            b = lax.rem(p, 2)
+            load_b(half, p).wait()
+            pl.when(p < 3)(lambda: load_b(half, p + 1).start())
+
+            @pl.when(p > 1)
+            def _():
+                for cp in save_pair(half, p - 2):
+                    cp.wait()
+
+            for h in range(2):
+                both = nt(wb[b].reshape(2 * SHARD_FF, D), si[h])
+                for i in range(2):
+                    g = both[i * SHARD_FF : i * SHARD_FF + HALF_FF]
+                    u = both[i * SHARD_FF + HALF_FF : (i + 1) * SHARD_FF]
+                    hid[b, i, h] = low(g * (1.0 / (1.0 + jnp.exp(-g))) * u)
+                    gu[b, i, h] = low(both[i * SHARD_FF : (i + 1) * SHARD_FF])
+            grad = sum(
+                nn(jnp.concatenate([hid[b, 0, h], hid[b, 1, h]], axis=0), fg[h]) for h in range(2))
+            dd[b] = low(grad).reshape(2, HALF_FF, D)
+            for cp in save_pair(half, p):
+                cp.start()
+
+            if half == 0:
+                service(A_STAGES + 11 + p)
+            else:
+                pl.when(p == 2)(lambda: service(A_STAGES + 15))
+
+        for p in (2, 3):
+            for cp in save_pair(half, p):
                 cp.wait()
 
-        for h in range(2):
-            both = nt(wb[b], si[h])
-            g, u = both[:SHARD_FF], both[SHARD_FF:]
-            gu[b, h] = low(both)
-            hid[b, h] = low(g * (1.0 / (1.0 + jnp.exp(-g))) * u)
-        dd[b] = low(nn(hid[b, 0], fg[0]) + nn(hid[b, 1], fg[1]))
-        for cp in save_shard(s):
-            cp.start()
-
-        pl.when(s == 3)(lambda: service(AB_STAGES + 4))
-
-    service(AB_STAGES + 5)
     lone_in(AB_STAGES, G_STAGES)
-    for s in (6, 7):
-        for cp in save_shard(s):
-            cp.wait()
 
     @pl.loop(0, G_STAGES)
     def _(g):
@@ -433,24 +481,26 @@
         pl.when(z > 0)(lambda: sent(1, plane(g)))
         for k in range(4):
             sent(21 + k, lone(g, x))
+        pl.when(jnp.logical_and(turned(g), z < 3))(lambda: sent(25, plane(g)))
+        pl.when(jnp.logical_and(turned(g), z > 0))(lambda: sent(26, plane(g)))
         for j in (1, 2, 3):
             @pl.when(z >= j)
             def _():
                 pl.when(z < 3)(lambda: sent(1 + 2 * j, plane(g)))
-                sent(8 + j, plane(g))
+                pl.when(jnp.logical_or(straight(g), z < 3))(lambda: sent(8 + j, plane(g)))
                 sent(11 + j, lone(g, x))
 
             @pl.when(z + j <= 3)
             def _():
                 pl.when(z > 0)(lambda: sent(2 + 2 * j, plane(g)))
-                sent(14 + j, plane(g))
+                pl.when(jnp.logical_or(straight(g), z > 0))(lambda: sent(14 + j, plane(g)))
                 sent(17 + j, lone(g, x))
 
     for cp in small + [share_fi, share_fg, share_att, share_si]:
         cp.wait_send()
     for g in groups:
         remote(cond_in, cond_out.at[g], cs.at[0], cr.at[g], (g, t)).wait_recv()
-    kept[1].wait()
+    kept[2].wait()
     for cp in saves:
         cp.wait()
 
@@ -467,22 +517,24 @@
         ((8, ROWS_ALL, D), bf), ((4, 16, 256), f32), ((16, D), f32),
         ((2, R, D), bf), ((2, R, D), bf), ((2, R, D), bf), ((R, D), f32),
         ((8, 2, 3 * HEAD, R), bf), ((8, 2, 2 * HEAD, R), bf), ((8, 2, 8, R), f32), ((2, 8 * HEAD, R), bf),
-        ((8, 2, B_ROWS, R), bf), ((8, 2, SHARD_FF, R), bf), ((8, C_ROWS, D), bf),
+        ((8, 2, 2, SHARD_FF, R), bf), ((8, 2, 2, HALF_FF, R), bf), ((8, 2, HALF_FF, D), bf),
     ]
     return pl.pallas_call(
         forward_kernel,
         out_shape=tuple(jax.ShapeDtypeStruct(s, e) for s, e in outs),
-        in_specs=[scalar, inside, inside, anywhere, anywhere] + [inside] * 9,
+        in_specs=[scalar] + [anywhere] * 4 + [inside] * 2 + [anywhere] + [inside] * 2 + [anywhere] * 2 + [inside] * 2,
         out_specs=(anywhere,) * len(outs),
         scratch_shapes=[
+            vm((3, 144, D), bf), vm((144, D), bf), vm((6, 144, D), bf), vm((R, D), bf), vm((R, D), bf),
             vm((ROWS_ALL, D), bf), vm((8, 16, D), f32), vm((8, 16, D), bf), vm((16, 256), f32), vm((8, 16, D), bf),
             vm((16, D), f32),
             vm((2, R, D), bf), vm((2, R, D), bf), vm((2, R, D), bf), vm((R, D), f32), vm((R, D), bf), vm((R, D), bf),
             vm((2, QKV_ROWS, D), bf), vm((8, HEAD, D), bf), vm((2, 8 * HEAD, R), bf),
             vm((2, 2, 3 * HEAD, R), bf), vm((2, 2, 2 * HEAD, R), bf), vm((2, 2, 8, R), f32),
-            vm((2, B_ROWS, D), bf), vm((2, 2, B_ROWS, R), bf), vm((2, 2, SHARD_FF, R), bf), vm((2, C_ROWS, D), bf),
-            dma((G_STAGES, 25)), dma((G_STAGES, 8, 2)), dma((7,)), dma((8,)), dma((3,)), dma((4,)),
-            dma((4,)), dma((4,)), dma((6,)), dma((2, 3)), dma((2, 3)), dma((4,)), dma((6,)),
+            vm((2, 2, SHARD_FF, D), bf), vm((2, 2, 2, SHARD_FF, R), bf), vm((2, 2, 2, HALF_FF, R), bf),
+            vm((2, 2, HALF_FF, D), bf),
+            dma((G_STAGES, 27)), dma((G_STAGES, 8, 2)), dma((7,)), dma((8,)), dma((3,)), dma((4,)),
+            dma((4,)), dma((4,)), dma((6,)), dma((2, 3)), dma((2, 3)), dma((6,)), dma((6,)), dma((5,)),
         ],
         compiler_params=pltpu.CompilerParams(
             collective_id=0, has_side_effects=True, vmem_limit_bytes=60 * 2**20),
@@ -492,9 +544,9 @@
 
 def backward_kernel(
     full, fi_in, si_in, fg_in, att_in, qkv_in, norm_in, stat_in, mixed_in, gu_in, hid_in, dd_in,
-    counts, tokens, out_grad, mod, gains, table,
-    result_out, tokens_out, grads, pay_all,
-    part, xin, yin, zin, fin, buf_a, buf_b, acc, after, att, sent, came, came_feed, result,
+    counts, tokens_hbm, out_grad_hbm, ada_hbm, mod, gains, table, cond,
+    result_out, tokens_out, grads, pay_all, sums_out, bias_out, cond_out, class_out,
+    tokens, out_grad, ada_w, cond_all, part, xin, yin, zin, fin, buf_a, buf_b, acc, after, att, sent, came, came_feed, result,
     wd, wb, wa, hid, gu, qkv, norm, stat, mixed, dqkv, dlow, gain_sum, payf, pay,
     xs, xr, ys, yr, zs, zr, fs, fr, es, er, ps, pr, ls, lw, x_free, y_free, z_free,
 ):
@@ -503,26 +555,28 @@
     d = x * 2 + c
     y_side, x_side, core = at(x, c, z, 1 - y), at(1 - x, c, z, y), at(x, 1 - c, z, y)
     up, down = at(x, c, z + 1, y), at(x, c, z - 1, y)
-    spot = x * 8 + t
-    mates = []
-    for k in range(1, 16):
-        o = lax.rem(spot + k, 16)
-        mates.append(((o // 8) * 2 + c, lax.rem(o, 8)))
-    greet(mates + [core])
+    mates = [at(x, c, lax.rem(z + k, 4), y) for k in (1, 2, 3)] + [x_side, y_side]
 
     loads = [
         pltpu.make_async_copy(fg_in, buf_a, ls.at[0]),
         pltpu.make_async_copy(si_in, buf_b, ls.at[1]),
         pltpu.make_async_copy(att_in, att, ls.at[2]),
+        pltpu.make_async_copy(tokens_hbm, tokens, ls.at[7]),
+        pltpu.make_async_copy(out_grad_hbm, out_grad, ls.at[8]),
+        pltpu.make_async_copy(ada_hbm, ada_w, ls.at[9]),
     ]
     load_dd = pltpu.make_async_copy(
-        dd_in, part.at[:, :, pl.ds(A_ROWS + B_ROWS, C_ROWS)], ls.at[6])
+        dd_in, part.at[:, :, pl.ds(C_FIRST, C_ROWS)], ls.at[6])
     load_dd.start()
+    greet(mates + [core])
     for cp in loads:
         cp.start()
 
+    def first_of(g):
+        return ROWS_ALL - (g + 1) * R_STAGE
+
     def rows_of(g):
-        return rows_at((R_STAGES - 1 - g) * R_STAGE, R_STAGE)
+        return rows_at(first_of(g), R_STAGE)
 
     def side_y(side):
         return 1 - y if side == 0 else y
@@ -561,7 +615,7 @@
         return pltpu.make_async_copy(part.at[z, y, rows_of(g)], grads.at[c, rows_of(g)], fs.at[g, 2])
 
     def add(zz, yy, g, piece):
-        first = (R_STAGES - 1 - g) * R_STAGE
+        first = first_of(g)
 
         @pl.loop(0, R_STAGE // 16)
         def _(i):
@@ -644,7 +698,7 @@
         @pl.when(ends)
         def _():
             plane_sum(g).wait()
-            add(z, y, g, lambda r: fin[rows_at((R_STAGES - 1 - g) * R_STAGE + r.start, 16), :])
+            add(z, y, g, lambda r: fin[rows_at(first_of(g) + r.start, 16), :])
 
         @pl.when(jnp.logical_or(ends, here))
         def _():
@@ -733,12 +787,14 @@
         cp.start()
         return cp
 
+    load_dd.wait()
+    send_stages(0, AHEAD)
     payf[...] = jnp.zeros_like(payf)
     gain_sum[...] = jnp.zeros_like(gain_sum)
     clear(acc)
     begin_g, turn_g = stream([
-        (lambda s: full.at[s, pl.ds(A_ROWS + B_ROWS, C_ROWS)], wd, 1),
-        (lambda s: full.at[s, pl.ds(A_ROWS, B_ROWS)], wb, 2),
+        (lambda s: full.at[s, pl.ds(C_FIRST, C_ROWS)], wd, 1),
+        (lambda s: full.at[s, pl.ds(B_FIRST, B_ROWS)], wb, 2),
         (lambda s: gu_in.at[s], gu, 3),
     ])
     begin_a, turn_a = stream([
@@ -750,11 +806,9 @@
     ])
     begin_f, turn_f = stream([
         (lambda s: hid_in.at[s], hid, 0),
-        (lambda s: full.at[s, pl.ds(A_ROWS + B_ROWS, C_ROWS)], wd, 1),
+        (lambda s: full.at[s, pl.ds(C_FIRST, C_ROWS)], wd, 1),
     ])
     begin_g(0)
-    load_dd.wait()
-    send_stages(0, AHEAD)
     loads[0].wait()
     loads[1].wait()
 
@@ -766,24 +820,28 @@
         grads_here = []
         for h in range(2):
             hg = nt(wd[b], buf_a[h])
-            g, u = wide(gu[b, h, :SHARD_FF]), wide(gu[b, h, SHARD_FF:])
-            sig = 1.0 / (1.0 + jnp.exp(-g))
-            act = g * sig
-            both = low(jnp.concatenate([hg * u * (sig + act * (1.0 - sig)), hg * act], axis=0))
+            both = []
+            for half in range(2):
+                g, u = wide(gu[b, half, h, :HALF_FF]), wide(gu[b, half, h, HALF_FF:])
+                sig = 1.0 / (1.0 + jnp.exp(-g))
+                act = g * sig
+                this = hg[half * HALF_FF : (half + 1) * HALF_FF]
+                both += [low(this * u * (sig + act * (1.0 - sig))), low(this * act)]
+            both = jnp.concatenate(both, axis=0)
             grads_here.append(both)
             gather_sum(h, both, wb[b])
-        part[zz, yy, A_ROWS : A_ROWS + B_ROWS, :] = low(
-            nn(grads_here[0], buf_b[0]) + nn(grads_here[1], buf_b[1]))
+        part[zz, yy, B_FIRST:C_FIRST, :] = low(nn(grads_here[0], buf_b[0]) + nn(grads_here[1], buf_b[1]))
 
         pl.when(lax.rem(k, 2) == 1)(lambda: service(k // 2, D_STAGES))
 
-    send_stages(D_STAGES, D_STAGES + AHEAD)
-    share_second = share_half(0, came)
-    service(D_STAGES, GU_STAGES)
-    begin_a(0)
     load_fi = pltpu.make_async_copy(fi_in, buf_a, ls.at[0])
     load_fi.start()
-    loads[2].wait()
+    share_second = share_half(0, came)
+    send_stages(D_STAGES, D_STAGES + AHEAD)
+    begin_a(0)
+    service(D_STAGES, GU_STAGES)
+    for cp in loads[2:]:
+        cp.wait()
     share_second.wait_recv()
 
     def after_rows(image, rows):
@@ -878,7 +936,7 @@
         b = lax.rem(k, 2)
         turn_f(k)
         for h in range(2):
-            gather_sum(h, hid[b, h], wd[b])
+            gather_sum(h, jnp.concatenate([hid[b, 0, h], hid[b, 1, h]], axis=0), wd[b])
 
     share_first.wait_send()
     share_feed = share_half(3, came_feed)
@@ -903,27 +961,73 @@
             row = slice(image * 8 + k, image * 8 + k + 1)
             payf[row, :] = payf[row, :] * real
     pay[...] = low(payf[...])
-    me = d * 8 + t
-    keep_pay = pltpu.make_async_copy(pay, pay_all.at[me], ls.at[5])
+    keep_pay = pltpu.make_async_copy(pay, pay_all.at[x, c, z, y], ls.at[5])
     keep_pay.start()
-    pays = [remote(pay, pay_all.at[me], ps.at[k], pr.at[k], o) for k, o in enumerate(mates)]
+    pay_x = remote(pay, pay_all.at[x, c, z, y], ps.at[0], pr.at[0], x_side)
+    pay_x.start()
+    service(GU_STAGES + 2, R_STAGES)
+    keep_pay.wait()
+    pay_x.wait_recv()
+    line = pay_all.at[:, c, z, y]
+    pay_y = remote(line, line, ps.at[1], pr.at[1], y_side)
+    pay_y.start()
+    service(GU_STAGES + 3, R_STAGES)
+    pay_y.wait_recv()
+    square = pay_all.at[:, c, z]
+    pays = [remote(square, square, ps.at[1 + k], pr.at[1 + k], at(x, c, lax.rem(z + k, 4), y)) for k in (1, 2, 3)]
     for cp in pays:
         cp.start()
 
-    @pl.loop(GU_STAGES + 2, GU_STAGES + 6)
+    @pl.loop(GU_STAGES + 4, GU_STAGES + 6)
     def _(i):
         service(i, R_STAGES)
 
-    keep_pay.wait()
     for cp in pays:
         cp.wait()
-    swaps = []
-    for xx in range(2):
-        rows = pl.ds(pl.multiple_of((xx * 2 + c) * 8, 8), 8)
-        swaps.append(remote(pay_all.at[rows], pay_all.at[rows], ps.at[15 + xx], pr.at[15 + xx], core))
-        swaps[-1].start()
-
-    @pl.loop(GU_STAGES + 6, R_STAGES + 5)
+    layer = pay_all.at[:, c]
+    swap = remote(layer, layer, ps.at[5], pr.at[5], core)
+    swap.start()
+
+    service(GU_STAGES + 6, R_STAGES)
+    share_feed.wait_send()
+    swap.wait()
+    load_pay = pltpu.make_async_copy(pay_all.reshape(32 * PAY, D), sent, ls.at[5])
+    load_pay.start()
+    service(GU_STAGES + 7, R_STAGES)
+    load_pay.wait()
+
+    def picked(count, which):
+        row = lax.broadcasted_iota(jnp.int32, (count, 32 * PAY), 0)
+        col = lax.broadcasted_iota(jnp.int32, (count, 32 * PAY), 1)
+        return nn(jnp.where(which(row, col), 1.0, 0.0).astype(jnp.bfloat16), sent[...])
+
+    act = jnp.zeros((64, 144), jnp.float32)
+    for k in range(6):
+        mg = picked(64, lambda row, col: col == row * 8 + k)
+        sums_out[k : k + 1, :] = jnp.sum(mg, axis=0, keepdims=True)
+        act = act + nt(low(mg), ada_w[k])
+    payf[:8, :] = picked(8, lambda row, col: jnp.logical_or(
+        jnp.logical_and(row == 0, lax.rem(col, PAY) == 14),
+        jnp.logical_and(row == 1 + lax.rem(col // (8 * PAY), 2), lax.rem(col, PAY) == 6 + t // 4)))
+    sums_out[6:8, :] = payf[0:2, :]
+    bias_out[...] = payf[:8, pl.ds(pl.multiple_of(lax.rem(t, 4) * 256, 128), 256)]
+    for group in range(4):
+        cond_all[group * 16 : (group + 1) * 16, :] = cond[group]
+    v = cond_all[:, :144]
+    sig = 1.0 / (1.0 + jnp.exp(-v))
+    cond_all[:, :144] = act * sig * (1.0 + v * (1.0 - sig))
+    cond_out[...] = cond_all[rows_at(d * 16, 16), :144]
+    rest = cond_all[:, :144]
+    classes = lax.broadcasted_iota(jnp.int32, (64, class_out.shape[1]), 1)
+    chosen = jnp.where(classes == cond_all[:, 144:145].astype(jnp.int32), 1.0, 0.0).astype(jnp.bfloat16)
+    total = jnp.zeros(class_out.shape, jnp.float32)
+    for _ in range(3):
+        piece = low(rest)
+        rest = rest - wide(piece)
+        total = total + tn(piece, chosen)
+    class_out[...] = total
+
+    @pl.loop(GU_STAGES + 8, R_STAGES + 5)
     def _(i):
         service(i, R_STAGES)
 
@@ -942,14 +1046,13 @@
         pl.when(z != 3 - lone)(lambda: own_copy(g).wait())
         core_copy(g, True).wait()
 
-    for cp in swaps:
-        cp.wait()
+    pay_x.wait_send()
+    pay_y.wait_send()
     share_ag.wait_send()
-    share_feed.wait_send()
     save_result.wait()
 
 
-def backward(saved, counts, tokens, out_grad, mod, gains, table):
+def backward(saved, counts, tokens, out_grad, ada_w, mod, gains, table, cond, classes):
     dma = pltpu.SemaphoreType.DMA
     regular = pltpu.SemaphoreType.REGULAR
     vm = pltpu.VMEM
@@ -957,31 +1060,32 @@
     anywhere = pl.BlockSpec(memory_space=pl.ANY)
     inside = pl.BlockSpec(memory_space=pltpu.VMEM)
     R = tokens.shape[0]
-    outs = [((R, D), bf), ((R, D), f32), ((2, ROWS_ALL, D), bf), ((32, PAY, D), bf)]
+    outs = [((R, D), bf), ((R, D), f32), ((2, ROWS_ALL, D), bf), ((2, 2, 4, 2, PAY, D), bf)]
+    small = [((8, D), f32), ((8, 256), f32), ((16, 144), f32), ((144, classes), f32)]
     return pl.pallas_call(
         backward_kernel,
-        out_shape=tuple(jax.ShapeDtypeStruct(s, e) for s, e in outs),
-        in_specs=[anywhere] * len(saved) + [pl.BlockSpec(memory_space=pltpu.SMEM)] + [inside] * 5,
-        out_specs=(anywhere,) * len(outs),
+        out_shape=tuple(jax.ShapeDtypeStruct(s, e) for s, e in outs + small),
+        in_specs=[anywhere] * len(saved) + [pl.BlockSpec(memory_space=pltpu.SMEM)] + [anywhere] * 3 + [inside] * 4,
+        out_specs=(anywhere,) * len(outs) + (inside,) * len(small),
         scratch_shapes=[
-            vm((4, 2, ROWS_ALL, D), bf), vm((X_RING, 2, R_STAGE, D), bf), vm((Y_RING, 3, R_STAGE, D), bf),
+            vm((R, D), bf), vm((R, D), bf), vm((6, 144, D), bf), vm((64, 256), f32), vm((4, 2, ROWS_ALL, D), bf), vm((X_RING, 2, R_STAGE, D), bf), vm((Y_RING, 3, R_STAGE, D), bf),
             vm((Z_RING, 4, R_STAGE, D), bf), vm((ROWS_ALL, D), bf),
             vm((2, R, D), bf), vm((2, R, D), bf), vm((2 * R, D), f32), vm((R, D), f32), vm((R, D), f32),
             vm((R, D), bf), vm((R, D), bf), vm((R, D), bf), vm((R, D), bf),
             vm((2, C_ROWS, D), bf), vm((2, B_ROWS, D), bf), vm((2, A_ROWS, D), bf),
-            vm((2, 2, SHARD_FF, R), bf), vm((2, 2, B_ROWS, R), bf), vm((2, 2, 3 * HEAD, R), bf),
+            vm((2, 2, 2, HALF_FF, R), bf), vm((2, 2, 2, SHARD_FF, R), bf), vm((2, 2, 3 * HEAD, R), bf),
             vm((2, 2, 2 * HEAD, R), bf), vm((2, 2, 8, R), f32), vm((2, 2, HEAD, R), bf),
             vm((2, QKV_ROWS, R), f32), vm((2, QKV_ROWS, R), bf), vm((2 * HD, PATCH), f32), vm((16, D), f32),
             vm((16, D), bf),
             dma((R_STAGES, 2)), dma((R_STAGES, 2)), dma((R_STAGES, 3)), dma((R_STAGES, 3)),
             dma((R_STAGES, 4)), dma((R_STAGES, 4)), dma((R_STAGES, 3)), dma((R_STAGES, 2)),
-            dma((4,)), dma((4,)), dma((17,)), dma((17,)), dma((7,)), dma((9, 2)),
+            dma((4,)), dma((4,)), dma((6,)), dma((6,)), dma((10,)), dma((9, 2)),
             regular, regular, regular((2,)),
         ],
         compiler_params=pltpu.CompilerParams(
             collective_id=1, has_side_effects=True, vmem_limit_bytes=62 * 2**20),
         name="backward",
-    )(*saved, counts, tokens, out_grad, mod, gains, table)
+    )(*saved, counts, tokens, out_grad, ada_w, mod, gains, table, cond)
 
 
 def normalize(vectors, axis=-1, count=None):
@@ -1013,9 +1117,9 @@
 def unpack_grads(both):
     qkv = both[:, :QKV].reshape(2, 3, HD, D).swapaxes(0, 1).reshape(3, 2 * HD, D)
     o = both[:, QKV:A_ROWS].reshape(2 * HD, D)
-    gu = both[:, A_ROWS : A_ROWS + B_ROWS].reshape(2, 2, SHARD_FF, D)
-    gu = gu.transpose(3, 1, 0, 2).reshape(D, 2, 2 * SHARD_FF)
-    dn = both[:, A_ROWS + B_ROWS :].reshape(2 * SHARD_FF, D)
+    gu = both[:, B_FIRST:C_FIRST].reshape(2, 2, 2, HALF_FF, D)
+    gu = gu.transpose(4, 2, 0, 1, 3).reshape(D, 2, 2 * SHARD_FF)
+    dn = both[:, C_FIRST:].reshape(2 * SHARD_FF, D)
     return [wide(v) for v in (qkv.transpose(2, 0, 1), o, gu, dn)]
 
 
@@ -1036,7 +1140,7 @@
     classes = jnp.arange(class_table.shape[0])
     condition = dot("in,nc->ic", low(labels[:, None] == classes[None, :]), class_table) + time_embed
     gu = lax.dynamic_slice_in_dim(gate_up_weight, c * SHARD_FF, SHARD_FF, 2)
-    gu = gu.transpose(1, 2, 0).reshape(B_ROWS, D)
+    gu = gu.reshape(D, 2, 2, HALF_FF).transpose(2, 1, 3, 0).reshape(B_ROWS, D)
     table = pair_tables(tokens.shape[0])
     (weights, cond_all, mod, first_in, second_in, feed_grad, attention, qkv_t, norm_t, stat_t, mixed, gu_t, hidden,
      down_part) = forward(
@@ -1044,28 +1148,17 @@
         ada_weight.transpose(1, 0, 2), ada_bias, qkv_bias, tokens, out_grad, qk_scale, table)
     saved = (weights, first_in, second_in, feed_grad, attention, qkv_t, norm_t, stat_t, mixed, gu_t, hidden,
              down_part.reshape(4, 2, C_ROWS, D))
-    result, tokens_grad, summed, pay_all = backward(saved, image_counts, tokens, out_grad, mod, qk_scale, table)
+    result, tokens_grad, summed, pay_all, sums, biases, cond_grad, table_grad = backward(
+        saved, image_counts, tokens, out_grad, ada_weight.transpose(1, 0, 2), mod, qk_scale, table, cond_all,
+        class_table.shape[0])
     qkv_weight_grad, out_weight_grad, gate_up_grad, down_grad = unpack_grads(summed)
-
-    cond_all = cond_all.reshape(4 * images, -1)
-    condition = cond_all[:, :columns_here]
-    chosen = low(cond_all[:, columns_here].astype(jnp.int32)[:, None] == classes[None, :])
-    cond_act = low(jax.nn.silu(condition))
-    first_image = lax.axis_index("dp") * images
-    pay_all = pay_all.reshape(32, 2, 8, D)
-    mod_grad = pay_all[:, :, :6].reshape(-1, 6, D)
-    scale_all = wide(pay_all[:, 1, 6, : 2 * HD])
-    qk_scale_grad = jnp.sum(scale_all, axis=0).reshape(2, HD)
-    bias_all = wide(pay_all[:, 0, 6:, : 4 * 256]).reshape(32, 8, 256)[..., :QKV]
-    bias_all = lax.dynamic_index_in_dim(bias_all, t, 1, keepdims=False).reshape(2, 2, 8, 3, HD)
-    bias_sum = jnp.sum(bias_all, axis=(0, 2))
-    qkv_bias_grad = bias_sum.swapaxes(0, 1).reshape(3, 2 * HD)
+    mod_grad = pay_all.reshape(-1, 8, D)[:, :6]
+    cond_act = low(jax.nn.silu(cond_all.reshape(4 * images, -1)[:, :columns_here]))
     ada_weight_grad = dot("ic,ikd->ckd", cond_act, mod_grad)
-    ada_bias_grad = jnp.sum(wide(mod_grad), axis=0)
-    act_grad = dot("ikd,ckd->ic", mod_grad, ada_weight)
-    cond_grad_all = act_grad * silu_slope(condition)
-    table_grad = jnp.dot(wide(chosen).T, cond_grad_all, precision=HIGH)
-    cond_grad = lax.dynamic_slice_in_dim(cond_grad_all, first_image, images, 0)
+    ada_bias_grad = sums[:6]
+    qk_scale_grad = sums[6, : 2 * HD].reshape(2, HD)
+    qkv_bias_grad = biases[1:3, :QKV].reshape(2, 3, HD).swapaxes(0, 1).reshape(3, 2 * HD)
+    table_grad = table_grad.T
     return (
         result, tokens_grad, cond_grad, table_grad, ada_weight_grad, ada_bias_grad,
         qkv_weight_grad, qkv_bias_grad, qk_scale_grad, out_weight_grad, gate_up_grad, down_grad,

time: 367 us -> 352 us (0.959)
  Pallas kernels: 327 us -> 317 us
  other arithmetic: 7.32 us -> 3.11 us
    pallas_call x1, Pallas kernels: 153 us -> 143 us  [forward(): pl.pallas_call(forward_kernel, out_shape=tuple((jax.ShapeDtypeStruct(s, e...]
    transpose x3 -> x2, local copies, waits for them, and re-layouts: 4.74 us -> 0.99 us  [the longest x1 0.98 us: fast(): gu = gu.reshape(D, 2, 2, HALF_FF).transpose(2, 1, 3, 0).reshape(B_ROWS, D)]
    unnamed x16 -> x23, local copies, waits for them, and re-layouts: 9.42 us -> 11.9 us
    dot_general x3 -> x2, matrix products: 7.93 us -> 5.87 us  [fast(): jnp.einsum(s, a, b, preferred_element_type=jnp.float32)]
where the time goes in v4:
time: 352 us; the launch traced here: 351 us
  Pallas kernels  317 us (90%)
  local copies, waits for them, and re-layouts  23.1 us (7%)
  matrix products  5.87 us (2%)
    pallas_call x1, Pallas kernels, backward(): pl.pallas_call(backward_kernel, out_shape=tuple((jax.ShapeDtypeStruct(s,...  174 us
    pallas_call x1, Pallas kernels, forward(): pl.pallas_call(forward_kernel, out_shape=tuple((jax.ShapeDtypeStruct(s, e...  143 us
    unnamed x23, local copies, waits for them, and re-layouts  11.9 us

profile of v4, /device:TPU:0, one launch (start us, length us, event | category | flops | bytes accessed | tf_op | source)
XLA Modules:
  0.0 350.9 jit_solution(16886040977288490983)
XLA Ops:
  0.6 0.0 copy-start
  1.5 0.7 convert_element_type.53
  2.1 1.3 copy.41.labels
  3.5 1.8 convolution_add_fusion.condition
  5.3 0.0 copy-done
  5.3 1.9 constant_dynamic-slice_fusion
  7.2 1.6 copy.47
  8.8 1.0 copy.40
  9.7 143.3 %forward.1 = (bf16[8,864,1152]{2,1,0:T(8,128)(2,1)}, f32[4,16,256]{2,1,0:T(8,128)}, f32[16,1152]{1,0:T(8,128)}, bf16[2,512,1152]{2,1,0:T(8,128)(2,1)}, bf16[2,51...) custom-call(s32[1]{0:T(128)S(6)} %copy.56.counts, ...), custom_call_target="tpu_custom_call" | custom-call | tf_op jit(solution)/shard_map/forward/pallas_call | solution.py:522
  153.0 174.0 %backward.1 = (bf16[512,1152]{1,0:T(8,128)(2,1)}, f32[512,1152]{1,0:T(8,128)}, bf16[2,864,1152]{2,1,0:T(8,128)(2,1)}, bf16[2,2,4,2,16,1152]{5,4,3,2,1,0:T(8,128)...) custom-call(bf16[8,864,1152]{2,1,0:T(8,128)(2,1)} %get-tuple-element.34.full, ...), custom_call_target="tpu_custom_call" | custom-call | tf_op jit(solution)/shard_map/backward/pallas_call | solution.py:1065
  327.0 0.7 slice_reduce_fusion
  327.7 0.6 reshape_squeeze.3
  328.4 0.7 slice.31
  329.1 0.1 reshape.87
  329.1 0.7 reshape.88
  329.8 1.0 slice.33
  330.8 0.9 bitcast_convert_fusion.1
  331.7 0.0 copy-start.2
  331.7 1.4 slice.35
  333.1 1.4 bitcast_convert_fusion
  334.5 0.0 copy-done.2
  334.5 0.1 slice.30
  334.6 0.1 slice.34
  334.7 0.1 convert_bitcast_fusion
  334.9 1.4 copy.43
  336.3 0.2 copy.45
  336.5 4.7 %copy.46 = f32[1152,2,384]{2,1,0:T(2,128)} copy(f32[1152,2,384]{0,2,1:T(8,128)S(1)} %bitcast.36) | data formatting | bytes 7077888
  341.3 0.0 copy-start.4
  341.3 4.1 %fusion = f32[144,6,1152]{2,0,1:T(8,128)} fusion(bf16[64,6,1152]{2,1,0:T(8,128)(2,1)} %bitcast.46, f32[64,256]{1,0:T(8,128)} %bitcast.48), kind=kOutput, calls=%fused_computation.2 | convolution fusion | flops 127448064 | bytes 4931584 | tf_op jit(solution)/shard_map/ic,ikd->ckd/dot_general | solution.py:1130
  345.3 0.0 copy-done.4
  345.3 0.0 copy-start.3
  345.3 0.0 copy-start.1
  345.3 1.0 copy.57
  346.3 1.1 copy-done.3
  347.4 0.0 copy-start.7
  347.4 0.0 copy-start.5
  347.4 0.0 copy-start.6
  347.4 1.4 copy.58
  348.8 0.0 copy-done.7
  348.8 0.6 copy.59
  349.4 0.0 copy-done.5
  349.4 0.8 copy.60
  350.3 0.0 copy-done.6
  350.3 0.6 copy.61
  350.9 0.0 copy-done.1
  (3 shorter events, 0.0 us)
Async XLA Ops:
  0.6 4.6 %copy-start = (bf16[1152,2,384]{2,1,0:T(2,128)(2,1)S(1)}, bf16[1152,2,384]{2,1,0:T(2,128)(2,1)}, u32[]{:S(2)}) copy-start(bf16[1152,2,384]{2,1,0:T(2,128)(2,1)} %param.26) | copy-start | bytes 5308420
  331.7 2.8 copy-start.2
  341.3 4.1 %copy-start.4 = (bf16[512,1152]{1,0:T(8,128)(2,1)S(1)}, bf16[512,1152]{1,0:T(8,128)(2,1)}, u32[]{:S(2)}) copy-start(bf16[512,1152]{1,0:T(8,128)(2,1)} %get-tuple-element.92) | copy-start | bytes 3538948
  345.3 2.1 copy-start.3
  345.3 5.5 %copy-start.1 = (bf16[1152,2,384]{2,1,0:T(2,128)(2,1)S(1)}, bf16[1152,2,384]{2,1,0:T(2,128)(2,1)}, u32[]{:S(2)}) copy-start(bf16[1152,2,384]{2,1,0:T(2,128)(2,1)} %param.26) | copy-start | bytes 5308420
  347.4 1.4 copy-start.7
  347.4 2.0 copy-start.5
  347.4 2.8 copy-start.6

commit v5 on v4

--- a/solution.py
+++ b/solution.py
@@ -243,7 +243,7 @@
 
     cond_in[...] = jnp.zeros_like(cond_in)
     cond_in[:, :144] = condition[...]
-    cond_in[:, 144:145] = wide(labels[...])
+    cond_in[:, 144:145] = columns(wide(labels[...]))[:16, :1]
     mod_in[...] = jnp.zeros_like(mod_in)
     for p in range(8):
         for k, row in enumerate((6, 7, 14)):
@@ -377,8 +377,7 @@
         for cp in save_head(s):
             cp.start()
 
-        pl.when(jnp.logical_or(lax.rem(s, 5) == 0, jnp.logical_or(lax.rem(s, 5) == 2, s == 3)))(
-            lambda: service(A_STAGES + 4 + (s + 1) // 2))
+        pl.when(jnp.logical_or(s == 0, lax.rem(s, 2) == 1))(lambda: service(A_STAGES + 4 + (s + 1) // 2))
 
     for s in (6, 7):
         for cp in save_head(s):
@@ -461,9 +460,9 @@
                 cp.start()
 
             if half == 0:
-                service(A_STAGES + 11 + p)
+                pl.when(lax.rem(p, 2) == 1)(lambda: service(A_STAGES + 11 + p // 2))
             else:
-                pl.when(p == 2)(lambda: service(A_STAGES + 15))
+                pl.when(p < 3)(lambda: service(A_STAGES + 13 + p))
 
         for p in (2, 3):
             for cp in save_pair(half, p):
@@ -545,7 +544,7 @@
 def backward_kernel(
     full, fi_in, si_in, fg_in, att_in, qkv_in, norm_in, stat_in, mixed_in, gu_in, hid_in, dd_in,
     counts, tokens_hbm, out_grad_hbm, ada_hbm, mod, gains, table, cond,
-    result_out, tokens_out, grads, pay_all, sums_out, bias_out, cond_out, class_out,
+    result_out, tokens_out, grads, pay_all, sums_out, scale_out, bias_out, cond_out, class_out,
     tokens, out_grad, ada_w, cond_all, part, xin, yin, zin, fin, buf_a, buf_b, acc, after, att, sent, came, came_feed, result,
     wd, wb, wa, hid, gu, qkv, norm, stat, mixed, dqkv, dlow, gain_sum, payf, pay,
     xs, xr, ys, yr, zs, zr, fs, fr, es, er, ps, pr, ls, lw, x_free, y_free, z_free,
@@ -1009,8 +1008,13 @@
     payf[:8, :] = picked(8, lambda row, col: jnp.logical_or(
         jnp.logical_and(row == 0, lax.rem(col, PAY) == 14),
         jnp.logical_and(row == 1 + lax.rem(col // (8 * PAY), 2), lax.rem(col, PAY) == 6 + t // 4)))
-    sums_out[6:8, :] = payf[0:2, :]
-    bias_out[...] = payf[:8, pl.ds(pl.multiple_of(lax.rem(t, 4) * 256, 128), 256)]
+    found = payf[:8, :256]
+    scale_out[0:1, :] = found[:1, :HD]
+    scale_out[1:2, :] = found[:1, HD : 2 * HD]
+    found = payf[:8, pl.ds(pl.multiple_of(lax.rem(t, 4) * 256, 128), 256)]
+    for k in range(3):
+        cut = slice(k * HD, (k + 1) * HD)
+        bias_out[k : k + 1, :] = jnp.concatenate([found[1:2, cut], found[2:3, cut]], axis=1)
     for group in range(4):
         cond_all[group * 16 : (group + 1) * 16, :] = cond[group]
     v = cond_all[:, :144]
@@ -1061,7 +1065,7 @@
     inside = pl.BlockSpec(memory_space=pltpu.VMEM)
     R = tokens.shape[0]
     outs = [((R, D), bf), ((R, D), f32), ((2, ROWS_ALL, D), bf), ((2, 2, 4, 2, PAY, D), bf)]
-    small = [((8, D), f32), ((8, 256), f32), ((16, 144), f32), ((144, classes), f32)]
+    small = [((6, D), f32), ((2, HD), f32), ((3, 2 * HD), f32), ((16, 144), f32), ((144, classes), f32)]
     return pl.pallas_call(
         backward_kernel,
         out_shape=tuple(jax.ShapeDtypeStruct(s, e) for s, e in outs + small),
@@ -1144,20 +1148,18 @@
     table = pair_tables(tokens.shape[0])
     (weights, cond_all, mod, first_in, second_in, feed_grad, attention, qkv_t, norm_t, stat_t, mixed, gu_t, hidden,
      down_part) = forward(
-        image_counts, qkv_weight.transpose(1, 2, 0), out_weight, gu, down_weight, condition, labels[:, None],
+        image_counts, qkv_weight.transpose(1, 2, 0), out_weight, gu, down_weight, condition, labels[None, :],
         ada_weight.transpose(1, 0, 2), ada_bias, qkv_bias, tokens, out_grad, qk_scale, table)
     saved = (weights, first_in, second_in, feed_grad, attention, qkv_t, norm_t, stat_t, mixed, gu_t, hidden,
              down_part.reshape(4, 2, C_ROWS, D))
-    result, tokens_grad, summed, pay_all, sums, biases, cond_grad, table_grad = backward(
+    (result, tokens_grad, summed, pay_all, ada_bias_grad, qk_scale_grad, qkv_bias_grad, cond_grad,
+     table_grad) = backward(
         saved, image_counts, tokens, out_grad, ada_weight.transpose(1, 0, 2), mod, qk_scale, table, cond_all,
         class_table.shape[0])
     qkv_weight_grad, out_weight_grad, gate_up_grad, down_grad = unpack_grads(summed)
     mod_grad = pay_all.reshape(-1, 8, D)[:, :6]
     cond_act = low(jax.nn.silu(cond_all.reshape(4 * images, -1)[:, :columns_here]))
     ada_weight_grad = dot("ic,ikd->ckd", cond_act, mod_grad)
-    ada_bias_grad = sums[:6]
-    qk_scale_grad = sums[6, : 2 * HD].reshape(2, HD)
-    qkv_bias_grad = biases[1:3, :QKV].reshape(2, 3, HD).swapaxes(0, 1).reshape(3, 2 * HD)
     table_grad = table_grad.T
     return (
         result, tokens_grad, cond_grad, table_grad, ada_weight_grad, ada_bias_grad,

time: 352 us -> 348 us (0.989)
    unnamed x23 -> x29, local copies, waits for them, and re-layouts: 11.9 us -> 13 us
where the time goes in v5:
time: 348 us; the launch traced here: 347 us
  Pallas kernels  317 us (91%)
  local copies, waits for them, and re-layouts  20.1 us (6%)
  matrix products  5.88 us (2%)
    pallas_call x1, Pallas kernels, backward(): pl.pallas_call(backward_kernel, out_shape=tuple((jax.ShapeDtypeStruct(s,...  174 us
    pallas_call x1, Pallas kernels, forward(): pl.pallas_call(forward_kernel, out_shape=tuple((jax.ShapeDtypeStruct(s, e...  142 us
    unnamed x29, local copies, waits for them, and re-layouts  13 us

profile of v5, /device:TPU:0, one launch (start us, length us, event | category | flops | bytes accessed | tf_op | source)
XLA Modules:
  0.0 347.4 jit_solution(383861393577928886)
XLA Ops:
  0.6 0.0 copy-start
  1.5 0.7 convert_element_type.53
  2.1 1.8 convolution_add_fusion.condition
  3.9 0.0 copy-done
  4.0 1.9 constant_dynamic-slice_fusion
  5.8 1.6 copy.36
  7.4 1.0 copy.31
  8.4 142.4 %forward.1 = (bf16[8,864,1152]{2,1,0:T(8,128)(2,1)}, f32[4,16,256]{2,1,0:T(8,128)}, f32[16,1152]{1,0:T(8,128)}, bf16[2,512,1152]{2,1,0:T(8,128)(2,1)}, bf16[2,51...) custom-call(s32[1]{0:T(128)S(6)} %copy.47.counts, ...), custom_call_target="tpu_custom_call" | custom-call | tf_op jit(solution)/shard_map/forward/pallas_call | solution.py:521
  150.8 174.3 %backward.1 = (bf16[512,1152]{1,0:T(8,128)(2,1)}, f32[512,1152]{1,0:T(8,128)}, bf16[2,864,1152]{2,1,0:T(8,128)(2,1)}, bf16[2,2,4,2,16,1152]{5,4,3,2,1,0:T(8,128)...) custom-call(bf16[8,864,1152]{2,1,0:T(8,128)(2,1)} %get-tuple-element, ...), custom_call_target="tpu_custom_call" | custom-call | tf_op jit(solution)/shard_map/backward/pallas_call | solution.py:1069
  325.1 1.0 slice.21
  326.1 0.9 bitcast_convert_fusion.1
  327.0 0.0 copy-start.2
  327.0 1.4 slice.23
  328.4 1.4 bitcast_convert_fusion
  329.8 0.0 copy-done.2
  329.8 0.1 slice.20
  329.9 0.1 slice.22
  330.0 0.1 convert_bitcast_fusion
  330.2 1.4 copy.33
  331.6 0.2 copy.34
  331.8 4.7 %copy.35 = f32[1152,2,384]{2,1,0:T(2,128)} copy(f32[1152,2,384]{0,2,1:T(8,128)S(1)} %bitcast.34) | data formatting | bytes 7077888
  336.5 0.0 copy-start.4
  336.6 4.1 %fusion = f32[144,6,1152]{2,0,1:T(8,128)} fusion(bf16[64,6,1152]{2,1,0:T(8,128)(2,1)} %bitcast.44, f32[64,256]{1,0:T(8,128)} %bitcast.46), kind=kOutput, calls=%fused_computation.2 | convolution fusion | flops 127448064 | bytes 4931584 | tf_op jit(solution)/shard_map/ic,ikd->ckd/dot_general | solution.py:1134
  340.6 0.0 copy-done.4
  340.6 0.0 copy-start.3
  340.6 0.0 copy-start.1
  340.6 1.0 copy.48
  341.6 1.1 copy-done.3
  342.7 0.0 copy-start.7
  342.7 0.0 copy-start.5
  342.7 0.0 copy-start.6
  342.7 0.0 copy-start.8
  342.7 0.0 copy-start.9
  342.7 1.4 copy.49
  344.1 0.0 copy-done.7
  344.1 0.6 copy.50
  344.7 0.0 copy-done.5
  344.8 0.8 copy.51
  345.6 0.0 copy-done.6
  345.6 0.6 copy.52
  346.2 0.0 copy-done.8
  346.2 0.6 copy.53
  346.8 0.0 copy-done.9
  346.8 0.6 copy.54
  347.3 0.0 copy-done.1
  (2 shorter events, 0.0 us)
Async XLA Ops:
  0.6 3.3 copy-start
  327.0 2.8 copy-start.2
  336.5 4.1 %copy-start.4 = (bf16[512,1152]{1,0:T(8,128)(2,1)S(1)}, bf16[512,1152]{1,0:T(8,128)(2,1)}, u32[]{:S(2)}) copy-start(bf16[512,1152]{1,0:T(8,128)(2,1)} %get-tuple-element.82) | copy-start | bytes 3538948
  340.6 2.1 copy-start.3
  340.6 6.7 %copy-start.1 = (bf16[1152,2,384]{2,1,0:T(2,128)(2,1)S(1)}, bf16[1152,2,384]{2,1,0:T(2,128)(2,1)}, u32[]{:S(2)}) copy-start(bf16[1152,2,384]{2,1,0:T(2,128)(2,1)} %param.26) | copy-start | bytes 5308420
  342.7 1.4 copy-start.7
  342.7 2.0 copy-start.5
  342.7 2.9 copy-start.6
  342.7 3.5 copy-start.8
  342.7 4.1 %copy-start.9 = (f32[2,72]{1,0:T(2,128)S(1)}, f32[2,72]{1,0:T(2,128)}, u32[]{:S(2)}) copy-start(f32[2,72]{1,0:T(2,128)} %get-tuple-element.90) | copy-start | bytes 1732

commit v6 on v5

--- a/solution.py
+++ b/solution.py
@@ -1122,7 +1122,7 @@
     qkv = both[:, :QKV].reshape(2, 3, HD, D).swapaxes(0, 1).reshape(3, 2 * HD, D)
     o = both[:, QKV:A_ROWS].reshape(2 * HD, D)
     gu = both[:, B_FIRST:C_FIRST].reshape(2, 2, 2, HALF_FF, D)
-    gu = gu.transpose(4, 2, 0, 1, 3).reshape(D, 2, 2 * SHARD_FF)
+    gu = lax.optimization_barrier(gu.transpose(4, 2, 0, 1, 3).reshape(D, 2, 2 * SHARD_FF))
     dn = both[:, C_FIRST:].reshape(2 * SHARD_FF, D)
     return [wide(v) for v in (qkv.transpose(2, 0, 1), o, gu, dn)]
 

time: 348 us -> 346 us (level)
    unnamed x29 -> x33, local copies, waits for them, and re-layouts: 13 us -> 12.9 us
where the time goes in v6:
time: 346 us
  Pallas kernels  317 us (92%)
  local copies, waits for them, and re-layouts  19.9 us (6%)
  matrix products  4.48 us (1%)
    pallas_call x1, Pallas kernels, backward(): pl.pallas_call(backward_kernel, out_shape=tuple((jax.ShapeDtypeStruct(s,...  174 us
    pallas_call x1, Pallas kernels, forward(): pl.pallas_call(forward_kernel, out_shape=tuple((jax.ShapeDtypeStruct(s, e...  142 us
    unnamed x33, local copies, waits for them, and re-layouts  12.9 us

profile of v6, /device:TPU:0, one launch (start us, length us, event | category | flops | bytes accessed | tf_op | source)
XLA Modules:
  0.0 345.7 jit_solution(10392149716602869385)
XLA Ops:
  0.6 0.0 copy-start
  1.5 0.7 convert_element_type.44
  2.1 1.8 convolution_add_fusion.condition
  3.9 0.0 copy-done
  4.0 1.9 constant_dynamic-slice_fusion
  5.8 1.6 copy.36
  7.4 1.0 copy.31
  8.4 142.4 %forward.1 = (bf16[8,864,1152]{2,1,0:T(8,128)(2,1)}, f32[4,16,256]{2,1,0:T(8,128)}, f32[16,1152]{1,0:T(8,128)}, bf16[2,512,1152]{2,1,0:T(8,128)(2,1)}, bf16[2,51...) custom-call(s32[1]{0:T(128)S(6)} %copy.47.counts, ...), custom_call_target="tpu_custom_call" | custom-call | tf_op jit(solution)/shard_map/forward/pallas_call | solution.py:521
  150.8 174.3 %backward.1 = (bf16[512,1152]{1,0:T(8,128)(2,1)}, f32[512,1152]{1,0:T(8,128)}, bf16[2,864,1152]{2,1,0:T(8,128)(2,1)}, bf16[2,2,4,2,16,1152]{5,4,3,2,1,0:T(8,128)...) custom-call(bf16[8,864,1152]{2,1,0:T(8,128)(2,1)} %get-tuple-element, ...), custom_call_target="tpu_custom_call" | custom-call | tf_op jit(solution)/shard_map/backward/pallas_call | solution.py:1069
  325.1 1.0 slice.21
  326.1 0.9 bitcast_convert_fusion.1
  327.0 0.0 copy-start.2
  327.0 1.4 slice.23
  328.4 1.4 bitcast_convert_fusion
  329.8 0.0 copy-done.2
  329.8 0.1 slice.20
  329.9 0.1 slice.22
  330.0 0.1 copy.34
  330.2 0.1 convert_bitcast_fusion
  330.3 1.4 copy.33
  331.7 0.0 copy-start.5
  331.7 0.0 copy-start.7
  331.7 4.6 %copy.35 = f32[1152,2,384]{2,1,0:T(2,128)} copy(bf16[1152,2,384]{0,2,1:T(8,128)(2,1)S(1)} %bitcast.36) | data formatting | bytes 5308416
  336.3 0.0 copy-done.5
  336.3 0.0 copy-done.7
  336.3 0.0 copy-start.4
  336.3 2.7 fusion
  339.0 0.0 copy-done.4
  339.0 0.0 copy-start.3
  339.0 0.0 copy-start.1
  339.0 1.0 copy.48
  340.0 1.1 copy-done.3
  341.1 0.0 copy-start.9
  341.1 0.0 copy-start.6
  341.1 0.0 copy-start.8
  341.1 0.0 copy-start.11
  341.1 1.4 copy.49
  342.5 0.0 copy-done.9
  342.5 0.6 copy.50
  343.1 0.0 copy-done.6
  343.1 0.8 copy.51
  344.0 0.0 copy-done.8
  344.0 0.6 copy.52
  344.6 0.0 copy-done.10
  344.6 0.6 copy.53
  345.2 0.0 copy-done.11
  345.2 0.6 copy.54
  345.7 0.0 copy-done.1
  (3 shorter events, 0.0 us)
Async XLA Ops:
  0.6 3.3 copy-start
  327.0 2.8 copy-start.2
  331.7 4.6 %copy-start.5 = (bf16[2,2,4,2,16,1152]{5,4,3,2,1,0:T(8,128)(2,1)S(1)}, bf16[2,2,4,2,16,1152]{5,4,3,2,1,0:T(8,128)(2,1)}, u32[]{:S(2)}) copy-start(bf16[2,2,4,2,16,1152]{5,4,3,2,1,0:T(8,128)(2,1)} %get-tuple-element.53) | copy-start | bytes 3538948
  331.7 4.6 %copy-start.7 = (f32[4,16,256]{2,1,0:T(8,128)S(1)}, f32[4,16,256]{2,1,0:T(8,128)}, u32[]{:S(2)}) copy-start(f32[4,16,256]{2,1,0:T(8,128)} %get-tuple-element.48.cond) | copy-start | bytes 196612
  336.3 2.7 copy-start.4
  339.0 2.1 copy-start.3
  339.0 6.7 %copy-start.1 = (bf16[1152,2,384]{2,1,0:T(2,128)(2,1)S(1)}, bf16[1152,2,384]{2,1,0:T(2,128)(2,1)}, u32[]{:S(2)}) copy-start(bf16[1152,2,384]{2,1,0:T(2,128)(2,1)} %param.26) | copy-start | bytes 5308420
  341.1 1.4 copy-start.9
  341.1 2.0 copy-start.6
  341.1 2.9 copy-start.8
  341.1 3.5 %copy-start.10 = (f32[3,144]{1,0:T(4,128)S(1)}, f32[3,144]{1,0:T(4,128)}, u32[]{:S(2)}) copy-start(f32[3,144]{1,0:T(4,128)} %get-tuple-element.89) | copy-start | bytes 5188
  341.1 4.1 %copy-start.11 = (f32[2,72]{1,0:T(2,128)S(1)}, f32[2,72]{1,0:T(2,128)}, u32[]{:S(2)}) copy-start(f32[2,72]{1,0:T(2,128)} %get-tuple-element.90) | copy-start | bytes 1732
